TPU v7x, 512 devices: a whole 4x4x16 slice. The times are simulated.
512 devices in a mesh: section: 4 (over x), dom: 128 (over z, y, core).
Axes of the slice: x: 4, y: 4, z: 16, core: 2. Of those that a mesh axis runs over, the one named last changes fastest.
Arguments:
- latent: bfloat16 [4, 16384, 512], P(None, 'dom'), may hold values from -32 to 32
- cotangent: bfloat16 [4, 16384, 512], P(None, 'dom'), may hold values from -6 to 6
- source_weight: bfloat16 [4, 512, 512], P('section'), may hold values from -0.25 to 0.25
- self_weight: bfloat16 [4, 512, 512], P('section'), may hold values from -0.25 to 0.25
- out_weight: bfloat16 [4, 512, 512], P('section'), may hold values from -0.25 to 0.25
- norm_gain: float32 [4, 512], P('section'), may hold values from 0.1 to 1.9
- edge_tiles: bfloat16 [512, 128, 128], P('dom'), may hold values from -0.4 to 0.4
- pair_source: int32 [512], P('dom'), may hold values from 0 to 127, as said below
- live_pairs: int32 [128], P('dom'), may hold values from 1 to 4, as said below
Outputs:
- layer_latents: bfloat16 [4, 4, 16384, 512], P('section', None, 'dom')
- layer_grads: bfloat16 [4, 4, 16384, 512], P('section', None, 'dom')
Inputs may be any that keep to these rules, and one draw needn't show every extreme that they name: `pair_source`: the sending block of every slot of partition d, live or not, is owned by a partition from d - 2 to d + 2. `live_pairs`: some partition has all 4 slots live.
All inputs are finite; a program needn't handle non-finite values.
Results may differ from a plain program's by a relative error of at most 0.025.
Values may be sent and summed in bfloat16 or wider, within the bound.
No kernel may reach another device: no remote copies, remote signals or barrier semaphores. Data moves between devices by JAX's collectives and lax.ppermute only.
A program may use at most 64 MiB of HBM per device.

v0:
```python
import jax
import jax.numpy as jnp
from jax import lax
from jax.sharding import PartitionSpec as P

WIN = 2


EPS = 1e-05


def from_behind(value, axis, steps):
    count = lax.axis_size(axis)
    initial, last = (max(0, -steps), min(count, count - steps))
    return lax.ppermute(value, axis, [(source, source + steps) for source in range(initial, last)])


def norm_rows(values, layer_gain):
    widened = values.astype(jnp.float32)
    centre = widened - jnp.mean(widened, axis=-1, keepdims=True)
    inv_scale = lax.rsqrt(jnp.mean(centre * centre, axis=-1, keepdims=True) + EPS)
    normed = centre * inv_scale
    return (normed, inv_scale, (normed * layer_gain).astype(jnp.bfloat16))


def pair_matrix(edge_tiles, live_count, blocks):
    slots, block_rows, _ = edge_tiles.shape
    slot_order = jnp.arange(slots, dtype=jnp.int32)
    target = slot_order * blocks // live_count
    select = (target[None, :] == jnp.arange(blocks, dtype=jnp.int32)[:, None]) & (
        slot_order < live_count
    )[None, :]
    spread = jnp.transpose(edge_tiles, (1, 0, 2))
    masked = jnp.where(select[:, None, :, None], spread[None], jnp.zeros((), edge_tiles.dtype))
    return masked.reshape(blocks * block_rows, slots * block_rows)


def gather_window(source):
    pieces = []
    for offset in range(-WIN, WIN + 1):
        if offset == 0:
            pieces.append(source)
        else:
            pieces.append(from_behind(source, "dom", -offset))
    return jnp.concatenate(pieces, axis=0)


def aggregate(window, matrix, slot_index):
    feature_count = window.shape[2]
    picked = window[slot_index].reshape(-1, feature_count)
    gathered = jnp.dot(matrix, picked, preferred_element_type=jnp.float32)
    return gathered


def spread_back(grad_pre, matrix, edge_tiles, slot_index, blocks):
    slots, block_rows, _ = edge_tiles.shape
    feature_count = grad_pre.shape[1]
    window_blocks = (2 * WIN + 1) * blocks
    contributions = jnp.dot(matrix.T, grad_pre, preferred_element_type=jnp.float32).reshape(
        slots, block_rows, feature_count
    )
    slot_onehot = (
        slot_index[None, :] == jnp.arange(window_blocks, dtype=jnp.int32)[:, None]
    ).astype(jnp.float32)
    per_slot = jnp.einsum(
        "wp,pjh->wjh", slot_onehot, contributions, precision=lax.Precision.HIGHEST
    )
    rounded = per_slot.astype(jnp.bfloat16)
    running_sum = jnp.zeros((blocks, block_rows, feature_count), jnp.float32)
    for offset in range(-WIN, WIN + 1):
        window_part = rounded[(offset + WIN) * blocks : (offset + WIN + 1) * blocks]
        if offset == 0:
            running_sum = running_sum + window_part.astype(jnp.float32)
        else:
            arrived = from_behind(window_part, "dom", offset)
            running_sum = running_sum + arrived.astype(jnp.float32)
    return running_sum.reshape(blocks * block_rows, feature_count).astype(jnp.bfloat16)


def body(
    latent,
    cotangent,
    source_weight,
    self_weight,
    out_weight,
    norm_gain,
    edge_tiles,
    pair_source,
    live_pairs,
):
    section_index = lax.axis_index("section")
    layer_count = lax.axis_size("section")
    dom_index = lax.axis_index("dom")
    sample_count = latent.shape[0]
    block_rows = edge_tiles.shape[1]
    blocks = latent.shape[1] // block_rows
    feature_count = latent.shape[2]
    live_count = live_pairs[0]
    slot_index = pair_source - (dom_index - WIN) * blocks
    layer_source = source_weight[0]
    layer_self = self_weight[0]
    layer_out = out_weight[0]
    layer_gain = norm_gain[0]
    matrix = pair_matrix(edge_tiles, live_count, blocks)
    sample_ids = jnp.arange(sample_count, dtype=jnp.int32)
    tick_count = sample_count + layer_count - 1
    incoming = latent[0]
    kept_input = jnp.zeros(latent.shape, latent.dtype)
    kept_pre = jnp.zeros(latent.shape, jnp.float32)
    latent_result = jnp.zeros_like(latent)
    for tick_index in range(tick_count):
        sample_now = tick_index - section_index
        picked = (sample_ids == sample_now)[:, None, None]
        entering = latent[min(tick_index, sample_count - 1)]
        current = jnp.where(section_index == 0, entering, incoming)
        forward_normed, forward_inv_scale, forward_unit = norm_rows(current, layer_gain)
        source = jnp.dot(forward_unit, layer_source, preferred_element_type=jnp.float32).astype(
            jnp.bfloat16
        )
        window = gather_window(source.reshape(blocks, block_rows, feature_count))
        gathered = aggregate(window, matrix, slot_index)
        pre_act = gathered + jnp.dot(forward_unit, layer_self, preferred_element_type=jnp.float32)
        activation = jax.nn.silu(pre_act).astype(jnp.bfloat16)
        updated = (
            current.astype(jnp.float32)
            + jnp.dot(activation, layer_out, preferred_element_type=jnp.float32)
        ).astype(jnp.bfloat16)
        updated, pre_act = (updated, pre_act)
        kept_input = jnp.where(picked, current[None], kept_input)
        kept_pre = jnp.where(picked, pre_act[None], kept_pre)
        latent_result = jnp.where(picked, updated[None], latent_result)
        if tick_index + 1 < tick_count:
            incoming = from_behind(updated, "section", 1)
    incoming_grad = cotangent[0]
    grad_result = jnp.zeros_like(cotangent)
    for tick_index in range(tick_count):
        sample_now = tick_index - (layer_count - 1 - section_index)
        picked = (sample_ids == sample_now)[:, None, None]
        safe_sample = jnp.clip(sample_now, 0, sample_count - 1)
        entering = cotangent[min(tick_index, sample_count - 1)]
        gradient = jnp.where(section_index == layer_count - 1, entering, incoming_grad)
        input_now = lax.dynamic_index_in_dim(kept_input, safe_sample, 0, keepdims=False)
        pre_act = lax.dynamic_index_in_dim(kept_pre, safe_sample, 0, keepdims=False)
        normed, inv_scale, unit = norm_rows(input_now, layer_gain)
        grad_activation = jnp.dot(gradient, layer_out.T, preferred_element_type=jnp.float32)
        sigma = jax.nn.sigmoid(pre_act)
        grad_pre = (grad_activation * sigma * (1.0 + pre_act * (1.0 - sigma))).astype(jnp.bfloat16)
        back = spread_back(grad_pre, matrix, edge_tiles, slot_index, blocks)
        grad_unit = jnp.dot(grad_pre, layer_self.T, preferred_element_type=jnp.float32)
        grad_unit = grad_unit + jnp.dot(back, layer_source.T, preferred_element_type=jnp.float32)
        grad_normed = grad_unit * layer_gain
        grad_in = inv_scale * (
            grad_normed
            - jnp.mean(grad_normed, axis=-1, keepdims=True)
            - normed * jnp.mean(grad_normed * normed, axis=-1, keepdims=True)
        )
        new_gradient = (gradient.astype(jnp.float32) + grad_in).astype(jnp.bfloat16)
        grad_result = jnp.where(picked, new_gradient[None], grad_result)
        if tick_index + 1 < tick_count:
            incoming_grad = from_behind(new_gradient, "section", -1)
    return (latent_result[None], grad_result[None])


def solution(mesh):
    in_specs = (
        P(None, "dom", None),
        P(None, "dom", None),
        P("section", None, None),
        P("section", None, None),
        P("section", None, None),
        P("section", None),
        P("dom", None, None),
        P("dom"),
        P("dom"),
    )
    out_specs = (P("section", None, "dom", None), P("section", None, "dom", None))
    return jax.shard_map(body, mesh=mesh, in_specs=in_specs, out_specs=out_specs, check_vma=False)
```

profile of v0, /device:TPU:125, one launch (start us, length us, event | category | flops | bytes accessed | tf_op | source)
XLA Modules:
  0.0 421.8 jit_solution(15191967327972445717)
XLA Ops:
  9.4 6.1 %collective-permute-start.1 = (bf16[1,128,512]{2,1,0:T(8,128)(2,1)S(1)}, bf16[1,128,512]{2,1,0:T(8,128)(2,1)S(1)}, u32[]{:S(2)}, u32[]{:S(2)}) collective-permute-start(bf16[1,128,512]{2,1,0:T(8,128)(2,1)S(1)} %fusion.35), channel_id=1, source_target_pairs={{0,1},{1,2},{2,3},{3,4},{4,5},{5,6},{6,7},{7,8},{8,9},{9,10},{10,1... | collective-permute-start | bytes 393224 | tf_op jit(solution)/shard_map/ppermute | solution.py:15
  26.3 3.5 collective-permute-done.4
  35.7 7.3 %collective-permute-start.6 = (bf16[1,128,512]{2,1,0:T(8,128)(2,1)S(1)}, bf16[1,128,512]{2,1,0:T(8,128)(2,1)S(1)}, u32[]{:S(2)}, u32[]{:S(2)}) collective-permute-start(bf16[1,128,512]{2,1,0:T(8,128)(2,1)S(1)} %fusion.36), channel_id=1, source_target_pairs={{0,1},{1,2},{2,3},{3,4},{4,5},{5,6},{6,7},{7,8},{8,9},{9,10},{10,1... | collective-permute-start | bytes 393224 | tf_op jit(solution)/shard_map/ppermute | solution.py:15
  43.0 3.6 collective-permute-start.5
  59.1 3.7 collective-permute-done.9
  67.9 7.0 %collective-permute-start.11 = (bf16[1,128,512]{2,1,0:T(8,128)(2,1)S(1)}, bf16[1,128,512]{2,1,0:T(8,128)(2,1)S(1)}, u32[]{:S(2)}, u32[]{:S(2)}) collective-permute-start(bf16[1,128,512]{2,1,0:T(8,128)(2,1)S(1)} %fusion.37), channel_id=1, source_target_pairs={{0,1},{1,2},{2,3},{3,4},{4,5},{5,6},{6,7},{7,8},{8,9},{9,10},{10,1... | collective-permute-start | bytes 393224 | tf_op jit(solution)/shard_map/ppermute | solution.py:15
  74.9 3.6 collective-permute-start.10
  100.2 7.0 %collective-permute-start.16 = (bf16[1,128,512]{2,1,0:T(8,128)(2,1)S(1)}, bf16[1,128,512]{2,1,0:T(8,128)(2,1)S(1)}, u32[]{:S(2)}, u32[]{:S(2)}) collective-permute-start(bf16[1,128,512]{2,1,0:T(8,128)(2,1)S(1)} %fusion.38), channel_id=1, source_target_pairs={{0,1},{1,2},{2,3},{3,4},{4,5},{5,6},{6,7},{7,8},{8,9},{9,10},{10,1... | collective-permute-start | bytes 393224 | tf_op jit(solution)/shard_map/ppermute | solution.py:15
  107.2 3.6 collective-permute-start.15
  132.4 7.0 %collective-permute-start.21 = (bf16[1,128,512]{2,1,0:T(8,128)(2,1)S(1)}, bf16[1,128,512]{2,1,0:T(8,128)(2,1)S(1)}, u32[]{:S(2)}, u32[]{:S(2)}) collective-permute-start(bf16[1,128,512]{2,1,0:T(8,128)(2,1)S(1)} %fusion.39), channel_id=1, source_target_pairs={{0,1},{1,2},{2,3},{3,4},{4,5},{5,6},{6,7},{7,8},{8,9},{9,10},{10,1... | collective-permute-start | bytes 393224 | tf_op jit(solution)/shard_map/ppermute | solution.py:15
  139.5 3.6 collective-permute-start.20
  164.7 7.0 %collective-permute-start.26 = (bf16[1,128,512]{2,1,0:T(8,128)(2,1)S(1)}, bf16[1,128,512]{2,1,0:T(8,128)(2,1)S(1)}, u32[]{:S(2)}, u32[]{:S(2)}) collective-permute-start(bf16[1,128,512]{2,1,0:T(8,128)(2,1)S(1)} %fusion.40), channel_id=1, source_target_pairs={{0,1},{1,2},{2,3},{3,4},{4,5},{5,6},{6,7},{7,8},{8,9},{9,10},{10,1... | collective-permute-start | bytes 393224 | tf_op jit(solution)/shard_map/ppermute | solution.py:15
  171.8 3.6 collective-permute-start.25
  188.5 3.7 collective-permute-done.29
  197.5 7.0 %collective-permute-start.31 = (bf16[1,128,512]{2,1,0:T(8,128)(2,1)S(1)}, bf16[1,128,512]{2,1,0:T(8,128)(2,1)S(1)}, u32[]{:S(2)}, u32[]{:S(2)}) collective-permute-start(bf16[1,128,512]{2,1,0:T(8,128)(2,1)S(1)} %fusion.41), channel_id=1, source_target_pairs={{0,1},{1,2},{2,3},{3,4},{4,5},{5,6},{6,7},{7,8},{8,9},{9,10},{10,1... | collective-permute-start | bytes 393224 | tf_op jit(solution)/shard_map/ppermute | solution.py:15
  204.5 3.8 collective-permute-start.30
  225.0 6.7 %collective-permute-start.37 = (bf16[1,128,512]{2,1,0:T(8,128)(2,1)S(1)}, bf16[1,128,512]{2,1,0:T(8,128)(2,1)S(1)}, u32[]{:S(2)}, u32[]{:S(2)}) collective-permute-start(bf16[1,128,512]{2,1,0:T(8,128)(2,1)S(1)} %get-tuple-element.68), channel_id=1, source_target_pairs={{0,2},{1,3},{2,4},{3,5},{4,6},{5,7},{6,8},{7,9},{8,10},{9,11},{10,... | collective-permute-start | bytes 393224 | tf_op jit(solution)/shard_map/ppermute | solution.py:15
  236.5 6.9 %collective-permute-done.35 = bf16[1,128,512]{2,1,0:T(8,128)(2,1)S(1)} collective-permute-done((bf16[1,128,512]{2,1,0:T(8,128)(2,1)S(1)}, bf16[1,128,512]{2,1,0:T(8,128)(2,1)S(1)}, u32[]{:S(2)}, u32[]{:S(2)}) %collective-permute-start.35) | collective-permute-done | bytes 131104 | tf_op jit(solution)/shard_map/ppermute | solution.py:15
  246.3 3.5 collective-permute-done.38
  254.6 6.7 %collective-permute-start.42 = (bf16[1,128,512]{2,1,0:T(8,128)(2,1)S(1)}, bf16[1,128,512]{2,1,0:T(8,128)(2,1)S(1)}, u32[]{:S(2)}, u32[]{:S(2)}) collective-permute-start(bf16[1,128,512]{2,1,0:T(8,128)(2,1)S(1)} %get-tuple-element.64), channel_id=1, source_target_pairs={{0,2},{1,3},{2,4},{3,5},{4,6},{5,7},{6,8},{7,9},{8,10},{9,11},{10,... | collective-permute-start | bytes 393224 | tf_op jit(solution)/shard_map/ppermute | solution.py:15
  266.0 6.8 %collective-permute-done.40 = bf16[1,128,512]{2,1,0:T(8,128)(2,1)S(1)} collective-permute-done((bf16[1,128,512]{2,1,0:T(8,128)(2,1)S(1)}, bf16[1,128,512]{2,1,0:T(8,128)(2,1)S(1)}, u32[]{:S(2)}, u32[]{:S(2)}) %collective-permute-start.40) | collective-permute-done | bytes 131104 | tf_op jit(solution)/shard_map/ppermute | solution.py:15
  284.0 6.7 %collective-permute-start.47 = (bf16[1,128,512]{2,1,0:T(8,128)(2,1)S(1)}, bf16[1,128,512]{2,1,0:T(8,128)(2,1)S(1)}, u32[]{:S(2)}, u32[]{:S(2)}) collective-permute-start(bf16[1,128,512]{2,1,0:T(8,128)(2,1)S(1)} %get-tuple-element.60), channel_id=1, source_target_pairs={{0,2},{1,3},{2,4},{3,5},{4,6},{5,7},{6,8},{7,9},{8,10},{9,11},{10,... | collective-permute-start | bytes 393224 | tf_op jit(solution)/shard_map/ppermute | solution.py:15
  295.3 6.9 %collective-permute-done.45 = bf16[1,128,512]{2,1,0:T(8,128)(2,1)S(1)} collective-permute-done((bf16[1,128,512]{2,1,0:T(8,128)(2,1)S(1)}, bf16[1,128,512]{2,1,0:T(8,128)(2,1)S(1)}, u32[]{:S(2)}, u32[]{:S(2)}) %collective-permute-start.45) | collective-permute-done | bytes 131104 | tf_op jit(solution)/shard_map/ppermute | solution.py:15
  313.3 6.7 %collective-permute-start.52 = (bf16[1,128,512]{2,1,0:T(8,128)(2,1)S(1)}, bf16[1,128,512]{2,1,0:T(8,128)(2,1)S(1)}, u32[]{:S(2)}, u32[]{:S(2)}) collective-permute-start(bf16[1,128,512]{2,1,0:T(8,128)(2,1)S(1)} %get-tuple-element.56), channel_id=1, source_target_pairs={{0,2},{1,3},{2,4},{3,5},{4,6},{5,7},{6,8},{7,9},{8,10},{9,11},{10,... | collective-permute-start | bytes 393224 | tf_op jit(solution)/shard_map/ppermute | solution.py:15
  324.7 6.9 %collective-permute-done.50 = bf16[1,128,512]{2,1,0:T(8,128)(2,1)S(1)} collective-permute-done((bf16[1,128,512]{2,1,0:T(8,128)(2,1)S(1)}, bf16[1,128,512]{2,1,0:T(8,128)(2,1)S(1)}, u32[]{:S(2)}, u32[]{:S(2)}) %collective-permute-start.50) | collective-permute-done | bytes 131104 | tf_op jit(solution)/shard_map/ppermute | solution.py:15
  334.3 3.5 collective-permute-done.53
  342.6 6.7 %collective-permute-start.57 = (bf16[1,128,512]{2,1,0:T(8,128)(2,1)S(1)}, bf16[1,128,512]{2,1,0:T(8,128)(2,1)S(1)}, u32[]{:S(2)}, u32[]{:S(2)}) collective-permute-start(bf16[1,128,512]{2,1,0:T(8,128)(2,1)S(1)} %get-tuple-element.52), channel_id=1, source_target_pairs={{0,2},{1,3},{2,4},{3,5},{4,6},{5,7},{6,8},{7,9},{8,10},{9,11},{10,... | collective-permute-start | bytes 393224 | tf_op jit(solution)/shard_map/ppermute | solution.py:15
  354.0 6.9 %collective-permute-done.55 = bf16[1,128,512]{2,1,0:T(8,128)(2,1)S(1)} collective-permute-done((bf16[1,128,512]{2,1,0:T(8,128)(2,1)S(1)}, bf16[1,128,512]{2,1,0:T(8,128)(2,1)S(1)}, u32[]{:S(2)}, u32[]{:S(2)}) %collective-permute-start.55) | collective-permute-done | bytes 131104 | tf_op jit(solution)/shard_map/ppermute | solution.py:15
  371.9 6.7 %collective-permute-start.62 = (bf16[1,128,512]{2,1,0:T(8,128)(2,1)S(1)}, bf16[1,128,512]{2,1,0:T(8,128)(2,1)S(1)}, u32[]{:S(2)}, u32[]{:S(2)}) collective-permute-start(bf16[1,128,512]{2,1,0:T(8,128)(2,1)S(1)} %get-tuple-element.48), channel_id=1, source_target_pairs={{0,2},{1,3},{2,4},{3,5},{4,6},{5,7},{6,8},{7,9},{8,10},{9,11},{10,... | collective-permute-start | bytes 393224 | tf_op jit(solution)/shard_map/ppermute | solution.py:15
  383.3 6.8 %collective-permute-done.60 = bf16[1,128,512]{2,1,0:T(8,128)(2,1)S(1)} collective-permute-done((bf16[1,128,512]{2,1,0:T(8,128)(2,1)S(1)}, bf16[1,128,512]{2,1,0:T(8,128)(2,1)S(1)}, u32[]{:S(2)}, u32[]{:S(2)}) %collective-permute-start.60) | collective-permute-done | bytes 131104 | tf_op jit(solution)/shard_map/ppermute | solution.py:15
  401.2 6.7 %collective-permute-start.67 = (bf16[1,128,512]{2,1,0:T(8,128)(2,1)S(1)}, bf16[1,128,512]{2,1,0:T(8,128)(2,1)S(1)}, u32[]{:S(2)}, u32[]{:S(2)}) collective-permute-start(bf16[1,128,512]{2,1,0:T(8,128)(2,1)S(1)} %get-tuple-element.44), channel_id=1, source_target_pairs={{0,2},{1,3},{2,4},{3,5},{4,6},{5,7},{6,8},{7,9},{8,10},{9,11},{10,... | collective-permute-start | bytes 393224 | tf_op jit(solution)/shard_map/ppermute | solution.py:15
  412.6 6.9 %collective-permute-done.65 = bf16[1,128,512]{2,1,0:T(8,128)(2,1)S(1)} collective-permute-done((bf16[1,128,512]{2,1,0:T(8,128)(2,1)S(1)}, bf16[1,128,512]{2,1,0:T(8,128)(2,1)S(1)}, u32[]{:S(2)}, u32[]{:S(2)}) %collective-permute-start.65) | collective-permute-done | bytes 131104 | tf_op jit(solution)/shard_map/ppermute | solution.py:15
  (435 shorter events, 234.8 us)
Async XLA Ops:
  4.1 17.4 %collective-permute-start.3 = (bf16[1,128,512]{2,1,0:T(8,128)(2,1)S(1)}, bf16[1,128,512]{2,1,0:T(8,128)(2,1)S(1)}, u32[]{:S(2)}, u32[]{:S(2)}) collective-permute-start(bf16[1,128,512]{2,1,0:T(8,128)(2,1)S(1)} %fusion.35), channel_id=1, source_target_pairs={{2,0},{3,1},{4,2},{5,3},{6,4},{7,5},{8,6},{9,7},{10,8},{11,9},{12,... | collective-permute-start | bytes 393224 | tf_op jit(solution)/shard_map/ppermute | solution.py:15
  6.5 15.0 %collective-permute-start.2 = (bf16[1,128,512]{2,1,0:T(8,128)(2,1)S(1)}, bf16[1,128,512]{2,1,0:T(8,128)(2,1)S(1)}, u32[]{:S(2)}, u32[]{:S(2)}) collective-permute-start(bf16[1,128,512]{2,1,0:T(8,128)(2,1)S(1)} %fusion.35), channel_id=1, source_target_pairs={{1,0},{2,1},{3,2},{4,3},{5,4},{6,5},{7,6},{8,7},{9,8},{10,9},{11,1... | collective-permute-start | bytes 393224 | tf_op jit(solution)/shard_map/ppermute | solution.py:15
  9.4 12.1 %collective-permute-start.1 = (bf16[1,128,512]{2,1,0:T(8,128)(2,1)S(1)}, bf16[1,128,512]{2,1,0:T(8,128)(2,1)S(1)}, u32[]{:S(2)}, u32[]{:S(2)}) collective-permute-start(bf16[1,128,512]{2,1,0:T(8,128)(2,1)S(1)} %fusion.35), channel_id=1, source_target_pairs={{0,1},{1,2},{2,3},{3,4},{4,5},{5,6},{6,7},{7,8},{8,9},{9,10},{10,1... | collective-permute-start | bytes 393224 | tf_op jit(solution)/shard_map/ppermute | solution.py:15
  30.4 21.5 %collective-permute-start.8 = (bf16[1,128,512]{2,1,0:T(8,128)(2,1)S(1)}, bf16[1,128,512]{2,1,0:T(8,128)(2,1)S(1)}, u32[]{:S(2)}, u32[]{:S(2)}) collective-permute-start(bf16[1,128,512]{2,1,0:T(8,128)(2,1)S(1)} %fusion.36), channel_id=1, source_target_pairs={{2,0},{3,1},{4,2},{5,3},{6,4},{7,5},{8,6},{9,7},{10,8},{11,9},{12,... | collective-permute-start | bytes 393224 | tf_op jit(solution)/shard_map/ppermute | solution.py:15
  32.4 18.9 %collective-permute-start.7 = (bf16[1,128,512]{2,1,0:T(8,128)(2,1)S(1)}, bf16[1,128,512]{2,1,0:T(8,128)(2,1)S(1)}, u32[]{:S(2)}, u32[]{:S(2)}) collective-permute-start(bf16[1,128,512]{2,1,0:T(8,128)(2,1)S(1)} %fusion.36), channel_id=1, source_target_pairs={{1,0},{2,1},{3,2},{4,3},{5,4},{6,5},{7,6},{8,7},{9,8},{10,9},{11,1... | collective-permute-start | bytes 393224 | tf_op jit(solution)/shard_map/ppermute | solution.py:15
  35.7 14.3 %collective-permute-start.6 = (bf16[1,128,512]{2,1,0:T(8,128)(2,1)S(1)}, bf16[1,128,512]{2,1,0:T(8,128)(2,1)S(1)}, u32[]{:S(2)}, u32[]{:S(2)}) collective-permute-start(bf16[1,128,512]{2,1,0:T(8,128)(2,1)S(1)} %fusion.36), channel_id=1, source_target_pairs={{0,1},{1,2},{2,3},{3,4},{4,5},{5,6},{6,7},{7,8},{8,9},{9,10},{10,1... | collective-permute-start | bytes 393224 | tf_op jit(solution)/shard_map/ppermute | solution.py:15
  63.4 20.4 %collective-permute-start.13 = (bf16[1,128,512]{2,1,0:T(8,128)(2,1)S(1)}, bf16[1,128,512]{2,1,0:T(8,128)(2,1)S(1)}, u32[]{:S(2)}, u32[]{:S(2)}) collective-permute-start(bf16[1,128,512]{2,1,0:T(8,128)(2,1)S(1)} %fusion.37), channel_id=1, source_target_pairs={{2,0},{3,1},{4,2},{5,3},{6,4},{7,5},{8,6},{9,7},{10,8},{11,9},{12,... | collective-permute-start | bytes 393224 | tf_op jit(solution)/shard_map/ppermute | solution.py:15
  65.3 17.8 %collective-permute-start.12 = (bf16[1,128,512]{2,1,0:T(8,128)(2,1)S(1)}, bf16[1,128,512]{2,1,0:T(8,128)(2,1)S(1)}, u32[]{:S(2)}, u32[]{:S(2)}) collective-permute-start(bf16[1,128,512]{2,1,0:T(8,128)(2,1)S(1)} %fusion.37), channel_id=1, source_target_pairs={{1,0},{2,1},{3,2},{4,3},{5,4},{6,5},{7,6},{8,7},{9,8},{10,9},{11,1... | collective-permute-start | bytes 393224 | tf_op jit(solution)/shard_map/ppermute | solution.py:15
  67.9 14.0 %collective-permute-start.11 = (bf16[1,128,512]{2,1,0:T(8,128)(2,1)S(1)}, bf16[1,128,512]{2,1,0:T(8,128)(2,1)S(1)}, u32[]{:S(2)}, u32[]{:S(2)}) collective-permute-start(bf16[1,128,512]{2,1,0:T(8,128)(2,1)S(1)} %fusion.37), channel_id=1, source_target_pairs={{0,1},{1,2},{2,3},{3,4},{4,5},{5,6},{6,7},{7,8},{8,9},{9,10},{10,1... | collective-permute-start | bytes 393224 | tf_op jit(solution)/shard_map/ppermute | solution.py:15
  95.7 20.4 %collective-permute-start.18 = (bf16[1,128,512]{2,1,0:T(8,128)(2,1)S(1)}, bf16[1,128,512]{2,1,0:T(8,128)(2,1)S(1)}, u32[]{:S(2)}, u32[]{:S(2)}) collective-permute-start(bf16[1,128,512]{2,1,0:T(8,128)(2,1)S(1)} %fusion.38), channel_id=1, source_target_pairs={{2,0},{3,1},{4,2},{5,3},{6,4},{7,5},{8,6},{9,7},{10,8},{11,9},{12,... | collective-permute-start | bytes 393224 | tf_op jit(solution)/shard_map/ppermute | solution.py:15
  97.6 17.8 %collective-permute-start.17 = (bf16[1,128,512]{2,1,0:T(8,128)(2,1)S(1)}, bf16[1,128,512]{2,1,0:T(8,128)(2,1)S(1)}, u32[]{:S(2)}, u32[]{:S(2)}) collective-permute-start(bf16[1,128,512]{2,1,0:T(8,128)(2,1)S(1)} %fusion.38), channel_id=1, source_target_pairs={{1,0},{2,1},{3,2},{4,3},{5,4},{6,5},{7,6},{8,7},{9,8},{10,9},{11,1... | collective-permute-start | bytes 393224 | tf_op jit(solution)/shard_map/ppermute | solution.py:15
  100.2 14.0 %collective-permute-start.16 = (bf16[1,128,512]{2,1,0:T(8,128)(2,1)S(1)}, bf16[1,128,512]{2,1,0:T(8,128)(2,1)S(1)}, u32[]{:S(2)}, u32[]{:S(2)}) collective-permute-start(bf16[1,128,512]{2,1,0:T(8,128)(2,1)S(1)} %fusion.38), channel_id=1, source_target_pairs={{0,1},{1,2},{2,3},{3,4},{4,5},{5,6},{6,7},{7,8},{8,9},{9,10},{10,1... | collective-permute-start | bytes 393224 | tf_op jit(solution)/shard_map/ppermute | solution.py:15
  128.0 20.4 %collective-permute-start.23 = (bf16[1,128,512]{2,1,0:T(8,128)(2,1)S(1)}, bf16[1,128,512]{2,1,0:T(8,128)(2,1)S(1)}, u32[]{:S(2)}, u32[]{:S(2)}) collective-permute-start(bf16[1,128,512]{2,1,0:T(8,128)(2,1)S(1)} %fusion.39), channel_id=1, source_target_pairs={{2,0},{3,1},{4,2},{5,3},{6,4},{7,5},{8,6},{9,7},{10,8},{11,9},{12,... | collective-permute-start | bytes 393224 | tf_op jit(solution)/shard_map/ppermute | solution.py:15
  129.9 17.8 %collective-permute-start.22 = (bf16[1,128,512]{2,1,0:T(8,128)(2,1)S(1)}, bf16[1,128,512]{2,1,0:T(8,128)(2,1)S(1)}, u32[]{:S(2)}, u32[]{:S(2)}) collective-permute-start(bf16[1,128,512]{2,1,0:T(8,128)(2,1)S(1)} %fusion.39), channel_id=1, source_target_pairs={{1,0},{2,1},{3,2},{4,3},{5,4},{6,5},{7,6},{8,7},{9,8},{10,9},{11,1... | collective-permute-start | bytes 393224 | tf_op jit(solution)/shard_map/ppermute | solution.py:15
  132.4 14.0 %collective-permute-start.21 = (bf16[1,128,512]{2,1,0:T(8,128)(2,1)S(1)}, bf16[1,128,512]{2,1,0:T(8,128)(2,1)S(1)}, u32[]{:S(2)}, u32[]{:S(2)}) collective-permute-start(bf16[1,128,512]{2,1,0:T(8,128)(2,1)S(1)} %fusion.39), channel_id=1, source_target_pairs={{0,1},{1,2},{2,3},{3,4},{4,5},{5,6},{6,7},{7,8},{8,9},{9,10},{10,1... | collective-permute-start | bytes 393224 | tf_op jit(solution)/shard_map/ppermute | solution.py:15
  160.2 20.4 %collective-permute-start.28 = (bf16[1,128,512]{2,1,0:T(8,128)(2,1)S(1)}, bf16[1,128,512]{2,1,0:T(8,128)(2,1)S(1)}, u32[]{:S(2)}, u32[]{:S(2)}) collective-permute-start(bf16[1,128,512]{2,1,0:T(8,128)(2,1)S(1)} %fusion.40), channel_id=1, source_target_pairs={{2,0},{3,1},{4,2},{5,3},{6,4},{7,5},{8,6},{9,7},{10,8},{11,9},{12,... | collective-permute-start | bytes 393224 | tf_op jit(solution)/shard_map/ppermute | solution.py:15
  162.2 17.8 %collective-permute-start.27 = (bf16[1,128,512]{2,1,0:T(8,128)(2,1)S(1)}, bf16[1,128,512]{2,1,0:T(8,128)(2,1)S(1)}, u32[]{:S(2)}, u32[]{:S(2)}) collective-permute-start(bf16[1,128,512]{2,1,0:T(8,128)(2,1)S(1)} %fusion.40), channel_id=1, source_target_pairs={{1,0},{2,1},{3,2},{4,3},{5,4},{6,5},{7,6},{8,7},{9,8},{10,9},{11,1... | collective-permute-start | bytes 393224 | tf_op jit(solution)/shard_map/ppermute | solution.py:15
  164.7 14.0 %collective-permute-start.26 = (bf16[1,128,512]{2,1,0:T(8,128)(2,1)S(1)}, bf16[1,128,512]{2,1,0:T(8,128)(2,1)S(1)}, u32[]{:S(2)}, u32[]{:S(2)}) collective-permute-start(bf16[1,128,512]{2,1,0:T(8,128)(2,1)S(1)} %fusion.40), channel_id=1, source_target_pairs={{0,1},{1,2},{2,3},{3,4},{4,5},{5,6},{6,7},{7,8},{8,9},{9,10},{10,1... | collective-permute-start | bytes 393224 | tf_op jit(solution)/shard_map/ppermute | solution.py:15
  192.9 21.9 %collective-permute-start.33 = (bf16[1,128,512]{2,1,0:T(8,128)(2,1)S(1)}, bf16[1,128,512]{2,1,0:T(8,128)(2,1)S(1)}, u32[]{:S(2)}, u32[]{:S(2)}) collective-permute-start(bf16[1,128,512]{2,1,0:T(8,128)(2,1)S(1)} %fusion.41), channel_id=1, source_target_pairs={{2,0},{3,1},{4,2},{5,3},{6,4},{7,5},{8,6},{9,7},{10,8},{11,9},{12,... | collective-permute-start | bytes 393224 | tf_op jit(solution)/shard_map/ppermute | solution.py:15
  194.9 19.8 %collective-permute-start.32 = (bf16[1,128,512]{2,1,0:T(8,128)(2,1)S(1)}, bf16[1,128,512]{2,1,0:T(8,128)(2,1)S(1)}, u32[]{:S(2)}, u32[]{:S(2)}) collective-permute-start(bf16[1,128,512]{2,1,0:T(8,128)(2,1)S(1)} %fusion.41), channel_id=1, source_target_pairs={{1,0},{2,1},{3,2},{4,3},{5,4},{6,5},{7,6},{8,7},{9,8},{10,9},{11,1... | collective-permute-start | bytes 393224 | tf_op jit(solution)/shard_map/ppermute | solution.py:15
  197.5 17.2 %collective-permute-start.31 = (bf16[1,128,512]{2,1,0:T(8,128)(2,1)S(1)}, bf16[1,128,512]{2,1,0:T(8,128)(2,1)S(1)}, u32[]{:S(2)}, u32[]{:S(2)}) collective-permute-start(bf16[1,128,512]{2,1,0:T(8,128)(2,1)S(1)} %fusion.41), channel_id=1, source_target_pairs={{0,1},{1,2},{2,3},{3,4},{4,5},{5,6},{6,7},{7,8},{8,9},{9,10},{10,1... | collective-permute-start | bytes 393224 | tf_op jit(solution)/shard_map/ppermute | solution.py:15
  223.1 13.4 %collective-permute-start.34 = (bf16[1,128,512]{2,1,0:T(8,128)(2,1)S(1)}, bf16[1,128,512]{2,1,0:T(8,128)(2,1)S(1)}, u32[]{:S(2)}, u32[]{:S(2)}) collective-permute-start(bf16[1,128,512]{2,1,0:T(8,128)(2,1)S(1)} %get-tuple-element.67), channel_id=1, source_target_pairs={{2,0},{3,1},{4,2},{5,3},{6,4},{7,5},{8,6},{9,7},{10,8},{11,9},{12,... | collective-permute-start | bytes 393224 | tf_op jit(solution)/shard_map/ppermute | solution.py:15
  225.0 11.4 %collective-permute-start.37 = (bf16[1,128,512]{2,1,0:T(8,128)(2,1)S(1)}, bf16[1,128,512]{2,1,0:T(8,128)(2,1)S(1)}, u32[]{:S(2)}, u32[]{:S(2)}) collective-permute-start(bf16[1,128,512]{2,1,0:T(8,128)(2,1)S(1)} %get-tuple-element.68), channel_id=1, source_target_pairs={{0,2},{1,3},{2,4},{3,5},{4,6},{5,7},{6,8},{7,9},{8,10},{9,11},{10,... | collective-permute-start | bytes 393224 | tf_op jit(solution)/shard_map/ppermute | solution.py:15
  252.7 13.3 %collective-permute-start.39 = (bf16[1,128,512]{2,1,0:T(8,128)(2,1)S(1)}, bf16[1,128,512]{2,1,0:T(8,128)(2,1)S(1)}, u32[]{:S(2)}, u32[]{:S(2)}) collective-permute-start(bf16[1,128,512]{2,1,0:T(8,128)(2,1)S(1)} %get-tuple-element.63), channel_id=1, source_target_pairs={{2,0},{3,1},{4,2},{5,3},{6,4},{7,5},{8,6},{9,7},{10,8},{11,9},{12,... | collective-permute-start | bytes 393224 | tf_op jit(solution)/shard_map/ppermute | solution.py:15
  254.6 11.4 %collective-permute-start.42 = (bf16[1,128,512]{2,1,0:T(8,128)(2,1)S(1)}, bf16[1,128,512]{2,1,0:T(8,128)(2,1)S(1)}, u32[]{:S(2)}, u32[]{:S(2)}) collective-permute-start(bf16[1,128,512]{2,1,0:T(8,128)(2,1)S(1)} %get-tuple-element.64), channel_id=1, source_target_pairs={{0,2},{1,3},{2,4},{3,5},{4,6},{5,7},{6,8},{7,9},{8,10},{9,11},{10,... | collective-permute-start | bytes 393224 | tf_op jit(solution)/shard_map/ppermute | solution.py:15
  282.0 13.3 %collective-permute-start.44 = (bf16[1,128,512]{2,1,0:T(8,128)(2,1)S(1)}, bf16[1,128,512]{2,1,0:T(8,128)(2,1)S(1)}, u32[]{:S(2)}, u32[]{:S(2)}) collective-permute-start(bf16[1,128,512]{2,1,0:T(8,128)(2,1)S(1)} %get-tuple-element.59), channel_id=1, source_target_pairs={{2,0},{3,1},{4,2},{5,3},{6,4},{7,5},{8,6},{9,7},{10,8},{11,9},{12,... | collective-permute-start | bytes 393224 | tf_op jit(solution)/shard_map/ppermute | solution.py:15
  311.4 13.3 %collective-permute-start.49 = (bf16[1,128,512]{2,1,0:T(8,128)(2,1)S(1)}, bf16[1,128,512]{2,1,0:T(8,128)(2,1)S(1)}, u32[]{:S(2)}, u32[]{:S(2)}) collective-permute-start(bf16[1,128,512]{2,1,0:T(8,128)(2,1)S(1)} %get-tuple-element.55), channel_id=1, source_target_pairs={{2,0},{3,1},{4,2},{5,3},{6,4},{7,5},{8,6},{9,7},{10,8},{11,9},{12,... | collective-permute-start | bytes 393224 | tf_op jit(solution)/shard_map/ppermute | solution.py:15
  313.3 11.4 %collective-permute-start.52 = (bf16[1,128,512]{2,1,0:T(8,128)(2,1)S(1)}, bf16[1,128,512]{2,1,0:T(8,128)(2,1)S(1)}, u32[]{:S(2)}, u32[]{:S(2)}) collective-permute-start(bf16[1,128,512]{2,1,0:T(8,128)(2,1)S(1)} %get-tuple-element.56), channel_id=1, source_target_pairs={{0,2},{1,3},{2,4},{3,5},{4,6},{5,7},{6,8},{7,9},{8,10},{9,11},{10,... | collective-permute-start | bytes 393224 | tf_op jit(solution)/shard_map/ppermute | solution.py:15
  340.7 13.3 %collective-permute-start.54 = (bf16[1,128,512]{2,1,0:T(8,128)(2,1)S(1)}, bf16[1,128,512]{2,1,0:T(8,128)(2,1)S(1)}, u32[]{:S(2)}, u32[]{:S(2)}) collective-permute-start(bf16[1,128,512]{2,1,0:T(8,128)(2,1)S(1)} %get-tuple-element.51), channel_id=1, source_target_pairs={{2,0},{3,1},{4,2},{5,3},{6,4},{7,5},{8,6},{9,7},{10,8},{11,9},{12,... | collective-permute-start | bytes 393224 | tf_op jit(solution)/shard_map/ppermute | solution.py:15
  370.0 13.3 %collective-permute-start.59 = (bf16[1,128,512]{2,1,0:T(8,128)(2,1)S(1)}, bf16[1,128,512]{2,1,0:T(8,128)(2,1)S(1)}, u32[]{:S(2)}, u32[]{:S(2)}) collective-permute-start(bf16[1,128,512]{2,1,0:T(8,128)(2,1)S(1)} %get-tuple-element.47), channel_id=1, source_target_pairs={{2,0},{3,1},{4,2},{5,3},{6,4},{7,5},{8,6},{9,7},{10,8},{11,9},{12,... | collective-permute-start | bytes 393224 | tf_op jit(solution)/shard_map/ppermute | solution.py:15
  371.9 11.4 %collective-permute-start.62 = (bf16[1,128,512]{2,1,0:T(8,128)(2,1)S(1)}, bf16[1,128,512]{2,1,0:T(8,128)(2,1)S(1)}, u32[]{:S(2)}, u32[]{:S(2)}) collective-permute-start(bf16[1,128,512]{2,1,0:T(8,128)(2,1)S(1)} %get-tuple-element.48), channel_id=1, source_target_pairs={{0,2},{1,3},{2,4},{3,5},{4,6},{5,7},{6,8},{7,9},{8,10},{9,11},{10,... | collective-permute-start | bytes 393224 | tf_op jit(solution)/shard_map/ppermute | solution.py:15
  399.3 13.3 %collective-permute-start.64 = (bf16[1,128,512]{2,1,0:T(8,128)(2,1)S(1)}, bf16[1,128,512]{2,1,0:T(8,128)(2,1)S(1)}, u32[]{:S(2)}, u32[]{:S(2)}) collective-permute-start(bf16[1,128,512]{2,1,0:T(8,128)(2,1)S(1)} %get-tuple-element.43), channel_id=1, source_target_pairs={{2,0},{3,1},{4,2},{5,3},{6,4},{7,5},{8,6},{9,7},{10,8},{11,9},{12,... | collective-permute-start | bytes 393224 | tf_op jit(solution)/shard_map/ppermute | solution.py:15
  (101 other events, 505.2 us)
where the time goes:
time: 424 us; the launch traced here: 422 us
  starting transfers between devices  227 us (54%)
  waiting for transfers between devices  101 us (24%)
  local copies, waits for them, and re-layouts  38.1 us (9%)
  matrix products  35.2 us (8%)
  other arithmetic  16.7 us (4%)
    ppermute x68, starting transfers between devices, from_behind(): lax.ppermute(value, axis, [(source, source + steps) for source in range(i...  227 us
    ppermute x68, waiting for transfers between devices, from_behind(): lax.ppermute(value, axis, [(source, source + steps) for source in range(i...  101 us
    unnamed x159, local copies, waits for them, and re-layouts  22.8 us
    dot_general x7, matrix products, spread_back(): jnp.einsum('wp,pjh->wjh', slot_onehot, contributions, precision=lax.Preci...  13.4 us
    gather x7, local copies, waits for them, and re-layouts, aggregate(): picked = window[slot_index].reshape(-1, feature_count)  9.49 us
  transfers between devices with their start and end apart: 68, of which 25 were waited for; matrix products, arithmetic and copies ran while one was open for 7% of the time, Pallas kernels for 0%

commit v1 on v0

v1 whole, which is shorter than its diff:
```python
import functools

import jax
import jax.numpy as jnp
import numpy as np
from jax import lax
from jax.experimental import pallas as pl
from jax.experimental.pallas import tpu as pltpu
from jax.sharding import Mesh, PartitionSpec as P

EPS = 1e-05
H = 512
B = 128
PAIR = 2 * B
BAND = 3 * PAIR
REACH = 4
W_ROWS = 3 * H + 32
W_HALF = W_ROWS // 2
F32, BF16 = jnp.float32, jnp.bfloat16
VMEM = pl.BlockSpec(memory_space=pltpu.VMEM)
SMEM = pl.BlockSpec(memory_space=pltpu.SMEM)


def rows(index, size=PAIR):
    if isinstance(index, int):
        return pl.ds(index * size, size)
    return pl.ds(pl.multiple_of(index * size, size), size)


def dot(a, b):
    return jnp.dot(a, b, preferred_element_type=F32)


def dot_t(a, b):
    return lax.dot_general(a, b, (((1,), (1,)), ((), ())), preferred_element_type=F32)


def normed_rows(values):
    wide = values.astype(F32)
    centre = wide - jnp.mean(wide, axis=-1, keepdims=True)
    inv = lax.rsqrt(jnp.mean(centre * centre, axis=-1, keepdims=True) + EPS)
    return centre * inv, inv


def call(kernel, outs, specs, scratch, limit_mib, name, flops=0):
    return pl.pallas_call(
        kernel,
        out_shape=[jax.ShapeDtypeStruct(s, d) for s, d in outs],
        in_specs=specs,
        out_specs=[VMEM] * len(outs),
        scratch_shapes=scratch,
        compiler_params=pltpu.CompilerParams(vmem_limit_bytes=limit_mib << 20),
        name=name,
    )


def prepare_kernel(ids, source, live, latent, cotangent, w_a, w_b, w_c, gain, tiles, own, weights):
    sample = ids[0]
    own[:, 0:H] = latent[sample]
    own[:, H + BAND :] = cotangent[sample]
    slots = tiles.shape[0]
    base = 2 * (ids[2] - 1)
    for column in range(6):
        total = jnp.zeros((B, B), F32)
        for slot in range(slots):
            hit = (source[slot] - base == column) & (slot < live[0])
            total = total + jnp.where(hit, tiles[slot].astype(F32), 0.0)
        own[:, H + column * B : H + (column + 1) * B] = total.astype(BF16)
    weights[0:H, :] = w_a[0]
    weights[H : 2 * H, :] = w_b[0]
    weights[2 * H : 3 * H, :] = w_c[0]
    rest = jnp.broadcast_to(gain[0:1, :], (16, H))
    high = rest.astype(BF16).astype(F32)
    rest = rest - high
    mid = rest.astype(BF16).astype(F32)
    low = rest - mid
    row = lax.broadcasted_iota(jnp.int32, (16, H), 0)
    terms = jnp.where(row == 0, high, jnp.where(row == 1, mid, jnp.where(row == 2, low, 0.0)))
    weights[3 * H : 3 * H + 16, :] = terms.astype(BF16)
    weights[3 * H + 16 : 3 * H + 32, :] = jnp.zeros((16, H), BF16)


def layer_gain(weights, layer):
    terms = weights[layer * W_ROWS + 3 * H : layer * W_ROWS + 3 * H + 16, :].astype(F32)
    return jnp.sum(terms, axis=0, keepdims=True)


def weight(weights, layer, which):
    start = layer * W_ROWS + which * H
    return weights[start : start + H, :]


def forward_kernel(
    ids, own, m1, m2, m3, m4, t1, t2, t3, t4, w_own, w_m, w_t, w_mh, w_th,
    latents, grad_pre, turned, v3_out, v2_out, v1_out, v0_out, f2_out, f1_out, f0_out, weights,
    v_a, v_b, band, unit, source,
):
    section, core = ids[0], ids[1]
    weights[pl.ds(pl.multiple_of(section * W_ROWS, 16), W_ROWS), :] = w_own[...]
    before, after = (section + 3) % 4, (section + 1) % 4
    mine = jnp.where(core == 0, before, after)
    theirs = jnp.where(core == 0, after, before)
    far = (section + 2) % 4
    weights[pl.ds(pl.multiple_of(mine * W_ROWS, 16), W_ROWS), :] = w_m[...]
    weights[pl.ds(pl.multiple_of(theirs * W_ROWS, 16), W_ROWS), :] = w_t[...]
    weights[pl.ds(pl.multiple_of(far * W_ROWS + core * W_HALF, 16), W_HALF), :] = w_mh[...]
    weights[pl.ds(pl.multiple_of(far * W_ROWS + (1 - core) * W_HALF, 16), W_HALF), :] = w_th[...]

    v_a[rows(REACH), :] = own[:, 0:H]
    band[rows(REACH - 1), :] = own[:, H : H + BAND]
    for step, (m, t) in enumerate(((m1, t1), (m2, t2), (m3, t3), (m4, t4)), start=1):
        at_m = REACH - step + 2 * step * core
        at_t = 2 * REACH - at_m
        v_a[rows(at_m), :] = m[:, 0:H]
        v_a[rows(at_t), :] = t[:, 0:H]
        if step < REACH:
            band[rows(at_m - 1), :] = m[:, H : H + BAND]
            band[rows(at_t - 1), :] = t[:, H : H + BAND]

    mine_rows = rows(core, B)
    v0_out[...] = own[:, 0:H]
    now, later = v_a, v_b
    for layer in range(4):
        low, high = layer, 2 * REACH - layer
        gain = layer_gain(weights, layer)

        def project(j):
            value, _ = normed_rows(now[rows(j), :])
            held = (value * gain).astype(BF16)
            unit[rows(j), :] = held
            source[rows(j), :] = dot(held, weight(weights, layer, 0)).astype(BF16)

        def update(j):
            window = source[pl.ds(pl.multiple_of((j - 1) * PAIR, PAIR), BAND), :]
            pre = dot(band[rows(j - 1), :], window)
            pre = pre + dot(unit[rows(j), :], weight(weights, layer, 1))
            sigma = 1.0 / (1.0 + jnp.exp(-pre))
            act = (pre * sigma).astype(BF16)
            value = now[rows(j), :].astype(F32) + dot(act, weight(weights, layer, 2))
            later[rows(j), :] = value.astype(BF16)
            return sigma * (1.0 + pre * (1.0 - sigma))

        def step(j, carry):
            factor = update(j)
            if layer == 1:
                f1_out[rows(j - 2), :] = factor
            if layer in (0, 2):
                out = f0_out if layer == 0 else f2_out
                if layer == 2:
                    out[rows(j - 3), :] = factor
                else:
                    @pl.when((j >= 3) & (j <= 5))
                    def _():
                        out[rows(j - 3), :] = factor
            project(j + 2)
            return carry

        def first(j, carry):
            project(j)
            return carry

        lax.fori_loop(low, low + 3, first, 0)
        if layer < 3:
            lax.fori_loop(low + 1, high - 1, step, 0)
            factor = update(high - 1)
            if layer == 1:
                f1_out[rows(high - 3), :] = factor
            if layer == 2:
                f2_out[rows(high - 4), :] = factor
        else:
            factor = update(REACH)
            incoming = dot_t(own[:, H + BAND :], weight(weights, 3, 2))
            grad_pre[...] = (incoming * factor).astype(BF16)
        latents[layer] = later[pl.ds(pl.multiple_of(REACH * PAIR + core * B, B), B), :]
        if layer == 0:
            v1_out[...] = later[3 * PAIR : 6 * PAIR, :]
        if layer == 1:
            v2_out[...] = later[4 * PAIR : 5 * PAIR, :]
        if layer == 2:
            v3_out[...] = later[3 * PAIR : 6 * PAIR, :]
        now, later = later, now

    for j in range(3, 6):
        for i in range(j - 1, j + 2):
            column = (j - i + 1) * PAIR
            piece = band[(i - 1) * PAIR : i * PAIR, column : column + PAIR]
            turned[(j - 3) * PAIR : (j - 2) * PAIR, (i - j + 1) * PAIR : (i - j + 2) * PAIR] = (
                piece.astype(F32).T.astype(BF16)
            )


def grad_pair(gradient, grad_pre, window, turned, values, weights, layer):
    back = dot(turned, window).astype(BF16)
    grad_unit = dot_t(grad_pre, weight(weights, layer, 1))
    grad_unit = grad_unit + dot_t(back, weight(weights, layer, 0))
    normed, inv = normed_rows(values)
    e = grad_unit * layer_gain(weights, layer)
    grad_in = inv * (
        e
        - jnp.mean(e, axis=-1, keepdims=True)
        - normed * jnp.mean(e * normed, axis=-1, keepdims=True)
    )
    return (gradient.astype(F32) + grad_in).astype(BF16)


def place(target, own, received, other, core, steps, offset):
    target[rows(offset), :] = own
    for step in range(1, steps + 1):
        at_m = offset - step + 2 * step * core
        at_t = 2 * offset - at_m
        target[rows(at_m), :] = received[(step - 1) * PAIR : step * PAIR, :]
        target[rows(at_t), :] = other[(step - 1) * PAIR : step * PAIR, :]


def backward_a_kernel(
    ids, grad_pre, received, other, own, m1, t1, turned, v3, v2, f2, weights,
    g3_out, g2_out, held, cot, g3, gp2,
):
    core = ids[1]
    place(held, grad_pre[...], received, other, core, 2, 2)
    cot[rows(1), :] = own[...]
    cot[rows(2 * core), :] = m1[...]
    cot[rows(2 - 2 * core), :] = t1[...]
    for j in range(3):
        g3[rows(j), :] = grad_pair(
            cot[rows(j), :], held[rows(j + 1), :], held[j * PAIR : j * PAIR + BAND, :],
            turned[rows(j), :], v3[rows(j), :], weights, 3,
        )
        gp2[rows(j), :] = (dot_t(g3[rows(j), :], weight(weights, 2, 2)) * f2[rows(j), :]).astype(BF16)
    g3_out[...] = g3[pl.ds(pl.multiple_of(PAIR + core * B, B), B), :]
    g2_out[...] = grad_pair(
        g3[rows(1), :], gp2[rows(1), :], gp2[...], turned[rows(1), :], v2[...], weights, 2
    )


def backward_b_kernel(
    ids, g2_own, received, other, turned, v1, v0, f1, f0, weights,
    g1_out, g0_out, g2, gp1, g1, gp0,
):
    core = ids[1]
    place(g2, g2_own[...], received, other, core, 2, 2)
    for j in range(5):
        gp1[rows(j), :] = (dot_t(g2[rows(j), :], weight(weights, 1, 2)) * f1[rows(j), :]).astype(BF16)
    for j in range(3):
        g1[rows(j), :] = grad_pair(
            g2[rows(j + 1), :], gp1[rows(j + 1), :], gp1[j * PAIR : j * PAIR + BAND, :],
            turned[rows(j), :], v1[rows(j), :], weights, 1,
        )
        gp0[rows(j), :] = (dot_t(g1[rows(j), :], weight(weights, 0, 2)) * f0[rows(j), :]).astype(BF16)
    g1_out[...] = g1[pl.ds(pl.multiple_of(PAIR + core * B, B), B), :]
    g0 = grad_pair(g1[rows(1), :], gp0[rows(1), :], gp0[...], turned[rows(1), :], v0[...], weights, 0)
    g1[rows(0), :] = g0
    g0_out[...] = g1[rows(core, B), :]


def swap(value):
    return lax.ppermute(value, "core", [(0, 1), (1, 0)])


def spread(value, steps):
    chips = lax.axis_size("chip")
    pairs = []
    for c in range(chips):
        if c + steps < chips:
            pairs.append((2 * c, 2 * (c + steps)))
        if c - steps >= 0:
            pairs.append((2 * c + 1, 2 * (c - steps) + 1))
    return lax.ppermute(value, ("chip", "core"), pairs)


def around(value):
    count = lax.axis_size("section")
    pairs = []
    for s in range(count):
        pairs.append((2 * s, 2 * ((s + 1) % count)))
        pairs.append((2 * s + 1, 2 * ((s - 1) % count) + 1))
    return lax.ppermute(value, ("section", "core"), pairs)


def to_layers(stacked, section):
    count = stacked.shape[0]
    out = jnp.zeros_like(stacked)
    keep = lax.dynamic_index_in_dim(stacked, section, 0, keepdims=True)
    out = lax.dynamic_update_slice_in_dim(out, keep, section, 0)
    for step in range(1, count):
        piece = lax.dynamic_index_in_dim(stacked, (section + step) % count, 0, keepdims=True)
        got = lax.ppermute(piece, "section", [(s, (s + step) % count) for s in range(count)])
        out = lax.dynamic_update_slice_in_dim(out, got, (section - step) % count, 0)
    return out


def body(latent, cotangent, w_a, w_b, w_c, gain, tiles, pair_source, live_pairs):
    section, core, chip = lax.axis_index("section"), lax.axis_index("core"), lax.axis_index("chip")
    ids = jnp.stack([section, core, chip]).astype(jnp.int32)
    wide = H + BAND

    own, w_own = call(
        prepare_kernel,
        [((B, wide + H), BF16), ((W_ROWS, H), BF16)],
        [SMEM, SMEM, SMEM] + [VMEM] * 7,
        [],
        32,
        "prepare",
    )(ids, pair_source, live_pairs, latent, cotangent, w_a, w_b, w_c, gain, tiles)

    w_m = around(w_own)
    partner = swap(own)
    first = jnp.where(core == 0, own, partner)
    second = jnp.where(core == 0, partner, own)
    pair = jnp.concatenate([first, second], axis=0)
    m1 = spread(pair, 1)
    near = pair[:, :wide]
    m2, m3 = spread(near, 2), spread(near, 3)
    m4 = spread(pair[:, :H], 4)
    w_mh = around(lax.dynamic_slice_in_dim(w_m, core * W_HALF, W_HALF, 0))
    w_t, w_th = swap(w_m), swap(w_mh)
    t1, t2, t3, t4 = swap(m1), swap(m2), swap(m3), swap(m4)

    span = 2 * REACH + 1
    latents, grad_pre, turned, v3, v2, v1, v0, f2, f1, f0, weights = call(
        forward_kernel,
        [
            ((4, B, H), BF16), ((PAIR, H), BF16), ((3 * PAIR, BAND), BF16),
            ((3 * PAIR, H), BF16), ((PAIR, H), BF16), ((3 * PAIR, H), BF16), ((PAIR, H), BF16),
            ((3 * PAIR, H), F32), ((5 * PAIR, H), F32), ((3 * PAIR, H), F32),
            ((4 * W_ROWS, H), BF16),
        ],
        [SMEM] + [VMEM] * 14,
        [
            pltpu.VMEM((span * PAIR, H), BF16), pltpu.VMEM((span * PAIR, H), BF16),
            pltpu.VMEM(((span - 2) * PAIR, BAND), BF16),
            pltpu.VMEM((span * PAIR, H), BF16), pltpu.VMEM((span * PAIR, H), BF16),
        ],
        56,
        "forward",
    )(ids, pair, m1, m2, m3, m4, t1, t2, t3, t4, w_own, w_m, w_t, w_mh, w_th)

    received = jnp.concatenate([spread(grad_pre, 1), spread(grad_pre, 2)], axis=0)
    other = swap(received)
    g3, g2 = call(
        backward_a_kernel,
        [((B, H), BF16), ((PAIR, H), BF16)],
        [SMEM] + [VMEM] * 11,
        [
            pltpu.VMEM((5 * PAIR, H), BF16), pltpu.VMEM((3 * PAIR, H), BF16),
            pltpu.VMEM((3 * PAIR, H), BF16), pltpu.VMEM((3 * PAIR, H), BF16),
        ],
        40,
        "backward_a",
    )(ids, grad_pre, received, other, pair[:, wide:], m1[:, wide:], t1[:, wide:], turned, v3, v2, f2, weights)

    latent_result = to_layers(latents, section)

    received = jnp.concatenate([spread(g2, 1), spread(g2, 2)], axis=0)
    other = swap(received)
    g1, g0 = call(
        backward_b_kernel,
        [((B, H), BF16), ((B, H), BF16)],
        [SMEM] + [VMEM] * 9,
        [
            pltpu.VMEM((5 * PAIR, H), BF16), pltpu.VMEM((5 * PAIR, H), BF16),
            pltpu.VMEM((3 * PAIR, H), BF16), pltpu.VMEM((3 * PAIR, H), BF16),
        ],
        40,
        "backward_b",
    )(ids, g2, received, other, turned, v1, v0, f1, f0, weights)

    g2_own = lax.dynamic_slice_in_dim(g2, core * B, B, 0)
    grad_result = to_layers(jnp.stack([g0, g1, g2_own, g3]), section)
    return (latent_result[None], grad_result[None])


def solution(mesh):
    devices = np.asarray(mesh.devices)
    sections, parts = devices.shape
    split = Mesh(devices.reshape(sections, parts // 2, 2), ("section", "chip", "core"))
    dom = ("chip", "core")
    in_specs = (
        P(None, dom, None),
        P(None, dom, None),
        P("section", None, None),
        P("section", None, None),
        P("section", None, None),
        P("section", None),
        P(dom, None, None),
        P(dom),
        P(dom),
    )
    out_specs = (P("section", None, dom, None), P("section", None, dom, None))
    return jax.shard_map(body, mesh=split, in_specs=in_specs, out_specs=out_specs, check_vma=False)
```

time: 424 us -> 194 us (0.46)
  the two profiles are of different devices: /device:TPU:125 before, /device:TPU:104 now
where the time goes in v1:
time: 194 us; the launch traced here: 192 us
  starting transfers between devices  84.6 us (44%)
  Pallas kernels  43.5 us (22%)
  waiting for transfers between devices  34 us (18%)
  local copies, waits for them, and re-layouts  26 us (13%)
  between operations  2.13 us (1%)
  other arithmetic  2 us (1%)
    ppermute x8, starting transfers between devices, spread(): return lax.ppermute(value, ('chip', 'core'), pairs)  37.1 us
    pallas_call x1, Pallas kernels, body(): call(forward_kernel, [((4, B, H), BF16), ((PAIR, H), BF16), ((3 * PAIR, B...  33.4 us
    ppermute x9, starting transfers between devices, swap(): return lax.ppermute(value, 'core', [(0, 1), (1, 0)])  21.7 us
    unnamed x74, local copies, waits for them, and re-layouts  20.4 us
    ppermute x6, starting transfers between devices, to_layers(): lax.ppermute(piece, 'section', [(s, (s + step) % count) for s in range(co...  20.2 us
    ppermute x8, waiting for transfers between devices, spread(): return lax.ppermute(value, ('chip', 'core'), pairs)  18.9 us
    ppermute x2, waiting for transfers between devices, around(): return lax.ppermute(value, ('section', 'core'), pairs)  6.07 us
    ppermute x2, starting transfers between devices, around(): return lax.ppermute(value, ('section', 'core'), pairs)  5.59 us
  transfers between devices with their start and end apart: 25, of which 9 were waited for; matrix products, arithmetic and copies ran while one was open for 4% of the time, Pallas kernels for 3%

profile of v1, /device:TPU:104, one launch (start us, length us, event | category | flops | bytes accessed | tf_op | source)
XLA Modules:
  0.0 192.3 jit_solution(14326215786801097514)
XLA Ops:
  9.6 3.4 %collective-permute-start.9 = (bf16[1568,512]{1,0:T(8,128)(2,1)S(1)}, bf16[1568,512]{1,0:T(8,128)(2,1)}, u32[]{:S(2)}, u32[]{:S(2)}) collective-permute-start(bf16[1568,512]{1,0:T(8,128)(2,1)S(1)} %get-tuple-element.20.w_own), channel_id=1, source_target_pairs={{0,128},{1,385},{128,256},{129,1},{256,384},{257,129},{384,0},{385... | collective-permute-start | bytes 4816904 | tf_op jit(solution)/shard_map/ppermute | solution.py:277
  13.0 2.7 %collective-permute-start = (bf16[128,1792]{1,0:T(8,128)(2,1)S(1)}, bf16[128,1792]{1,0:T(8,128)(2,1)S(1)}, u32[]{:S(2)}, u32[]{:S(2)}) collective-permute-start(bf16[128,1792]{1,0:T(8,128)(2,1)S(1)} %get-tuple-element.19), channel_id=1, source_target_pairs={{0,1},{1,0},{2,3},{3,2},{4,5},{5,4},{6,7},{7,6},{8,9},{9,8},{10,11... | collective-permute-start | bytes 1376264 | tf_op jit(solution)/shard_map/ppermute | solution.py:257
  18.0 5.0 %collective-permute-start.4 = (bf16[256,512]{1,0:T(8,128)(2,1)}, bf16[256,512]{1,0:T(8,128)(2,1)S(1)}, u32[]{:S(2)}, u32[]{:S(2)}) collective-permute-start(bf16[256,512]{1,0:T(8,128)(2,1)} %get-tuple-element.37), channel_id=1, source_target_pairs={{0,8},{2,10},{4,12},{6,14},{8,16},{9,1},{10,18},{11,3},{12,20},{13... | collective-permute-start | bytes 786440 | tf_op jit(solution)/shard_map/ppermute | solution.py:268
  24.0 3.5 %collective-permute-start.1 = (bf16[256,1792]{1,0:T(8,128)(2,1)}, bf16[256,1792]{1,0:T(8,128)(2,1)}, u32[]{:S(2)}, u32[]{:S(2)}) collective-permute-start(bf16[256,1792]{1,0:T(8,128)(2,1)} %pad_maximum_fusion.own), channel_id=1, source_target_pairs={{0,2},{2,4},{3,1},{4,6},{5,3},{6,8},{7,5},{8,10},{9,7},{10,12},{11... | collective-permute-start | bytes 2752520 | tf_op jit(solution)/shard_map/ppermute | solution.py:268
  27.5 6.1 %collective-permute-done.9.w_m = bf16[1568,512]{1,0:T(8,128)(2,1)} collective-permute-done((bf16[1568,512]{1,0:T(8,128)(2,1)S(1)}, bf16[1568,512]{1,0:T(8,128)(2,1)}, u32[]{:S(2)}, u32[]{:S(2)}) %collective-permute-start.9) | collective-permute-done | bytes 1605664 | tf_op jit(solution)/shard_map/ppermute | solution.py:277
  34.8 2.2 %collective-permute-start.11 = (bf16[784,512]{1,0:T(8,128)(2,1)S(1)}, bf16[784,512]{1,0:T(8,128)(2,1)S(1)}, u32[]{:S(2)}, u32[]{:S(2)}) collective-permute-start(bf16[784,512]{1,0:T(8,128)(2,1)S(1)} %constant_dynamic-slice_fusion.6), channel_id=1, source_target_pairs={{0,128},{1,385},{128,256},{129,1},{256,384},{257,129},{384,0},{385... | collective-permute-start | bytes 2408456 | tf_op jit(solution)/shard_map/ppermute | solution.py:277
  37.0 2.8 %collective-permute-start.10 = (bf16[1568,512]{1,0:T(8,128)(2,1)}, bf16[1568,512]{1,0:T(8,128)(2,1)S(1)}, u32[]{:S(2)}, u32[]{:S(2)}) collective-permute-start(bf16[1568,512]{1,0:T(8,128)(2,1)} %collective-permute-done.9.w_m), channel_id=1, source_target_pairs={{0,1},{1,0},{2,3},{3,2},{4,5},{5,4},{6,7},{7,6},{8,9},{9,8},{10,11... | collective-permute-start | bytes 4816904 | tf_op jit(solution)/shard_map/ppermute | solution.py:257
  39.8 1.9 collective-permute-start.8
  41.8 4.2 %collective-permute-start.2 = (bf16[256,1280]{1,0:T(8,128)(2,1)S(1)}, bf16[256,1280]{1,0:T(8,128)(2,1)S(1)}, u32[]{:S(2)}, u32[]{:S(2)}) collective-permute-start(bf16[256,1280]{1,0:T(8,128)(2,1)S(1)} %fusion), channel_id=1, source_target_pairs={{0,4},{2,6},{4,8},{5,1},{6,10},{7,3},{8,12},{9,5},{10,14},{11,7},{... | collective-permute-start | bytes 1966088 | tf_op jit(solution)/shard_map/ppermute | solution.py:268
  46.0 5.8 %collective-permute-start.3 = (bf16[256,1280]{1,0:T(8,128)(2,1)S(1)}, bf16[256,1280]{1,0:T(8,128)(2,1)S(1)}, u32[]{:S(2)}, u32[]{:S(2)}) collective-permute-start(bf16[256,1280]{1,0:T(8,128)(2,1)S(1)} %fusion), channel_id=1, source_target_pairs={{0,6},{2,8},{4,10},{6,12},{7,1},{8,14},{9,3},{10,16},{11,5},{12,18... | collective-permute-start | bytes 1966088 | tf_op jit(solution)/shard_map/ppermute | solution.py:268
  53.8 2.4 %collective-permute-start.12 = (bf16[784,512]{1,0:T(8,128)(2,1)S(1)}, bf16[784,512]{1,0:T(8,128)(2,1)S(1)}, u32[]{:S(2)}, u32[]{:S(2)}) collective-permute-start(bf16[784,512]{1,0:T(8,128)(2,1)S(1)} %collective-permute-done.11.w_mh), channel_id=1, source_target_pairs={{0,1},{1,0},{2,3},{3,2},{4,5},{5,4},{6,7},{7,6},{8,9},{9,8},{10,11... | collective-permute-start | bytes 2408456 | tf_op jit(solution)/shard_map/ppermute | solution.py:257
  56.2 11.9 %collective-permute-done.2.m2 = bf16[256,1280]{1,0:T(8,128)(2,1)S(1)} collective-permute-done((bf16[256,1280]{1,0:T(8,128)(2,1)S(1)}, bf16[256,1280]{1,0:T(8,128)(2,1)S(1)}, u32[]{:S(2)}, u32[]{:S(2)}) %collective-permute-start.2) | collective-permute-done | bytes 655392 | tf_op jit(solution)/shard_map/ppermute | solution.py:268
  68.1 4.0 %collective-permute-start.6 = (bf16[256,1280]{1,0:T(8,128)(2,1)S(1)}, bf16[256,1280]{1,0:T(8,128)(2,1)S(1)}, u32[]{:S(2)}, u32[]{:S(2)}) collective-permute-start(bf16[256,1280]{1,0:T(8,128)(2,1)S(1)} %collective-permute-done.2.m2), channel_id=1, source_target_pairs={{0,1},{1,0},{2,3},{3,2},{4,5},{5,4},{6,7},{7,6},{8,9},{9,8},{10,11... | collective-permute-start | bytes 1966088 | tf_op jit(solution)/shard_map/ppermute | solution.py:257
  74.1 2.0 %collective-permute-done.7.t3 = bf16[256,1280]{1,0:T(8,128)(2,1)S(1)} collective-permute-done((bf16[256,1280]{1,0:T(8,128)(2,1)S(1)}, bf16[256,1280]{1,0:T(8,128)(2,1)S(1)}, u32[]{:S(2)}, u32[]{:S(2)}) %collective-permute-start.7) | collective-permute-done | bytes 655392 | tf_op jit(solution)/shard_map/ppermute | solution.py:257
  78.8 33.4 %forward.1 = (bf16[4,128,512]{2,1,0:T(8,128)(2,1)}, bf16[256,512]{1,0:T(8,128)(2,1)}, bf16[768,768]{1,0:T(8,128)(2,1)}, bf16[768,512]{1,0:T(8,128)(2,1)}, bf16[2...) custom-call(s32[3]{0:T(128)} %copy-done.20, ...), custom_call_target="tpu_custom_call" | custom-call | tf_op jit(solution)/shard_map/forward/pallas_call | solution.py:320
  112.2 4.2 %collective-permute-start.16 = (bf16[256,512]{1,0:T(8,128)(2,1)}, bf16[256,512]{1,0:T(8,128)(2,1)S(1)}, u32[]{:S(2)}, u32[]{:S(2)}) collective-permute-start(bf16[256,512]{1,0:T(8,128)(2,1)} %get-tuple-element.22.grad_pre), channel_id=1, source_target_pairs={{0,2},{2,4},{3,1},{4,6},{5,3},{6,8},{7,5},{8,10},{9,7},{10,12},{11... | collective-permute-start | bytes 786440 | tf_op jit(solution)/shard_map/ppermute | solution.py:268
  116.3 4.2 %collective-permute-start.17 = (bf16[256,512]{1,0:T(8,128)(2,1)}, bf16[256,512]{1,0:T(8,128)(2,1)S(1)}, u32[]{:S(2)}, u32[]{:S(2)}) collective-permute-start(bf16[256,512]{1,0:T(8,128)(2,1)} %get-tuple-element.22.grad_pre), channel_id=1, source_target_pairs={{0,4},{2,6},{4,8},{5,1},{6,10},{7,3},{8,12},{9,5},{10,14},{11,7},{... | collective-permute-start | bytes 786440 | tf_op jit(solution)/shard_map/ppermute | solution.py:268
  120.8 6.7 %collective-permute-done.17 = bf16[256,512]{1,0:T(8,128)(2,1)S(1)} collective-permute-done((bf16[256,512]{1,0:T(8,128)(2,1)}, bf16[256,512]{1,0:T(8,128)(2,1)S(1)}, u32[]{:S(2)}, u32[]{:S(2)}) %collective-permute-start.17) | collective-permute-done | bytes 262176 | tf_op jit(solution)/shard_map/ppermute | solution.py:268
  127.5 2.1 %collective-permute-start.18 = (bf16[512,512]{1,0:T(8,128)(2,1)S(1)}, bf16[512,512]{1,0:T(8,128)(2,1)S(1)}, u32[]{:S(2)}, u32[]{:S(2)}) collective-permute-start(bf16[512,512]{1,0:T(8,128)(2,1)S(1)} %constant_dynamic-update-slice_fusion.received), channel_id=1, source_target_pairs={{0,1},{1,0},{2,3},{3,2},{4,5},{5,4},{6,7},{7,6},{8,9},{9,8},{10,11... | collective-permute-start | bytes 1572872 | tf_op jit(solution)/shard_map/ppermute | solution.py:257
  131.6 2.8 %copy-done = bf16[6272,512]{1,0:T(8,128)(2,1)S(1)} copy-done((bf16[6272,512]{1,0:T(8,128)(2,1)S(1)}, bf16[6272,512]{1,0:T(8,128)(2,1)}, u32[]{:S(2)}) %copy-start) | copy-done | bytes 6422552
  137.8 4.4 %backward_a.1 = (bf16[128,512]{1,0:T(8,128)(2,1)S(1)}, bf16[256,512]{1,0:T(8,128)(2,1)S(1)}) custom-call(s32[3]{0:T(128)S(1)} %copy-done.21, bf16[256,512]{1,0:T(8,128)(2,1)S(1)} %copy-done.15, bf16[512,512]{1,0:T(8,128)(2,1)S(1)} %constant_dynamic-update-slice_fusion.received, bf16[512,512]{1,0:T(8,128)(2,1)S(1)} %collective-permute-done.18.other, ...), custom_call_target="tpu_custom_call" | custom-call | tf_op jit(solution)/shard_map/backward_a/pallas_call | solution.py:340
  142.8 4.0 %collective-permute-start.19 = (bf16[256,512]{1,0:T(8,128)(2,1)S(1)}, bf16[256,512]{1,0:T(8,128)(2,1)S(1)}, u32[]{:S(2)}, u32[]{:S(2)}) collective-permute-start(bf16[256,512]{1,0:T(8,128)(2,1)S(1)} %get-tuple-element.28.g2_own), channel_id=1, source_target_pairs={{0,2},{2,4},{3,1},{4,6},{5,3},{6,8},{7,5},{8,10},{9,7},{10,12},{11... | collective-permute-start | bytes 786440 | tf_op jit(solution)/shard_map/ppermute | solution.py:268
  146.9 6.2 %collective-permute-start.20 = (bf16[256,512]{1,0:T(8,128)(2,1)S(1)}, bf16[256,512]{1,0:T(8,128)(2,1)S(1)}, u32[]{:S(2)}, u32[]{:S(2)}) collective-permute-start(bf16[256,512]{1,0:T(8,128)(2,1)S(1)} %get-tuple-element.28.g2_own), channel_id=1, source_target_pairs={{0,4},{2,6},{4,8},{5,1},{6,10},{7,3},{8,12},{9,5},{10,14},{11,7},{... | collective-permute-start | bytes 786440 | tf_op jit(solution)/shard_map/ppermute | solution.py:268
  154.4 2.5 %collective-permute-start.13 = (bf16[1,128,512]{2,1,0:T(8,128)(2,1)S(1)}, bf16[1,128,512]{2,1,0:T(8,128)(2,1)S(1)}, u32[]{:S(2)}, u32[]{:S(2)}) collective-permute-start(bf16[1,128,512]{2,1,0:T(8,128)(2,1)S(1)} %get-tuple-element.45), channel_id=1, source_target_pairs={{0,128},{128,256},{256,384},{384,0},{1,129},{129,257},{257,385},{3... | collective-permute-start | bytes 393224 | tf_op jit(solution)/shard_map/ppermute | solution.py:287
  156.9 4.8 %collective-permute-start.14 = (bf16[1,128,512]{2,1,0:T(8,128)(2,1)S(1)}, bf16[1,128,512]{2,1,0:T(8,128)(2,1)S(1)}, u32[]{:S(2)}, u32[]{:S(2)}) collective-permute-start(bf16[1,128,512]{2,1,0:T(8,128)(2,1)S(1)} %get-tuple-element.44), channel_id=1, source_target_pairs={{0,256},{128,384},{256,0},{384,128},{1,257},{129,385},{257,1},{385... | collective-permute-start | bytes 393224 | tf_op jit(solution)/shard_map/ppermute | solution.py:287
  161.7 2.9 %collective-permute-start.15 = (bf16[1,128,512]{2,1,0:T(8,128)(2,1)S(1)}, bf16[1,128,512]{2,1,0:T(8,128)(2,1)S(1)}, u32[]{:S(2)}, u32[]{:S(2)}) collective-permute-start(bf16[1,128,512]{2,1,0:T(8,128)(2,1)S(1)} %get-tuple-element.43), channel_id=1, source_target_pairs={{0,384},{128,0},{256,128},{384,256},{1,385},{129,1},{257,129},{385... | collective-permute-start | bytes 393224 | tf_op jit(solution)/shard_map/ppermute | solution.py:287
  169.5 2.8 %copy-done.1 = bf16[6272,512]{1,0:T(8,128)(2,1)S(1)} copy-done((bf16[6272,512]{1,0:T(8,128)(2,1)S(1)}, bf16[6272,512]{1,0:T(8,128)(2,1)}, u32[]{:S(2)}) %copy-start.1) | copy-done | bytes 6422552
  172.3 5.0 %backward_b.1 = (bf16[128,512]{1,0:T(8,128)(2,1)S(1)}, bf16[128,512]{1,0:T(8,128)(2,1)S(1)}) custom-call(s32[3]{0:T(128)S(1)} %copy-done.21, bf16[256,512]{1,0:T(8,128)(2,1)S(1)} %get-tuple-element.28.g2_own, bf16[512,512]{1,0:T(8,128)(2,1)S(1)} %constant_dynamic-update-slice_fusion.2.received, bf16[512,512]{1,0:T(8,128)(2,1)S(1)} %collective-permute-done.21.other, ...), custom_call_target="tpu_custom_call" | custom-call | tf_op jit(solution)/shard_map/backward_b/pallas_call | solution.py:356
  177.5 3.0 %collective-permute-start.22 = (bf16[1,128,512]{2,1,0:T(8,128)(2,1)S(1)}, bf16[1,128,512]{2,1,0:T(8,128)(2,1)S(1)}, u32[]{:S(2)}, u32[]{:S(2)}) collective-permute-start(bf16[1,128,512]{2,1,0:T(8,128)(2,1)S(1)} %get-tuple-element.42), channel_id=1, source_target_pairs={{0,128},{128,256},{256,384},{384,0},{1,129},{129,257},{257,385},{3... | collective-permute-start | bytes 393224 | tf_op jit(solution)/shard_map/ppermute | solution.py:287
  180.5 2.5 %collective-permute-start.23 = (bf16[1,128,512]{2,1,0:T(8,128)(2,1)S(1)}, bf16[1,128,512]{2,1,0:T(8,128)(2,1)S(1)}, u32[]{:S(2)}, u32[]{:S(2)}) collective-permute-start(bf16[1,128,512]{2,1,0:T(8,128)(2,1)S(1)} %get-tuple-element.41), channel_id=1, source_target_pairs={{0,256},{128,384},{256,0},{384,128},{1,257},{129,385},{257,1},{385... | collective-permute-start | bytes 393224 | tf_op jit(solution)/shard_map/ppermute | solution.py:287
  183.0 4.5 %collective-permute-start.24 = (bf16[1,128,512]{2,1,0:T(8,128)(2,1)S(1)}, bf16[1,128,512]{2,1,0:T(8,128)(2,1)S(1)}, u32[]{:S(2)}, u32[]{:S(2)}) collective-permute-start(bf16[1,128,512]{2,1,0:T(8,128)(2,1)S(1)} %get-tuple-element.40), channel_id=1, source_target_pairs={{0,384},{128,0},{256,128},{384,256},{1,385},{129,1},{257,129},{385... | collective-permute-start | bytes 393224 | tf_op jit(solution)/shard_map/ppermute | solution.py:287
  189.2 2.3 %collective-permute-done.24 = bf16[1,128,512]{2,1,0:T(8,128)(2,1)S(1)} collective-permute-done((bf16[1,128,512]{2,1,0:T(8,128)(2,1)S(1)}, bf16[1,128,512]{2,1,0:T(8,128)(2,1)S(1)}, u32[]{:S(2)}, u32[]{:S(2)}) %collective-permute-start.24) | collective-permute-done | bytes 131104 | tf_op jit(solution)/shard_map/ppermute | solution.py:287
  (120 shorter events, 33.9 us)
Async XLA Ops:
  9.6 24.0 %collective-permute-start.9 = (bf16[1568,512]{1,0:T(8,128)(2,1)S(1)}, bf16[1568,512]{1,0:T(8,128)(2,1)}, u32[]{:S(2)}, u32[]{:S(2)}) collective-permute-start(bf16[1568,512]{1,0:T(8,128)(2,1)S(1)} %get-tuple-element.20.w_own), channel_id=1, source_target_pairs={{0,128},{1,385},{128,256},{129,1},{256,384},{257,129},{384,0},{385... | collective-permute-start | bytes 4816904 | tf_op jit(solution)/shard_map/ppermute | solution.py:277
  13.0 4.2 %collective-permute-start = (bf16[128,1792]{1,0:T(8,128)(2,1)S(1)}, bf16[128,1792]{1,0:T(8,128)(2,1)S(1)}, u32[]{:S(2)}, u32[]{:S(2)}) collective-permute-start(bf16[128,1792]{1,0:T(8,128)(2,1)S(1)} %get-tuple-element.19), channel_id=1, source_target_pairs={{0,1},{1,0},{2,3},{3,2},{4,5},{5,4},{6,7},{7,6},{8,9},{9,8},{10,11... | collective-permute-start | bytes 1376264 | tf_op jit(solution)/shard_map/ppermute | solution.py:257
  18.0 21.8 %collective-permute-start.4 = (bf16[256,512]{1,0:T(8,128)(2,1)}, bf16[256,512]{1,0:T(8,128)(2,1)S(1)}, u32[]{:S(2)}, u32[]{:S(2)}) collective-permute-start(bf16[256,512]{1,0:T(8,128)(2,1)} %get-tuple-element.37), channel_id=1, source_target_pairs={{0,8},{2,10},{4,12},{6,14},{8,16},{9,1},{10,18},{11,3},{12,20},{13... | collective-permute-start | bytes 786440 | tf_op jit(solution)/shard_map/ppermute | solution.py:268
  24.0 27.8 %collective-permute-start.1 = (bf16[256,1792]{1,0:T(8,128)(2,1)}, bf16[256,1792]{1,0:T(8,128)(2,1)}, u32[]{:S(2)}, u32[]{:S(2)}) collective-permute-start(bf16[256,1792]{1,0:T(8,128)(2,1)} %pad_maximum_fusion.own), channel_id=1, source_target_pairs={{0,2},{2,4},{3,1},{4,6},{5,3},{6,8},{7,5},{8,10},{9,7},{10,12},{11... | collective-permute-start | bytes 2752520 | tf_op jit(solution)/shard_map/ppermute | solution.py:268
  34.8 19.0 %collective-permute-start.11 = (bf16[784,512]{1,0:T(8,128)(2,1)S(1)}, bf16[784,512]{1,0:T(8,128)(2,1)S(1)}, u32[]{:S(2)}, u32[]{:S(2)}) collective-permute-start(bf16[784,512]{1,0:T(8,128)(2,1)S(1)} %constant_dynamic-slice_fusion.6), channel_id=1, source_target_pairs={{0,128},{1,385},{128,256},{129,1},{256,384},{257,129},{384,0},{385... | collective-permute-start | bytes 2408456 | tf_op jit(solution)/shard_map/ppermute | solution.py:277
  37.0 39.2 %collective-permute-start.10 = (bf16[1568,512]{1,0:T(8,128)(2,1)}, bf16[1568,512]{1,0:T(8,128)(2,1)S(1)}, u32[]{:S(2)}, u32[]{:S(2)}) collective-permute-start(bf16[1568,512]{1,0:T(8,128)(2,1)} %collective-permute-done.9.w_m), channel_id=1, source_target_pairs={{0,1},{1,0},{2,3},{3,2},{4,5},{5,4},{6,7},{7,6},{8,9},{9,8},{10,11... | collective-permute-start | bytes 4816904 | tf_op jit(solution)/shard_map/ppermute | solution.py:257
  39.8 6.2 %collective-permute-start.8 = (bf16[256,512]{1,0:T(8,128)(2,1)S(1)}, bf16[256,512]{1,0:T(8,128)(2,1)S(1)}, u32[]{:S(2)}, u32[]{:S(2)}) collective-permute-start(bf16[256,512]{1,0:T(8,128)(2,1)S(1)} %collective-permute-done.4.m4), channel_id=1, source_target_pairs={{0,1},{1,0},{2,3},{3,2},{4,5},{5,4},{6,7},{7,6},{8,9},{9,8},{10,11... | collective-permute-start | bytes 786440 | tf_op jit(solution)/shard_map/ppermute | solution.py:257
  41.8 26.4 %collective-permute-start.2 = (bf16[256,1280]{1,0:T(8,128)(2,1)S(1)}, bf16[256,1280]{1,0:T(8,128)(2,1)S(1)}, u32[]{:S(2)}, u32[]{:S(2)}) collective-permute-start(bf16[256,1280]{1,0:T(8,128)(2,1)S(1)} %fusion), channel_id=1, source_target_pairs={{0,4},{2,6},{4,8},{5,1},{6,10},{7,3},{8,12},{9,5},{10,14},{11,7},{... | collective-permute-start | bytes 1966088 | tf_op jit(solution)/shard_map/ppermute | solution.py:268
  46.0 30.2 %copy-start.35 = (bf16[256,512]{1,0:T(8,128)(2,1)}, bf16[256,512]{1,0:T(8,128)(2,1)S(1)}, u32[]{:S(2)}) copy-start(bf16[256,512]{1,0:T(8,128)(2,1)S(1)} %collective-permute-done.8.t4) | copy-start | bytes 786436
  46.0 26.2 %collective-permute-start.3 = (bf16[256,1280]{1,0:T(8,128)(2,1)S(1)}, bf16[256,1280]{1,0:T(8,128)(2,1)S(1)}, u32[]{:S(2)}, u32[]{:S(2)}) collective-permute-start(bf16[256,1280]{1,0:T(8,128)(2,1)S(1)} %fusion), channel_id=1, source_target_pairs={{0,6},{2,8},{4,10},{6,12},{7,1},{8,14},{9,3},{10,16},{11,5},{12,18... | collective-permute-start | bytes 1966088 | tf_op jit(solution)/shard_map/ppermute | solution.py:268
  51.8 24.3 %collective-permute-start.5 = (bf16[256,1792]{1,0:T(8,128)(2,1)}, bf16[256,1792]{1,0:T(8,128)(2,1)S(1)}, u32[]{:S(2)}, u32[]{:S(2)}) collective-permute-start(bf16[256,1792]{1,0:T(8,128)(2,1)} %collective-permute-done.1.m1), channel_id=1, source_target_pairs={{0,1},{1,0},{2,3},{3,2},{4,5},{5,4},{6,7},{7,6},{8,9},{9,8},{10,11... | collective-permute-start | bytes 2752520 | tf_op jit(solution)/shard_map/ppermute | solution.py:257
  53.8 22.4 %copy-start.26 = (bf16[784,512]{1,0:T(8,128)(2,1)}, bf16[784,512]{1,0:T(8,128)(2,1)S(1)}, u32[]{:S(2)}) copy-start(bf16[784,512]{1,0:T(8,128)(2,1)S(1)} %collective-permute-done.11.w_mh) | copy-start | bytes 2408452
  53.8 22.4 %collective-permute-start.12 = (bf16[784,512]{1,0:T(8,128)(2,1)S(1)}, bf16[784,512]{1,0:T(8,128)(2,1)S(1)}, u32[]{:S(2)}, u32[]{:S(2)}) collective-permute-start(bf16[784,512]{1,0:T(8,128)(2,1)S(1)} %collective-permute-done.11.w_mh), channel_id=1, source_target_pairs={{0,1},{1,0},{2,3},{3,2},{4,5},{5,4},{6,7},{7,6},{8,9},{9,8},{10,11... | collective-permute-start | bytes 2408456 | tf_op jit(solution)/shard_map/ppermute | solution.py:257
  68.1 6.0 %collective-permute-start.6 = (bf16[256,1280]{1,0:T(8,128)(2,1)S(1)}, bf16[256,1280]{1,0:T(8,128)(2,1)S(1)}, u32[]{:S(2)}, u32[]{:S(2)}) collective-permute-start(bf16[256,1280]{1,0:T(8,128)(2,1)S(1)} %collective-permute-done.2.m2), channel_id=1, source_target_pairs={{0,1},{1,0},{2,3},{3,2},{4,5},{5,4},{6,7},{7,6},{8,9},{9,8},{10,11... | collective-permute-start | bytes 1966088 | tf_op jit(solution)/shard_map/ppermute | solution.py:257
  72.2 4.0 %collective-permute-start.7 = (bf16[256,1280]{1,0:T(8,128)(2,1)S(1)}, bf16[256,1280]{1,0:T(8,128)(2,1)S(1)}, u32[]{:S(2)}, u32[]{:S(2)}) collective-permute-start(bf16[256,1280]{1,0:T(8,128)(2,1)S(1)} %collective-permute-done.3.m3), channel_id=1, source_target_pairs={{0,1},{1,0},{2,3},{3,2},{4,5},{5,4},{6,7},{7,6},{8,9},{9,8},{10,11... | collective-permute-start | bytes 1966088 | tf_op jit(solution)/shard_map/ppermute | solution.py:257
  112.1 19.5 %copy-start.2 = (bf16[768,768]{1,0:T(8,128)(2,1)S(1)}, bf16[768,768]{1,0:T(8,128)(2,1)}, u32[]{:S(2)}) copy-start(bf16[768,768]{1,0:T(8,128)(2,1)} %get-tuple-element.23.turned) | copy-start | bytes 3538948
  112.1 19.5 %copy-start.8 = (bf16[768,512]{1,0:T(8,128)(2,1)S(1)}, bf16[768,512]{1,0:T(8,128)(2,1)}, u32[]{:S(2)}) copy-start(bf16[768,512]{1,0:T(8,128)(2,1)} %get-tuple-element.24.v3) | copy-start | bytes 2359300
  112.1 19.5 %copy-start.21 = (s32[3]{0:T(128)S(1)}, s32[3]{0:T(128)}, u32[]{:S(2)}) copy-start(s32[3]{0:T(128)} %copy-done.20) | copy-start | bytes 40
  112.2 8.6 %collective-permute-start.16 = (bf16[256,512]{1,0:T(8,128)(2,1)}, bf16[256,512]{1,0:T(8,128)(2,1)S(1)}, u32[]{:S(2)}, u32[]{:S(2)}) collective-permute-start(bf16[256,512]{1,0:T(8,128)(2,1)} %get-tuple-element.22.grad_pre), channel_id=1, source_target_pairs={{0,2},{2,4},{3,1},{4,6},{5,3},{6,8},{7,5},{8,10},{9,7},{10,12},{11... | collective-permute-start | bytes 786440 | tf_op jit(solution)/shard_map/ppermute | solution.py:268
  116.3 11.2 %collective-permute-start.17 = (bf16[256,512]{1,0:T(8,128)(2,1)}, bf16[256,512]{1,0:T(8,128)(2,1)S(1)}, u32[]{:S(2)}, u32[]{:S(2)}) collective-permute-start(bf16[256,512]{1,0:T(8,128)(2,1)} %get-tuple-element.22.grad_pre), channel_id=1, source_target_pairs={{0,4},{2,6},{4,8},{5,1},{6,10},{7,3},{8,12},{9,5},{10,14},{11,7},{... | collective-permute-start | bytes 786440 | tf_op jit(solution)/shard_map/ppermute | solution.py:268
  127.5 4.1 %collective-permute-start.18 = (bf16[512,512]{1,0:T(8,128)(2,1)S(1)}, bf16[512,512]{1,0:T(8,128)(2,1)S(1)}, u32[]{:S(2)}, u32[]{:S(2)}) collective-permute-start(bf16[512,512]{1,0:T(8,128)(2,1)S(1)} %constant_dynamic-update-slice_fusion.received), channel_id=1, source_target_pairs={{0,1},{1,0},{2,3},{3,2},{4,5},{5,4},{6,7},{7,6},{8,9},{9,8},{10,11... | collective-permute-start | bytes 1572872 | tf_op jit(solution)/shard_map/ppermute | solution.py:257
  137.8 31.7 %copy-start.6 = (f32[768,512]{1,0:T(8,128)S(1)}, f32[768,512]{1,0:T(8,128)}, u32[]{:S(2)}) copy-start(f32[768,512]{1,0:T(8,128)} %get-tuple-element.32.f0) | copy-start | bytes 4718596
  137.8 31.7 %copy-start.14 = (bf16[256,512]{1,0:T(8,128)(2,1)S(1)}, bf16[256,512]{1,0:T(8,128)(2,1)}, u32[]{:S(2)}) copy-start(bf16[256,512]{1,0:T(8,128)(2,1)} %get-tuple-element.30.v0) | copy-start | bytes 786436
  142.8 22.8 %collective-permute-start.19 = (bf16[256,512]{1,0:T(8,128)(2,1)S(1)}, bf16[256,512]{1,0:T(8,128)(2,1)S(1)}, u32[]{:S(2)}, u32[]{:S(2)}) collective-permute-start(bf16[256,512]{1,0:T(8,128)(2,1)S(1)} %get-tuple-element.28.g2_own), channel_id=1, source_target_pairs={{0,2},{2,4},{3,1},{4,6},{5,3},{6,8},{7,5},{8,10},{9,7},{10,12},{11... | collective-permute-start | bytes 786440 | tf_op jit(solution)/shard_map/ppermute | solution.py:268
  146.9 18.7 %collective-permute-start.20 = (bf16[256,512]{1,0:T(8,128)(2,1)S(1)}, bf16[256,512]{1,0:T(8,128)(2,1)S(1)}, u32[]{:S(2)}, u32[]{:S(2)}) collective-permute-start(bf16[256,512]{1,0:T(8,128)(2,1)S(1)} %get-tuple-element.28.g2_own), channel_id=1, source_target_pairs={{0,4},{2,6},{4,8},{5,1},{6,10},{7,3},{8,12},{9,5},{10,14},{11,7},{... | collective-permute-start | bytes 786440 | tf_op jit(solution)/shard_map/ppermute | solution.py:268
  154.4 13.2 %collective-permute-start.13 = (bf16[1,128,512]{2,1,0:T(8,128)(2,1)S(1)}, bf16[1,128,512]{2,1,0:T(8,128)(2,1)S(1)}, u32[]{:S(2)}, u32[]{:S(2)}) collective-permute-start(bf16[1,128,512]{2,1,0:T(8,128)(2,1)S(1)} %get-tuple-element.45), channel_id=1, source_target_pairs={{0,128},{128,256},{256,384},{384,0},{1,129},{129,257},{257,385},{3... | collective-permute-start | bytes 393224 | tf_op jit(solution)/shard_map/ppermute | solution.py:287
  156.9 10.7 %collective-permute-start.14 = (bf16[1,128,512]{2,1,0:T(8,128)(2,1)S(1)}, bf16[1,128,512]{2,1,0:T(8,128)(2,1)S(1)}, u32[]{:S(2)}, u32[]{:S(2)}) collective-permute-start(bf16[1,128,512]{2,1,0:T(8,128)(2,1)S(1)} %get-tuple-element.44), channel_id=1, source_target_pairs={{0,256},{128,384},{256,0},{384,128},{1,257},{129,385},{257,1},{385... | collective-permute-start | bytes 393224 | tf_op jit(solution)/shard_map/ppermute | solution.py:287
  161.7 18.7 %collective-permute-start.15 = (bf16[1,128,512]{2,1,0:T(8,128)(2,1)S(1)}, bf16[1,128,512]{2,1,0:T(8,128)(2,1)S(1)}, u32[]{:S(2)}, u32[]{:S(2)}) collective-permute-start(bf16[1,128,512]{2,1,0:T(8,128)(2,1)S(1)} %get-tuple-element.43), channel_id=1, source_target_pairs={{0,384},{128,0},{256,128},{384,256},{1,385},{129,1},{257,129},{385... | collective-permute-start | bytes 393224 | tf_op jit(solution)/shard_map/ppermute | solution.py:287
  165.6 3.8 %collective-permute-start.21 = (bf16[512,512]{1,0:T(8,128)(2,1)S(1)}, bf16[512,512]{1,0:T(8,128)(2,1)S(1)}, u32[]{:S(2)}, u32[]{:S(2)}) collective-permute-start(bf16[512,512]{1,0:T(8,128)(2,1)S(1)} %constant_dynamic-update-slice_fusion.2.received), channel_id=1, source_target_pairs={{0,1},{1,0},{2,3},{3,2},{4,5},{5,4},{6,7},{7,6},{8,9},{9,8},{10,11... | collective-permute-start | bytes 1572872 | tf_op jit(solution)/shard_map/ppermute | solution.py:257
  177.5 10.2 %collective-permute-start.22 = (bf16[1,128,512]{2,1,0:T(8,128)(2,1)S(1)}, bf16[1,128,512]{2,1,0:T(8,128)(2,1)S(1)}, u32[]{:S(2)}, u32[]{:S(2)}) collective-permute-start(bf16[1,128,512]{2,1,0:T(8,128)(2,1)S(1)} %get-tuple-element.42), channel_id=1, source_target_pairs={{0,128},{128,256},{256,384},{384,0},{1,129},{129,257},{257,385},{3... | collective-permute-start | bytes 393224 | tf_op jit(solution)/shard_map/ppermute | solution.py:287
  180.5 8.7 %collective-permute-start.23 = (bf16[1,128,512]{2,1,0:T(8,128)(2,1)S(1)}, bf16[1,128,512]{2,1,0:T(8,128)(2,1)S(1)}, u32[]{:S(2)}, u32[]{:S(2)}) collective-permute-start(bf16[1,128,512]{2,1,0:T(8,128)(2,1)S(1)} %get-tuple-element.41), channel_id=1, source_target_pairs={{0,256},{128,384},{256,0},{384,128},{1,257},{129,385},{257,1},{385... | collective-permute-start | bytes 393224 | tf_op jit(solution)/shard_map/ppermute | solution.py:287
  183.0 8.4 %collective-permute-start.24 = (bf16[1,128,512]{2,1,0:T(8,128)(2,1)S(1)}, bf16[1,128,512]{2,1,0:T(8,128)(2,1)S(1)}, u32[]{:S(2)}, u32[]{:S(2)}) collective-permute-start(bf16[1,128,512]{2,1,0:T(8,128)(2,1)S(1)} %get-tuple-element.40), channel_id=1, source_target_pairs={{0,384},{128,0},{256,128},{384,256},{1,385},{129,1},{257,129},{385... | collective-permute-start | bytes 393224 | tf_op jit(solution)/shard_map/ppermute | solution.py:287
  (29 other events, 114.3 us)

commit v2 on v1

v2 whole, which is shorter than its diff:
```python
import functools

import jax
import jax.numpy as jnp
import numpy as np
from jax import lax
from jax.experimental import pallas as pl
from jax.experimental.pallas import tpu as pltpu
from jax.sharding import Mesh, PartitionSpec as P

EPS = 1e-05
H = 512
B = 128
PAIR = 2 * B
BAND = 3 * PAIR
REACH = 4
W_ROWS = 3 * H + 32
W_HALF = W_ROWS // 2
F32, BF16 = jnp.float32, jnp.bfloat16
VMEM = pl.BlockSpec(memory_space=pltpu.VMEM)
HBM = pl.BlockSpec(memory_space=pltpu.HBM)
FWD_MIB, BWD_MIB = 24, 12


def rows(index, size=PAIR):
    if isinstance(index, int):
        return pl.ds(index * size, size)
    return pl.ds(pl.multiple_of(index * size, size), size)


def dot(a, b):
    return jnp.dot(a, b, preferred_element_type=F32)


def dot_t(a, b):
    return lax.dot_general(a, b, (((1,), (1,)), ((), ())), preferred_element_type=F32)


def normed_rows(values):
    wide = values.astype(F32)
    centre = wide - jnp.mean(wide, axis=-1, keepdims=True)
    inv = lax.rsqrt(jnp.mean(centre * centre, axis=-1, keepdims=True) + EPS)
    return centre * inv, inv


def call(kernel, outs, specs, scratch, limit_mib, name, flops=0):
    return pl.pallas_call(
        kernel,
        out_shape=[jax.ShapeDtypeStruct(s, d) for s, d in outs],
        in_specs=specs,
        out_specs=[VMEM] * len(outs),
        scratch_shapes=scratch,
        compiler_params=pltpu.CompilerParams(vmem_limit_bytes=limit_mib << 20),
        name=name,
    )


def weights_kernel(w_a, w_b, w_c, gain, weights, half, gain_here, sems):
    copies = [pltpu.make_async_copy(gain, gain_here, sems.at[3])]
    for which, ref in enumerate((w_a, w_b, w_c)):
        copies.append(pltpu.make_async_copy(ref.at[0], weights.at[rows(which, H)], sems.at[which]))
    for copy in copies:
        copy.start()
    copies[0].wait()
    rest = jnp.broadcast_to(gain_here[0:1, :], (16, H))
    high = rest.astype(BF16).astype(F32)
    rest = rest - high
    mid = rest.astype(BF16).astype(F32)
    low = rest - mid
    row = lax.broadcasted_iota(jnp.int32, (16, H), 0)
    terms = jnp.where(row == 0, high, jnp.where(row == 1, mid, jnp.where(row == 2, low, 0.0)))
    weights[3 * H : 3 * H + 16, :] = terms.astype(BF16)
    weights[3 * H + 16 : 3 * H + 32, :] = jnp.zeros((16, H), BF16)
    for copy in copies[1:]:
        copy.wait()
    core = lax.axis_index("core")
    half[...] = weights[pl.ds(pl.multiple_of(core * W_HALF, 16), W_HALF), :]


def prepare_kernel(source, live, latent, cotangent, tiles, own, value, slope, tile, index, count, sems):
    sample = lax.axis_index("section")
    copies = [
        pltpu.make_async_copy(tiles, tile, sems.at[0]),
        pltpu.make_async_copy(source, index, sems.at[1]),
        pltpu.make_async_copy(live, count, sems.at[2]),
        pltpu.make_async_copy(latent.at[sample], value, sems.at[3]),
        pltpu.make_async_copy(cotangent.at[sample], slope, sems.at[4]),
    ]
    for copy in copies:
        copy.start()
    for copy in copies[:3]:
        copy.wait()
    slots = tile.shape[0]
    base = 2 * (lax.axis_index("chip") - 1)
    for column in range(6):
        total = jnp.zeros((B, B), F32)
        for slot in range(slots):
            hit = (index[slot] - base == column) & (slot < count[0])
            total = total + jnp.where(hit, tile[slot].astype(F32), 0.0)
        own[:, H + column * B : H + (column + 1) * B] = total.astype(BF16)
    for copy in copies[3:]:
        copy.wait()
    own[:, 0:H] = value[...]
    own[:, H + BAND :] = slope[...]


def pack_kernel(own, partner, pair, near, value):
    core = lax.axis_index("core")
    for ref, held in ((own, core), (partner, 1 - core)):
        pair[rows(held, B), :] = ref[...]
        near[rows(held, B), :] = ref[:, 0 : H + BAND]
        value[rows(held, B), :] = ref[:, 0:H]


def layer_gain(weights, layer):
    terms = weights[layer * W_ROWS + 3 * H : layer * W_ROWS + 3 * H + 16, :].astype(F32)
    return jnp.sum(terms, axis=0, keepdims=True)


def weight(weights, layer, which):
    start = layer * W_ROWS + which * H
    return weights[start : start + H, :]


def forward_kernel(
    own, m1, m2, m3, m4, t1, t2, t3, t4, w_own, w_m, w_t, w_mh, w_th,
    latents, grad_pre, turned, v3_out, v2_out, v1_out, f2_out, f1_out, f0_out, weights, w_low,
    v_a, v_b, band, unit, source,
):
    section, core = lax.axis_index("section"), lax.axis_index("core")
    weights[pl.ds(pl.multiple_of(section * W_ROWS, 16), W_ROWS), :] = w_own[...]
    before, after = (section + 3) % 4, (section + 1) % 4
    mine = jnp.where(core == 0, before, after)
    theirs = jnp.where(core == 0, after, before)
    far = (section + 2) % 4
    weights[pl.ds(pl.multiple_of(mine * W_ROWS, 16), W_ROWS), :] = w_m[...]
    weights[pl.ds(pl.multiple_of(theirs * W_ROWS, 16), W_ROWS), :] = w_t[...]
    weights[pl.ds(pl.multiple_of(far * W_ROWS + core * W_HALF, 16), W_HALF), :] = w_mh[...]
    weights[pl.ds(pl.multiple_of(far * W_ROWS + (1 - core) * W_HALF, 16), W_HALF), :] = w_th[...]

    v_a[rows(REACH), :] = own[:, 0:H]
    band[rows(REACH - 1), :] = own[:, H : H + BAND]
    for step, (m, t) in enumerate(((m1, t1), (m2, t2), (m3, t3), (m4, t4)), start=1):
        at_m = REACH - step + 2 * step * core
        at_t = 2 * REACH - at_m
        v_a[rows(at_m), :] = m[:, 0:H]
        v_a[rows(at_t), :] = t[:, 0:H]
        if step < REACH:
            band[rows(at_m - 1), :] = m[:, H : H + BAND]
            band[rows(at_t - 1), :] = t[:, H : H + BAND]

    w_low[...] = weights[0 : 2 * W_ROWS, :]
    now, later = v_a, v_b
    for layer in range(4):
        low, high = layer, 2 * REACH - layer
        gain = layer_gain(weights, layer)

        def project(j):
            value, _ = normed_rows(now[rows(j), :])
            held = (value * gain).astype(BF16)
            unit[rows(j), :] = held
            source[rows(j), :] = dot(held, weight(weights, layer, 0)).astype(BF16)

        def update(j):
            pre = dot(band[rows(j - 1), :], source[(j - 1) * PAIR : (j - 1) * PAIR + BAND, :])
            pre = pre + dot(unit[rows(j), :], weight(weights, layer, 1))
            sigma = 0.5 + 0.5 * jnp.tanh(0.5 * pre)
            act = (pre * sigma).astype(BF16)
            value = now[rows(j), :].astype(F32) + dot(act, weight(weights, layer, 2))
            later[rows(j), :] = value.astype(BF16)
            reach = (1, 2, 1, 0)[layer]
            if abs(j - REACH) <= reach:
                factor = sigma * (1.0 + pre * (1.0 - sigma))
                if layer == 3:
                    incoming = dot_t(own[:, H + BAND :], weight(weights, 3, 2))
                    grad_pre[...] = (incoming * factor).astype(BF16)
                else:
                    out = (f0_out, f1_out, f2_out)[layer]
                    out[rows(j - REACH + reach), :] = factor.astype(BF16)

        for j in range(low, low + 3):
            project(j)
        for j in range(low + 1, high):
            update(j)
            if j + 2 <= high:
                project(j + 2)
        latents[layer] = later[pl.ds(pl.multiple_of(REACH * PAIR + core * B, B), B), :]
        if layer == 0:
            v1_out[...] = later[3 * PAIR : 6 * PAIR, :]
        if layer == 1:
            v2_out[...] = later[4 * PAIR : 5 * PAIR, :]
        if layer == 2:
            v3_out[...] = later[3 * PAIR : 6 * PAIR, :]
        now, later = later, now

    for j in range(3, 6):
        for i in range(j - 1, j + 2):
            column = (j - i + 1) * PAIR
            piece = band[(i - 1) * PAIR : i * PAIR, column : column + PAIR]
            turned[(j - 3) * PAIR : (j - 2) * PAIR, (i - j + 1) * PAIR : (i - j + 2) * PAIR] = (
                piece.astype(F32).T.astype(BF16)
            )


def grad_pair(gradient, grad_pre, window, turned, values, weights, layer):
    back = dot(turned, window).astype(BF16)
    grad_unit = dot_t(grad_pre, weight(weights, layer, 1))
    grad_unit = grad_unit + dot_t(back, weight(weights, layer, 0))
    normed, inv = normed_rows(values)
    e = grad_unit * layer_gain(weights, layer)
    grad_in = inv * (
        e
        - jnp.mean(e, axis=-1, keepdims=True)
        - normed * jnp.mean(e * normed, axis=-1, keepdims=True)
    )
    return (gradient.astype(F32) + grad_in).astype(BF16)


def place(target, own, sides, core):
    middle = len(sides)
    target[rows(middle), :] = own[...]
    for step, (mine, theirs) in enumerate(sides, start=1):
        at_m = middle - step + 2 * step * core
        target[rows(at_m), :] = mine[...]
        target[rows(2 * middle - at_m), :] = theirs[...]


def backward_a_kernel(
    grad_pre, r1, r2, o1, o2, own, m1, t1, turned, v3, v2, f2, weights,
    g3_out, g2_out, held, cot, g3, gp2,
):
    core = lax.axis_index("core")
    place(held, grad_pre, ((r1, o1), (r2, o2)), core)
    cot[rows(1), :] = own[:, H + BAND :]
    cot[rows(2 * core), :] = m1[:, H + BAND :]
    cot[rows(2 - 2 * core), :] = t1[:, H + BAND :]
    for j in range(3):
        g3[rows(j), :] = grad_pair(
            cot[rows(j), :], held[rows(j + 1), :], held[j * PAIR : j * PAIR + BAND, :],
            turned[rows(j), :], v3[rows(j), :], weights, 3,
        )
        gp2[rows(j), :] = (dot_t(g3[rows(j), :], weight(weights, 2, 2)) * f2[rows(j), :]).astype(BF16)
    g3_out[...] = g3[pl.ds(pl.multiple_of(PAIR + core * B, B), B), :]
    g2_out[...] = grad_pair(
        g3[rows(1), :], gp2[rows(1), :], gp2[...], turned[rows(1), :], v2[...], weights, 2
    )


def backward_b_kernel(
    g2_own, r1, r2, o1, o2, g3_mine, turned, v1, own, f1, f0, weights,
    grads, g2, gp1, g1, gp0,
):
    core = lax.axis_index("core")
    place(g2, g2_own, ((r1, o1), (r2, o2)), core)
    for j in range(5):
        gp1[rows(j), :] = (dot_t(g2[rows(j), :], weight(weights, 1, 2)) * f1[rows(j), :]).astype(BF16)
    for j in range(3):
        g1[rows(j), :] = grad_pair(
            g2[rows(j + 1), :], gp1[rows(j + 1), :], gp1[j * PAIR : j * PAIR + BAND, :],
            turned[rows(j), :], v1[rows(j), :], weights, 1,
        )
        gp0[rows(j), :] = (dot_t(g1[rows(j), :], weight(weights, 0, 2)) * f0[rows(j), :]).astype(BF16)
    mine = pl.ds(pl.multiple_of(PAIR + core * B, B), B)
    grads[3] = g3_mine[...]
    grads[2] = g2_own[rows(core, B), :]
    grads[1] = g1[mine, :]
    g0 = grad_pair(g1[rows(1), :], gp0[rows(1), :], gp0[...], turned[rows(1), :], own[:, 0:H], weights, 0)
    g1[rows(1), :] = g0
    grads[0] = g1[mine, :]


def swap(value):
    return lax.ppermute(value, "core", [(0, 1), (1, 0)])


def spread(value, steps):
    chips = lax.axis_size("chip")
    pairs = []
    for c in range(chips):
        if c + steps < chips:
            pairs.append((2 * c, 2 * (c + steps)))
        if c - steps >= 0:
            pairs.append((2 * c + 1, 2 * (c - steps) + 1))
    return lax.ppermute(value, ("chip", "core"), pairs)


def around(value):
    count = lax.axis_size("section")
    pairs = []
    for s in range(count):
        pairs.append((2 * s, 2 * ((s + 1) % count)))
        pairs.append((2 * s + 1, 2 * ((s - 1) % count) + 1))
    return lax.ppermute(value, ("section", "core"), pairs)


def opposite(value):
    count = lax.axis_size("section")
    return lax.ppermute(value, "section", [(s, (s + count // 2) % count) for s in range(count)])


def to_layers(stacked, section):
    count = stacked.shape[0]
    out = jnp.zeros_like(stacked)
    keep = lax.dynamic_index_in_dim(stacked, section, 0, keepdims=True)
    out = lax.dynamic_update_slice_in_dim(out, keep, section, 0)
    for step in range(1, count):
        piece = lax.dynamic_index_in_dim(stacked, (section + step) % count, 0, keepdims=True)
        got = lax.ppermute(piece, "section", [(s, (s + step) % count) for s in range(count)])
        out = lax.dynamic_update_slice_in_dim(out, got, (section - step) % count, 0)
    return out


def body(latent, cotangent, w_a, w_b, w_c, gain, tiles, pair_source, live_pairs):
    section = lax.axis_index("section")
    wide = H + BAND

    w_own, w_half = call(
        weights_kernel,
        [((W_ROWS, H), BF16), ((W_HALF, H), BF16)],
        [HBM] * 4,
        [pltpu.VMEM((1, H), F32), pltpu.SemaphoreType.DMA((4,))],
        4,
        "weights",
    )(w_a, w_b, w_c, gain)
    w_m, w_mh = around(w_own), opposite(w_half)
    (own,) = call(
        prepare_kernel,
        [((B, wide + H), BF16)],
        [HBM] * 5,
        [
            pltpu.VMEM((B, H), BF16), pltpu.VMEM((B, H), BF16), pltpu.VMEM(tiles.shape, BF16),
            pltpu.SMEM(pair_source.shape, jnp.int32), pltpu.SMEM(live_pairs.shape, jnp.int32),
            pltpu.SemaphoreType.DMA((5,)),
        ],
        4,
        "prepare",
    )(pair_source, live_pairs, latent, cotangent, tiles)
    pair, near, value = call(
        pack_kernel,
        [((PAIR, wide + H), BF16), ((PAIR, wide), BF16), ((PAIR, H), BF16)],
        [VMEM] * 2,
        [],
        4,
        "pack",
    )(own, swap(own))
    m1, m2, m3, m4 = spread(pair, 1), spread(near, 2), spread(near, 3), spread(value, 4)
    w_m, m1, m2, m3, m4 = lax.optimization_barrier((w_m, m1, m2, m3, m4))
    w_t, w_th = swap(w_m), swap(w_mh)
    t1, t2, t3, t4 = swap(m1), swap(m2), swap(m3), swap(m4)

    span = 2 * REACH + 1
    latents, grad_pre, turned, v3, v2, v1, f2, f1, f0, weights, w_low = call(
        forward_kernel,
        [
            ((4, B, H), BF16), ((PAIR, H), BF16), ((3 * PAIR, BAND), BF16),
            ((3 * PAIR, H), BF16), ((PAIR, H), BF16), ((3 * PAIR, H), BF16),
            ((3 * PAIR, H), BF16), ((5 * PAIR, H), BF16), ((3 * PAIR, H), BF16),
            ((4 * W_ROWS, H), BF16), ((2 * W_ROWS, H), BF16),
        ],
        [VMEM] * 14,
        [
            pltpu.VMEM((span * PAIR, H), BF16), pltpu.VMEM((span * PAIR, H), BF16),
            pltpu.VMEM(((span - 2) * PAIR, BAND), BF16),
            pltpu.VMEM((span * PAIR, H), BF16), pltpu.VMEM((span * PAIR, H), BF16),
        ],
        FWD_MIB,
        "forward",
    )(pair, m1, m2, m3, m4, t1, t2, t3, t4, w_own, w_m, w_t, w_mh, w_th)

    r1, r2 = spread(grad_pre, 1), spread(grad_pre, 2)
    g3, g2 = call(
        backward_a_kernel,
        [((B, H), BF16), ((PAIR, H), BF16)],
        [VMEM] * 13,
        [
            pltpu.VMEM((5 * PAIR, H), BF16), pltpu.VMEM((3 * PAIR, H), BF16),
            pltpu.VMEM((3 * PAIR, H), BF16), pltpu.VMEM((3 * PAIR, H), BF16),
        ],
        BWD_MIB,
        "backward_a",
    )(grad_pre, r1, r2, swap(r1), swap(r2), pair, m1, t1, turned, v3, v2, f2, weights)

    latent_result = to_layers(latents, section)

    r1, r2 = spread(g2, 1), spread(g2, 2)
    (grads,) = call(
        backward_b_kernel,
        [((4, B, H), BF16)],
        [VMEM] * 12,
        [
            pltpu.VMEM((5 * PAIR, H), BF16), pltpu.VMEM((5 * PAIR, H), BF16),
            pltpu.VMEM((3 * PAIR, H), BF16), pltpu.VMEM((3 * PAIR, H), BF16),
        ],
        BWD_MIB,
        "backward_b",
    )(g2, r1, r2, swap(r1), swap(r2), g3, turned, v1, pair, f1, f0, w_low)

    grad_result = to_layers(grads, section)
    return (latent_result[None], grad_result[None])


def solution(mesh):
    devices = np.asarray(mesh.devices)
    sections, parts = devices.shape
    split = Mesh(devices.reshape(sections, parts // 2, 2), ("section", "chip", "core"))
    dom = ("chip", "core")
    in_specs = (
        P(None, dom, None),
        P(None, dom, None),
        P("section", None, None),
        P("section", None, None),
        P("section", None, None),
        P("section", None),
        P(dom, None, None),
        P(dom),
        P(dom),
    )
    out_specs = (P("section", None, dom, None), P("section", None, dom, None))
    return jax.shard_map(body, mesh=split, in_specs=in_specs, out_specs=out_specs, check_vma=False)
```

time: 194 us -> 180 us (0.928)
  starting transfers between devices: 84.6 us -> 110 us
  Pallas kernels: 43.5 us -> 26.5 us
  local copies, waits for them, and re-layouts: 26 us -> 12.2 us
  waiting for transfers between devices: 34 us -> 27.5 us
  other arithmetic: 2 us -> 0 us
    pallas_call x1, Pallas kernels: 33.4 us -> 15.3 us  [body(): call(forward_kernel, [((4, B, H), BF16), ((PAIR, H), BF16), ((3 * PAIR, B...]
    ppermute x9 -> x11, starting transfers between devices: 21.7 us -> 37.4 us  [swap(): return lax.ppermute(value, 'core', [(0, 1), (1, 0)])]
    unnamed x74 -> x34, local copies, waits for them, and re-layouts: 20.4 us -> 8.32 us
    ppermute x8, starting transfers between devices: 37.1 us -> 45 us  [spread(): return lax.ppermute(value, ('chip', 'core'), pairs)]
    ppermute x2 -> x1, waiting for transfers between devices: 6.07 us -> 0.01 us  [around(): return lax.ppermute(value, ('section', 'core'), pairs)]
    ppermute x0 -> x1, starting transfers between devices: none -> 4.08 us  [opposite(): lax.ppermute(value, 'section', [(s, (s + count // 2) % count) for s in ra...]
    ppermute x2 -> x1, starting transfers between devices: 5.59 us -> 3.53 us  [around(): return lax.ppermute(value, ('section', 'core'), pairs)]
    ppermute x9 -> x11, waiting for transfers between devices: 5.25 us -> 3.9 us  [swap(): return lax.ppermute(value, 'core', [(0, 1), (1, 0)])]
  transfers between devices with their start and end apart: 25 -> 27, of which waited for: 9 -> 11; matrix products, arithmetic and copies ran while one was open for 4% -> 2% of each run, Pallas kernels for 3% -> 4%
where the time goes in v2:
time: 180 us; the launch traced here: 178 us
  starting transfers between devices  110 us (61%)
  waiting for transfers between devices  27.5 us (15%)
  Pallas kernels  26.5 us (15%)
  local copies, waits for them, and re-layouts  12.2 us (7%)
  between operations  1.92 us (1%)
    ppermute x8, starting transfers between devices, spread(): return lax.ppermute(value, ('chip', 'core'), pairs)  45 us
    ppermute x11, starting transfers between devices, swap(): return lax.ppermute(value, 'core', [(0, 1), (1, 0)])  37.4 us
    ppermute x6, starting transfers between devices, to_layers(): lax.ppermute(piece, 'section', [(s, (s + step) % count) for s in range(co...  20.4 us
    ppermute x8, waiting for transfers between devices, spread(): return lax.ppermute(value, ('chip', 'core'), pairs)  18.4 us
    pallas_call x1, Pallas kernels, body(): call(forward_kernel, [((4, B, H), BF16), ((PAIR, H), BF16), ((3 * PAIR, B...  15.3 us
    unnamed x34, local copies, waits for them, and re-layouts  8.32 us
    pallas_call x1, Pallas kernels, body(): call(backward_b_kernel, [((4, B, H), BF16)], [VMEM] * 12, [pltpu.VMEM((5...  5.59 us
    ppermute x6, waiting for transfers between devices, to_layers(): lax.ppermute(piece, 'section', [(s, (s + step) % count) for s in range(co...  4.54 us
  transfers between devices with their start and end apart: 27, of which 11 were waited for; matrix products, arithmetic and copies ran while one was open for 2% of the time, Pallas kernels for 4%

profile of v2, /device:TPU:104, one launch (start us, length us, event | category | flops | bytes accessed | tf_op | source)
XLA Modules:
  0.0 178.4 jit_solution(10330895919268310016)
XLA Ops:
  4.7 3.5 %collective-permute-start.1 = (bf16[1568,512]{1,0:T(8,128)(2,1)S(1)}, bf16[1568,512]{1,0:T(8,128)(2,1)S(1)}, u32[]{:S(2)}, u32[]{:S(2)}) collective-permute-start(bf16[1568,512]{1,0:T(8,128)(2,1)S(1)} %get-tuple-element.26.w_own), channel_id=1, source_target_pairs={{0,128},{1,385},{128,256},{129,1},{256,384},{257,129},{384,0},{385... | collective-permute-start | bytes 4816904 | tf_op jit(solution)/shard_map/ppermute | solution.py:293
  10.5 2.7 %collective-permute-start = (bf16[128,1792]{1,0:T(8,128)(2,1)S(1)}, bf16[128,1792]{1,0:T(8,128)(2,1)S(1)}, u32[]{:S(2)}, u32[]{:S(2)}) collective-permute-start(bf16[128,1792]{1,0:T(8,128)(2,1)S(1)} %prepare.1.own), channel_id=1, source_target_pairs={{0,1},{1,0},{2,3},{3,2},{4,5},{5,4},{6,7},{7,6},{8,9},{9,8},{10,11... | collective-permute-start | bytes 1376264 | tf_op jit(solution)/shard_map/ppermute | solution.py:273
  14.7 3.5 %collective-permute-start.2 = (bf16[256,1792]{1,0:T(8,128)(2,1)S(1)}, bf16[256,1792]{1,0:T(8,128)(2,1)S(1)}, u32[]{:S(2)}, u32[]{:S(2)}) collective-permute-start(bf16[256,1792]{1,0:T(8,128)(2,1)S(1)} %get-tuple-element.25.own), channel_id=1, source_target_pairs={{0,2},{2,4},{3,1},{4,6},{5,3},{6,8},{7,5},{8,10},{9,7},{10,12},{11... | collective-permute-start | bytes 2752520 | tf_op jit(solution)/shard_map/ppermute | solution.py:284
  18.2 5.4 %collective-permute-start.3 = (bf16[256,1280]{1,0:T(8,128)(2,1)S(1)}, bf16[256,1280]{1,0:T(8,128)(2,1)S(1)}, u32[]{:S(2)}, u32[]{:S(2)}) collective-permute-start(bf16[256,1280]{1,0:T(8,128)(2,1)S(1)} %get-tuple-element.27), channel_id=1, source_target_pairs={{0,4},{2,6},{4,8},{5,1},{6,10},{7,3},{8,12},{9,5},{10,14},{11,7},{... | collective-permute-start | bytes 1966088 | tf_op jit(solution)/shard_map/ppermute | solution.py:284
  23.7 4.3 %collective-permute-start.4 = (bf16[256,1280]{1,0:T(8,128)(2,1)S(1)}, bf16[256,1280]{1,0:T(8,128)(2,1)S(1)}, u32[]{:S(2)}, u32[]{:S(2)}) collective-permute-start(bf16[256,1280]{1,0:T(8,128)(2,1)S(1)} %get-tuple-element.27), channel_id=1, source_target_pairs={{0,6},{2,8},{4,10},{6,12},{7,1},{8,14},{9,3},{10,16},{11,5},{12,18... | collective-permute-start | bytes 1966088 | tf_op jit(solution)/shard_map/ppermute | solution.py:284
  28.0 3.8 %collective-permute-start.5 = (bf16[256,512]{1,0:T(8,128)(2,1)S(1)}, bf16[256,512]{1,0:T(8,128)(2,1)S(1)}, u32[]{:S(2)}, u32[]{:S(2)}) collective-permute-start(bf16[256,512]{1,0:T(8,128)(2,1)S(1)} %get-tuple-element.28), channel_id=1, source_target_pairs={{0,8},{2,10},{4,12},{6,14},{8,16},{9,1},{10,18},{11,3},{12,20},{13... | collective-permute-start | bytes 786440 | tf_op jit(solution)/shard_map/ppermute | solution.py:284
  31.8 11.2 %collective-permute-done.5.m4 = bf16[256,512]{1,0:T(8,128)(2,1)S(1)} collective-permute-done((bf16[256,512]{1,0:T(8,128)(2,1)S(1)}, bf16[256,512]{1,0:T(8,128)(2,1)S(1)}, u32[]{:S(2)}, u32[]{:S(2)}) %collective-permute-start.5) | collective-permute-done | bytes 262176 | tf_op jit(solution)/shard_map/ppermute | solution.py:284
  43.0 4.1 %collective-permute-start.11 = (bf16[784,512]{1,0:T(8,128)(2,1)S(1)}, bf16[784,512]{1,0:T(8,128)(2,1)S(1)}, u32[]{:S(2)}, u32[]{:S(2)}) collective-permute-start(bf16[784,512]{1,0:T(8,128)(2,1)S(1)} %get-tuple-element.34), channel_id=1, source_target_pairs={{0,256},{128,384},{256,0},{384,128},{1,257},{129,385},{257,1},{385... | collective-permute-start | bytes 2408456 | tf_op jit(solution)/shard_map/ppermute | solution.py:298
  47.1 2.5 %collective-permute-done.3.m2 = bf16[256,1280]{1,0:T(8,128)(2,1)S(1)} collective-permute-done((bf16[256,1280]{1,0:T(8,128)(2,1)S(1)}, bf16[256,1280]{1,0:T(8,128)(2,1)S(1)}, u32[]{:S(2)}, u32[]{:S(2)}) %collective-permute-start.3) | collective-permute-done | bytes 655392 | tf_op jit(solution)/shard_map/ppermute | solution.py:284
  51.2 8.9 %collective-permute-start.10 = (bf16[1568,512]{1,0:T(8,128)(2,1)S(1)}, bf16[1568,512]{1,0:T(8,128)(2,1)S(1)}, u32[]{:S(2)}, u32[]{:S(2)}) collective-permute-start(bf16[1568,512]{1,0:T(8,128)(2,1)S(1)} %collective-permute-done.1.w_m), channel_id=1, source_target_pairs={{0,1},{1,0},{2,3},{3,2},{4,5},{5,4},{6,7},{7,6},{8,9},{9,8},{10,11... | collective-permute-start | bytes 4816904 | tf_op jit(solution)/shard_map/ppermute | solution.py:273
  60.8 8.1 %collective-permute-start.12 = (bf16[784,512]{1,0:T(8,128)(2,1)S(1)}, bf16[784,512]{1,0:T(8,128)(2,1)S(1)}, u32[]{:S(2)}, u32[]{:S(2)}) collective-permute-start(bf16[784,512]{1,0:T(8,128)(2,1)S(1)} %collective-permute-done.11.w_mh), channel_id=1, source_target_pairs={{0,1},{1,0},{2,3},{3,2},{4,5},{5,4},{6,7},{7,6},{8,9},{9,8},{10,11... | collective-permute-start | bytes 2408456 | tf_op jit(solution)/shard_map/ppermute | solution.py:273
  68.9 1.9 %collective-permute-start.6 = (bf16[256,1792]{1,0:T(8,128)(2,1)S(1)}, bf16[256,1792]{1,0:T(8,128)(2,1)S(1)}, u32[]{:S(2)}, u32[]{:S(2)}) collective-permute-start(bf16[256,1792]{1,0:T(8,128)(2,1)S(1)} %collective-permute-done.2.m1), channel_id=1, source_target_pairs={{0,1},{1,0},{2,3},{3,2},{4,5},{5,4},{6,7},{7,6},{8,9},{9,8},{10,11... | collective-permute-start | bytes 2752520 | tf_op jit(solution)/shard_map/ppermute | solution.py:273
  70.8 2.4 %collective-permute-start.7 = (bf16[256,1280]{1,0:T(8,128)(2,1)S(1)}, bf16[256,1280]{1,0:T(8,128)(2,1)S(1)}, u32[]{:S(2)}, u32[]{:S(2)}) collective-permute-start(bf16[256,1280]{1,0:T(8,128)(2,1)S(1)} %collective-permute-done.3.m2), channel_id=1, source_target_pairs={{0,1},{1,0},{2,3},{3,2},{4,5},{5,4},{6,7},{7,6},{8,9},{9,8},{10,11... | collective-permute-start | bytes 1966088 | tf_op jit(solution)/shard_map/ppermute | solution.py:273
  73.2 1.9 %collective-permute-start.8 = (bf16[256,1280]{1,0:T(8,128)(2,1)S(1)}, bf16[256,1280]{1,0:T(8,128)(2,1)S(1)}, u32[]{:S(2)}, u32[]{:S(2)}) collective-permute-start(bf16[256,1280]{1,0:T(8,128)(2,1)S(1)} %collective-permute-done.4.m3), channel_id=1, source_target_pairs={{0,1},{1,0},{2,3},{3,2},{4,5},{5,4},{6,7},{7,6},{8,9},{9,8},{10,11... | collective-permute-start | bytes 1966088 | tf_op jit(solution)/shard_map/ppermute | solution.py:273
  75.2 2.6 %collective-permute-start.9 = (bf16[256,512]{1,0:T(8,128)(2,1)S(1)}, bf16[256,512]{1,0:T(8,128)(2,1)S(1)}, u32[]{:S(2)}, u32[]{:S(2)}) collective-permute-start(bf16[256,512]{1,0:T(8,128)(2,1)S(1)} %collective-permute-done.5.m4), channel_id=1, source_target_pairs={{0,1},{1,0},{2,3},{3,2},{4,5},{5,4},{6,7},{7,6},{8,9},{9,8},{10,11... | collective-permute-start | bytes 786440 | tf_op jit(solution)/shard_map/ppermute | solution.py:273
  78.8 15.3 %forward.1 = (bf16[4,128,512]{2,1,0:T(8,128)(2,1)S(1)}, bf16[256,512]{1,0:T(8,128)(2,1)S(1)}, bf16[768,768]{1,0:T(8,128)(2,1)S(1)}, bf16[768,512]{1,0:T(8,128)(2...) custom-call(bf16[256,1792]{1,0:T(8,128)(2,1)S(1)} %get-tuple-element, ...), custom_call_target="tpu_custom_call" | custom-call | tf_op jit(solution)/shard_map/forward/pallas_call | solution.py:352
  94.1 5.4 %collective-permute-start.16 = (bf16[256,512]{1,0:T(8,128)(2,1)S(1)}, bf16[256,512]{1,0:T(8,128)(2,1)S(1)}, u32[]{:S(2)}, u32[]{:S(2)}) collective-permute-start(bf16[256,512]{1,0:T(8,128)(2,1)S(1)} %get-tuple-element.36.grad_pre), channel_id=1, source_target_pairs={{0,2},{2,4},{3,1},{4,6},{5,3},{6,8},{7,5},{8,10},{9,7},{10,12},{11... | collective-permute-start | bytes 786440 | tf_op jit(solution)/shard_map/ppermute | solution.py:284
  99.5 11.1 %collective-permute-start.17 = (bf16[256,512]{1,0:T(8,128)(2,1)S(1)}, bf16[256,512]{1,0:T(8,128)(2,1)S(1)}, u32[]{:S(2)}, u32[]{:S(2)}) collective-permute-start(bf16[256,512]{1,0:T(8,128)(2,1)S(1)} %get-tuple-element.36.grad_pre), channel_id=1, source_target_pairs={{0,4},{2,6},{4,8},{5,1},{6,10},{7,3},{8,12},{9,5},{10,14},{11,7},{... | collective-permute-start | bytes 786440 | tf_op jit(solution)/shard_map/ppermute | solution.py:284
  112.5 3.1 %collective-permute-done.17.r2 = bf16[256,512]{1,0:T(8,128)(2,1)S(1)} collective-permute-done((bf16[256,512]{1,0:T(8,128)(2,1)S(1)}, bf16[256,512]{1,0:T(8,128)(2,1)S(1)}, u32[]{:S(2)}, u32[]{:S(2)}) %collective-permute-start.17) | collective-permute-done | bytes 262176 | tf_op jit(solution)/shard_map/ppermute | solution.py:284
  115.6 2.5 %collective-permute-start.19 = (bf16[256,512]{1,0:T(8,128)(2,1)S(1)}, bf16[256,512]{1,0:T(8,128)(2,1)S(1)}, u32[]{:S(2)}, u32[]{:S(2)}) collective-permute-start(bf16[256,512]{1,0:T(8,128)(2,1)S(1)} %collective-permute-done.17.r2), channel_id=1, source_target_pairs={{0,1},{1,0},{2,3},{3,2},{4,5},{5,4},{6,7},{7,6},{8,9},{9,8},{10,11... | collective-permute-start | bytes 786440 | tf_op jit(solution)/shard_map/ppermute | solution.py:273
  119.3 4.4 %backward_a.1 = (bf16[128,512]{1,0:T(8,128)(2,1)S(1)}, bf16[256,512]{1,0:T(8,128)(2,1)}) custom-call(bf16[256,512]{1,0:T(8,128)(2,1)S(1)} %get-tuple-element.36.grad_pre, bf16[256,512]{1,0:T(8,128)(2,1)S(1)} %collective-permute-done.16.r1, bf16[256,512]{1,0:T(8,128)(2,1)S(1)} %collective-permute-done.17.r2, bf16[256,512]{1,0:T(8,128)(2,1)S(1)} %collective-permute-done.18.o1, ...), custom_call_target="tpu_custom_call" | custom-call | tf_op jit(solution)/shard_map/backward_a/pallas_call | solution.py:371
  123.7 4.3 %collective-permute-start.20 = (bf16[256,512]{1,0:T(8,128)(2,1)}, bf16[256,512]{1,0:T(8,128)(2,1)}, u32[]{:S(2)}, u32[]{:S(2)}) collective-permute-start(bf16[256,512]{1,0:T(8,128)(2,1)} %get-tuple-element.42.g2_own), channel_id=1, source_target_pairs={{0,2},{2,4},{3,1},{4,6},{5,3},{6,8},{7,5},{8,10},{9,7},{10,12},{11... | collective-permute-start | bytes 786440 | tf_op jit(solution)/shard_map/ppermute | solution.py:284
  128.1 7.1 %collective-permute-start.21 = (bf16[256,512]{1,0:T(8,128)(2,1)}, bf16[256,512]{1,0:T(8,128)(2,1)}, u32[]{:S(2)}, u32[]{:S(2)}) collective-permute-start(bf16[256,512]{1,0:T(8,128)(2,1)} %get-tuple-element.42.g2_own), channel_id=1, source_target_pairs={{0,4},{2,6},{4,8},{5,1},{6,10},{7,3},{8,12},{9,5},{10,14},{11,7},{... | collective-permute-start | bytes 786440 | tf_op jit(solution)/shard_map/ppermute | solution.py:284
  137.1 3.0 %collective-permute-start.13 = (bf16[1,128,512]{2,1,0:T(8,128)(2,1)}, bf16[1,128,512]{2,1,0:T(8,128)(2,1)}, u32[]{:S(2)}, u32[]{:S(2)}) collective-permute-start(bf16[1,128,512]{2,1,0:T(8,128)(2,1)} %get-tuple-element.53), channel_id=1, source_target_pairs={{0,128},{128,256},{256,384},{384,0},{1,129},{129,257},{257,385},{3... | collective-permute-start | bytes 393224 | tf_op jit(solution)/shard_map/ppermute | solution.py:308
  140.2 3.8 %collective-permute-start.14 = (bf16[1,128,512]{2,1,0:T(8,128)(2,1)}, bf16[1,128,512]{2,1,0:T(8,128)(2,1)S(1)}, u32[]{:S(2)}, u32[]{:S(2)}) collective-permute-start(bf16[1,128,512]{2,1,0:T(8,128)(2,1)} %get-tuple-element.52), channel_id=1, source_target_pairs={{0,256},{128,384},{256,0},{384,128},{1,257},{129,385},{257,1},{385... | collective-permute-start | bytes 393224 | tf_op jit(solution)/shard_map/ppermute | solution.py:308
  144.0 4.0 %collective-permute-start.15 = (bf16[1,128,512]{2,1,0:T(8,128)(2,1)}, bf16[1,128,512]{2,1,0:T(8,128)(2,1)S(1)}, u32[]{:S(2)}, u32[]{:S(2)}) collective-permute-start(bf16[1,128,512]{2,1,0:T(8,128)(2,1)} %get-tuple-element.51), channel_id=1, source_target_pairs={{0,384},{128,0},{256,128},{384,256},{1,385},{129,1},{257,129},{385... | collective-permute-start | bytes 393224 | tf_op jit(solution)/shard_map/ppermute | solution.py:308
  150.9 2.4 %collective-permute-start.23 = (bf16[256,512]{1,0:T(8,128)(2,1)}, bf16[256,512]{1,0:T(8,128)(2,1)S(1)}, u32[]{:S(2)}, u32[]{:S(2)}) collective-permute-start(bf16[256,512]{1,0:T(8,128)(2,1)} %collective-permute-done.21.r2), channel_id=1, source_target_pairs={{0,1},{1,0},{2,3},{3,2},{4,5},{5,4},{6,7},{7,6},{8,9},{9,8},{10,11... | collective-permute-start | bytes 786440 | tf_op jit(solution)/shard_map/ppermute | solution.py:273
  157.7 5.6 %backward_b.1 = bf16[4,128,512]{2,1,0:T(8,128)(2,1)S(1)} custom-call(bf16[256,512]{1,0:T(8,128)(2,1)} %get-tuple-element.42.g2_own, bf16[256,512]{1,0:T(8,128)(2,1)} %collective-permute-done.20.r1, bf16[256,512]{1,0:T(8,128)(2,1)} %collective-permute-done.21.r2, bf16[256,512]{1,0:T(8,128)(2,1)S(1)} %collective-permute-done.22.o1, ...), custom_call_target="tpu_custom_call" | custom-call | tf_op jit(solution)/shard_map/backward_b/pallas_call | solution.py:386
  165.4 3.6 %collective-permute-start.25 = (bf16[1,128,512]{2,1,0:T(8,128)(2,1)S(1)}, bf16[1,128,512]{2,1,0:T(8,128)(2,1)S(1)}, u32[]{:S(2)}, u32[]{:S(2)}) collective-permute-start(bf16[1,128,512]{2,1,0:T(8,128)(2,1)S(1)} %get-tuple-element.49), channel_id=1, source_target_pairs={{0,256},{128,384},{256,0},{384,128},{1,257},{129,385},{257,1},{385... | collective-permute-start | bytes 393224 | tf_op jit(solution)/shard_map/ppermute | solution.py:308
  168.9 4.0 %collective-permute-start.26 = (bf16[1,128,512]{2,1,0:T(8,128)(2,1)S(1)}, bf16[1,128,512]{2,1,0:T(8,128)(2,1)S(1)}, u32[]{:S(2)}, u32[]{:S(2)}) collective-permute-start(bf16[1,128,512]{2,1,0:T(8,128)(2,1)S(1)} %get-tuple-element.48), channel_id=1, source_target_pairs={{0,384},{128,0},{256,128},{384,256},{1,385},{129,1},{257,129},{385... | collective-permute-start | bytes 393224 | tf_op jit(solution)/shard_map/ppermute | solution.py:308
  173.0 2.0 %collective-permute-done.24 = bf16[1,128,512]{2,1,0:T(8,128)(2,1)S(1)} collective-permute-done((bf16[1,128,512]{2,1,0:T(8,128)(2,1)S(1)}, bf16[1,128,512]{2,1,0:T(8,128)(2,1)S(1)}, u32[]{:S(2)}, u32[]{:S(2)}) %collective-permute-start.24) | collective-permute-done | bytes 131104 | tf_op jit(solution)/shard_map/ppermute | solution.py:308
  175.1 2.5 %collective-permute-done.26 = bf16[1,128,512]{2,1,0:T(8,128)(2,1)S(1)} collective-permute-done((bf16[1,128,512]{2,1,0:T(8,128)(2,1)S(1)}, bf16[1,128,512]{2,1,0:T(8,128)(2,1)S(1)}, u32[]{:S(2)}, u32[]{:S(2)}) %collective-permute-start.26) | collective-permute-done | bytes 131104 | tf_op jit(solution)/shard_map/ppermute | solution.py:308
  (74 shorter events, 25.2 us)
Async XLA Ops:
  4.7 46.5 %collective-permute-start.1 = (bf16[1568,512]{1,0:T(8,128)(2,1)S(1)}, bf16[1568,512]{1,0:T(8,128)(2,1)S(1)}, u32[]{:S(2)}, u32[]{:S(2)}) collective-permute-start(bf16[1568,512]{1,0:T(8,128)(2,1)S(1)} %get-tuple-element.26.w_own), channel_id=1, source_target_pairs={{0,128},{1,385},{128,256},{129,1},{256,384},{257,129},{384,0},{385... | collective-permute-start | bytes 4816904 | tf_op jit(solution)/shard_map/ppermute | solution.py:293
  10.5 4.2 %collective-permute-start = (bf16[128,1792]{1,0:T(8,128)(2,1)S(1)}, bf16[128,1792]{1,0:T(8,128)(2,1)S(1)}, u32[]{:S(2)}, u32[]{:S(2)}) collective-permute-start(bf16[128,1792]{1,0:T(8,128)(2,1)S(1)} %prepare.1.own), channel_id=1, source_target_pairs={{0,1},{1,0},{2,3},{3,2},{4,5},{5,4},{6,7},{7,6},{8,9},{9,8},{10,11... | collective-permute-start | bytes 1376264 | tf_op jit(solution)/shard_map/ppermute | solution.py:273
  14.7 36.4 %collective-permute-start.2 = (bf16[256,1792]{1,0:T(8,128)(2,1)S(1)}, bf16[256,1792]{1,0:T(8,128)(2,1)S(1)}, u32[]{:S(2)}, u32[]{:S(2)}) collective-permute-start(bf16[256,1792]{1,0:T(8,128)(2,1)S(1)} %get-tuple-element.25.own), channel_id=1, source_target_pairs={{0,2},{2,4},{3,1},{4,6},{5,3},{6,8},{7,5},{8,10},{9,7},{10,12},{11... | collective-permute-start | bytes 2752520 | tf_op jit(solution)/shard_map/ppermute | solution.py:284
  18.2 31.4 %collective-permute-start.3 = (bf16[256,1280]{1,0:T(8,128)(2,1)S(1)}, bf16[256,1280]{1,0:T(8,128)(2,1)S(1)}, u32[]{:S(2)}, u32[]{:S(2)}) collective-permute-start(bf16[256,1280]{1,0:T(8,128)(2,1)S(1)} %get-tuple-element.27), channel_id=1, source_target_pairs={{0,4},{2,6},{4,8},{5,1},{6,10},{7,3},{8,12},{9,5},{10,14},{11,7},{... | collective-permute-start | bytes 1966088 | tf_op jit(solution)/shard_map/ppermute | solution.py:284
  23.7 27.5 %collective-permute-start.4 = (bf16[256,1280]{1,0:T(8,128)(2,1)S(1)}, bf16[256,1280]{1,0:T(8,128)(2,1)S(1)}, u32[]{:S(2)}, u32[]{:S(2)}) collective-permute-start(bf16[256,1280]{1,0:T(8,128)(2,1)S(1)} %get-tuple-element.27), channel_id=1, source_target_pairs={{0,6},{2,8},{4,10},{6,12},{7,1},{8,14},{9,3},{10,16},{11,5},{12,18... | collective-permute-start | bytes 1966088 | tf_op jit(solution)/shard_map/ppermute | solution.py:284
  28.0 15.0 %collective-permute-start.5 = (bf16[256,512]{1,0:T(8,128)(2,1)S(1)}, bf16[256,512]{1,0:T(8,128)(2,1)S(1)}, u32[]{:S(2)}, u32[]{:S(2)}) collective-permute-start(bf16[256,512]{1,0:T(8,128)(2,1)S(1)} %get-tuple-element.28), channel_id=1, source_target_pairs={{0,8},{2,10},{4,12},{6,14},{8,16},{9,1},{10,18},{11,3},{12,20},{13... | collective-permute-start | bytes 786440 | tf_op jit(solution)/shard_map/ppermute | solution.py:284
  43.0 17.7 %collective-permute-start.11 = (bf16[784,512]{1,0:T(8,128)(2,1)S(1)}, bf16[784,512]{1,0:T(8,128)(2,1)S(1)}, u32[]{:S(2)}, u32[]{:S(2)}) collective-permute-start(bf16[784,512]{1,0:T(8,128)(2,1)S(1)} %get-tuple-element.34), channel_id=1, source_target_pairs={{0,256},{128,384},{256,0},{384,128},{1,257},{129,385},{257,1},{385... | collective-permute-start | bytes 2408456 | tf_op jit(solution)/shard_map/ppermute | solution.py:298
  51.2 27.6 %collective-permute-start.10 = (bf16[1568,512]{1,0:T(8,128)(2,1)S(1)}, bf16[1568,512]{1,0:T(8,128)(2,1)S(1)}, u32[]{:S(2)}, u32[]{:S(2)}) collective-permute-start(bf16[1568,512]{1,0:T(8,128)(2,1)S(1)} %collective-permute-done.1.w_m), channel_id=1, source_target_pairs={{0,1},{1,0},{2,3},{3,2},{4,5},{5,4},{6,7},{7,6},{8,9},{9,8},{10,11... | collective-permute-start | bytes 4816904 | tf_op jit(solution)/shard_map/ppermute | solution.py:273
  60.8 14.4 %collective-permute-start.12 = (bf16[784,512]{1,0:T(8,128)(2,1)S(1)}, bf16[784,512]{1,0:T(8,128)(2,1)S(1)}, u32[]{:S(2)}, u32[]{:S(2)}) collective-permute-start(bf16[784,512]{1,0:T(8,128)(2,1)S(1)} %collective-permute-done.11.w_mh), channel_id=1, source_target_pairs={{0,1},{1,0},{2,3},{3,2},{4,5},{5,4},{6,7},{7,6},{8,9},{9,8},{10,11... | collective-permute-start | bytes 2408456 | tf_op jit(solution)/shard_map/ppermute | solution.py:273
  68.9 9.8 %collective-permute-start.6 = (bf16[256,1792]{1,0:T(8,128)(2,1)S(1)}, bf16[256,1792]{1,0:T(8,128)(2,1)S(1)}, u32[]{:S(2)}, u32[]{:S(2)}) collective-permute-start(bf16[256,1792]{1,0:T(8,128)(2,1)S(1)} %collective-permute-done.2.m1), channel_id=1, source_target_pairs={{0,1},{1,0},{2,3},{3,2},{4,5},{5,4},{6,7},{7,6},{8,9},{9,8},{10,11... | collective-permute-start | bytes 2752520 | tf_op jit(solution)/shard_map/ppermute | solution.py:273
  70.8 7.9 %collective-permute-start.7 = (bf16[256,1280]{1,0:T(8,128)(2,1)S(1)}, bf16[256,1280]{1,0:T(8,128)(2,1)S(1)}, u32[]{:S(2)}, u32[]{:S(2)}) collective-permute-start(bf16[256,1280]{1,0:T(8,128)(2,1)S(1)} %collective-permute-done.3.m2), channel_id=1, source_target_pairs={{0,1},{1,0},{2,3},{3,2},{4,5},{5,4},{6,7},{7,6},{8,9},{9,8},{10,11... | collective-permute-start | bytes 1966088 | tf_op jit(solution)/shard_map/ppermute | solution.py:273
  73.2 5.5 %collective-permute-start.8 = (bf16[256,1280]{1,0:T(8,128)(2,1)S(1)}, bf16[256,1280]{1,0:T(8,128)(2,1)S(1)}, u32[]{:S(2)}, u32[]{:S(2)}) collective-permute-start(bf16[256,1280]{1,0:T(8,128)(2,1)S(1)} %collective-permute-done.4.m3), channel_id=1, source_target_pairs={{0,1},{1,0},{2,3},{3,2},{4,5},{5,4},{6,7},{7,6},{8,9},{9,8},{10,11... | collective-permute-start | bytes 1966088 | tf_op jit(solution)/shard_map/ppermute | solution.py:273
  75.2 3.6 %collective-permute-start.9 = (bf16[256,512]{1,0:T(8,128)(2,1)S(1)}, bf16[256,512]{1,0:T(8,128)(2,1)S(1)}, u32[]{:S(2)}, u32[]{:S(2)}) collective-permute-start(bf16[256,512]{1,0:T(8,128)(2,1)S(1)} %collective-permute-done.5.m4), channel_id=1, source_target_pairs={{0,1},{1,0},{2,3},{3,2},{4,5},{5,4},{6,7},{7,6},{8,9},{9,8},{10,11... | collective-permute-start | bytes 786440 | tf_op jit(solution)/shard_map/ppermute | solution.py:273
  94.1 29.7 %copy-start = (bf16[3136,512]{1,0:T(8,128)(2,1)}, bf16[3136,512]{1,0:T(8,128)(2,1)S(1)}, u32[]{:S(2)}) copy-start(bf16[3136,512]{1,0:T(8,128)(2,1)S(1)} %get-tuple-element.47.weights) | copy-start | bytes 9633796
  94.1 29.7 %copy-start.2 = (bf16[768,512]{1,0:T(8,128)(2,1)}, bf16[768,512]{1,0:T(8,128)(2,1)S(1)}, u32[]{:S(2)}) copy-start(bf16[768,512]{1,0:T(8,128)(2,1)S(1)} %get-tuple-element.44.v1) | copy-start | bytes 2359300
  94.1 29.6 %copy-start.4 = (bf16[768,512]{1,0:T(8,128)(2,1)}, bf16[768,512]{1,0:T(8,128)(2,1)S(1)}, u32[]{:S(2)}) copy-start(bf16[768,512]{1,0:T(8,128)(2,1)S(1)} %get-tuple-element.46.f0) | copy-start | bytes 2359300
  94.1 29.6 %copy-start.9 = (bf16[4,128,512]{2,1,0:T(8,128)(2,1)}, bf16[4,128,512]{2,1,0:T(8,128)(2,1)S(1)}, u32[]{:S(2)}) copy-start(bf16[4,128,512]{2,1,0:T(8,128)(2,1)S(1)} %get-tuple-element.35) | copy-start | bytes 1572868
  94.1 16.5 %collective-permute-start.16 = (bf16[256,512]{1,0:T(8,128)(2,1)S(1)}, bf16[256,512]{1,0:T(8,128)(2,1)S(1)}, u32[]{:S(2)}, u32[]{:S(2)}) collective-permute-start(bf16[256,512]{1,0:T(8,128)(2,1)S(1)} %get-tuple-element.36.grad_pre), channel_id=1, source_target_pairs={{0,2},{2,4},{3,1},{4,6},{5,3},{6,8},{7,5},{8,10},{9,7},{10,12},{11... | collective-permute-start | bytes 786440 | tf_op jit(solution)/shard_map/ppermute | solution.py:284
  99.5 16.2 %collective-permute-start.17 = (bf16[256,512]{1,0:T(8,128)(2,1)S(1)}, bf16[256,512]{1,0:T(8,128)(2,1)S(1)}, u32[]{:S(2)}, u32[]{:S(2)}) collective-permute-start(bf16[256,512]{1,0:T(8,128)(2,1)S(1)} %get-tuple-element.36.grad_pre), channel_id=1, source_target_pairs={{0,4},{2,6},{4,8},{5,1},{6,10},{7,3},{8,12},{9,5},{10,14},{11,7},{... | collective-permute-start | bytes 786440 | tf_op jit(solution)/shard_map/ppermute | solution.py:284
  110.6 7.6 %collective-permute-start.18 = (bf16[256,512]{1,0:T(8,128)(2,1)S(1)}, bf16[256,512]{1,0:T(8,128)(2,1)S(1)}, u32[]{:S(2)}, u32[]{:S(2)}) collective-permute-start(bf16[256,512]{1,0:T(8,128)(2,1)S(1)} %collective-permute-done.16.r1), channel_id=1, source_target_pairs={{0,1},{1,0},{2,3},{3,2},{4,5},{5,4},{6,7},{7,6},{8,9},{9,8},{10,11... | collective-permute-start | bytes 786440 | tf_op jit(solution)/shard_map/ppermute | solution.py:273
  115.6 3.7 %collective-permute-start.19 = (bf16[256,512]{1,0:T(8,128)(2,1)S(1)}, bf16[256,512]{1,0:T(8,128)(2,1)S(1)}, u32[]{:S(2)}, u32[]{:S(2)}) collective-permute-start(bf16[256,512]{1,0:T(8,128)(2,1)S(1)} %collective-permute-done.17.r2), channel_id=1, source_target_pairs={{0,1},{1,0},{2,3},{3,2},{4,5},{5,4},{6,7},{7,6},{8,9},{9,8},{10,11... | collective-permute-start | bytes 786440 | tf_op jit(solution)/shard_map/ppermute | solution.py:273
  123.7 25.3 %collective-permute-start.20 = (bf16[256,512]{1,0:T(8,128)(2,1)}, bf16[256,512]{1,0:T(8,128)(2,1)}, u32[]{:S(2)}, u32[]{:S(2)}) collective-permute-start(bf16[256,512]{1,0:T(8,128)(2,1)} %get-tuple-element.42.g2_own), channel_id=1, source_target_pairs={{0,2},{2,4},{3,1},{4,6},{5,3},{6,8},{7,5},{8,10},{9,7},{10,12},{11... | collective-permute-start | bytes 786440 | tf_op jit(solution)/shard_map/ppermute | solution.py:284
  128.1 22.8 %collective-permute-start.21 = (bf16[256,512]{1,0:T(8,128)(2,1)}, bf16[256,512]{1,0:T(8,128)(2,1)}, u32[]{:S(2)}, u32[]{:S(2)}) collective-permute-start(bf16[256,512]{1,0:T(8,128)(2,1)} %get-tuple-element.42.g2_own), channel_id=1, source_target_pairs={{0,4},{2,6},{4,8},{5,1},{6,10},{7,3},{8,12},{9,5},{10,14},{11,7},{... | collective-permute-start | bytes 786440 | tf_op jit(solution)/shard_map/ppermute | solution.py:284
  137.1 16.3 %collective-permute-start.13 = (bf16[1,128,512]{2,1,0:T(8,128)(2,1)}, bf16[1,128,512]{2,1,0:T(8,128)(2,1)}, u32[]{:S(2)}, u32[]{:S(2)}) collective-permute-start(bf16[1,128,512]{2,1,0:T(8,128)(2,1)} %get-tuple-element.53), channel_id=1, source_target_pairs={{0,128},{128,256},{256,384},{384,0},{1,129},{129,257},{257,385},{3... | collective-permute-start | bytes 393224 | tf_op jit(solution)/shard_map/ppermute | solution.py:308
  140.1 14.6 %copy-start.3 = (bf16[768,512]{1,0:T(8,128)(2,1)S(1)}, bf16[768,512]{1,0:T(8,128)(2,1)}, u32[]{:S(2)}) copy-start(bf16[768,512]{1,0:T(8,128)(2,1)} %copy-done.2) | copy-start | bytes 2359300
  140.2 14.1 %collective-permute-start.14 = (bf16[1,128,512]{2,1,0:T(8,128)(2,1)}, bf16[1,128,512]{2,1,0:T(8,128)(2,1)S(1)}, u32[]{:S(2)}, u32[]{:S(2)}) collective-permute-start(bf16[1,128,512]{2,1,0:T(8,128)(2,1)} %get-tuple-element.52), channel_id=1, source_target_pairs={{0,256},{128,384},{256,0},{384,128},{1,257},{129,385},{257,1},{385... | collective-permute-start | bytes 393224 | tf_op jit(solution)/shard_map/ppermute | solution.py:308
  144.0 21.4 %collective-permute-start.15 = (bf16[1,128,512]{2,1,0:T(8,128)(2,1)}, bf16[1,128,512]{2,1,0:T(8,128)(2,1)S(1)}, u32[]{:S(2)}, u32[]{:S(2)}) collective-permute-start(bf16[1,128,512]{2,1,0:T(8,128)(2,1)} %get-tuple-element.51), channel_id=1, source_target_pairs={{0,384},{128,0},{256,128},{384,256},{1,385},{129,1},{257,129},{385... | collective-permute-start | bytes 393224 | tf_op jit(solution)/shard_map/ppermute | solution.py:308
  149.0 5.3 %collective-permute-start.22 = (bf16[256,512]{1,0:T(8,128)(2,1)}, bf16[256,512]{1,0:T(8,128)(2,1)S(1)}, u32[]{:S(2)}, u32[]{:S(2)}) collective-permute-start(bf16[256,512]{1,0:T(8,128)(2,1)} %collective-permute-done.20.r1), channel_id=1, source_target_pairs={{0,1},{1,0},{2,3},{3,2},{4,5},{5,4},{6,7},{7,6},{8,9},{9,8},{10,11... | collective-permute-start | bytes 786440 | tf_op jit(solution)/shard_map/ppermute | solution.py:273
  150.9 3.8 %collective-permute-start.23 = (bf16[256,512]{1,0:T(8,128)(2,1)}, bf16[256,512]{1,0:T(8,128)(2,1)S(1)}, u32[]{:S(2)}, u32[]{:S(2)}) collective-permute-start(bf16[256,512]{1,0:T(8,128)(2,1)} %collective-permute-done.21.r2), channel_id=1, source_target_pairs={{0,1},{1,0},{2,3},{3,2},{4,5},{5,4},{6,7},{7,6},{8,9},{9,8},{10,11... | collective-permute-start | bytes 786440 | tf_op jit(solution)/shard_map/ppermute | solution.py:273
  163.4 11.7 %collective-permute-start.24 = (bf16[1,128,512]{2,1,0:T(8,128)(2,1)S(1)}, bf16[1,128,512]{2,1,0:T(8,128)(2,1)S(1)}, u32[]{:S(2)}, u32[]{:S(2)}) collective-permute-start(bf16[1,128,512]{2,1,0:T(8,128)(2,1)S(1)} %get-tuple-element.50), channel_id=1, source_target_pairs={{0,128},{128,256},{256,384},{384,0},{1,129},{129,257},{257,385},{3... | collective-permute-start | bytes 393224 | tf_op jit(solution)/shard_map/ppermute | solution.py:308
  165.4 9.7 %collective-permute-start.25 = (bf16[1,128,512]{2,1,0:T(8,128)(2,1)S(1)}, bf16[1,128,512]{2,1,0:T(8,128)(2,1)S(1)}, u32[]{:S(2)}, u32[]{:S(2)}) collective-permute-start(bf16[1,128,512]{2,1,0:T(8,128)(2,1)S(1)} %get-tuple-element.49), channel_id=1, source_target_pairs={{0,256},{128,384},{256,0},{384,128},{1,257},{129,385},{257,1},{385... | collective-permute-start | bytes 393224 | tf_op jit(solution)/shard_map/ppermute | solution.py:308
  168.9 8.7 %collective-permute-start.26 = (bf16[1,128,512]{2,1,0:T(8,128)(2,1)S(1)}, bf16[1,128,512]{2,1,0:T(8,128)(2,1)S(1)}, u32[]{:S(2)}, u32[]{:S(2)}) collective-permute-start(bf16[1,128,512]{2,1,0:T(8,128)(2,1)S(1)} %get-tuple-element.48), channel_id=1, source_target_pairs={{0,384},{128,0},{256,128},{384,256},{1,385},{129,1},{257,129},{385... | collective-permute-start | bytes 393224 | tf_op jit(solution)/shard_map/ppermute | solution.py:308
  (12 other events, 33.9 us)

commit v3 on v2

--- a/solution.py
+++ b/solution.py
@@ -13,12 +13,15 @@
 B = 128
 PAIR = 2 * B
 BAND = 3 * PAIR
+SENT = 5 * B
+WIDE = H + SENT
 REACH = 4
 W_ROWS = 3 * H + 32
 W_HALF = W_ROWS // 2
 F32, BF16 = jnp.float32, jnp.bfloat16
 VMEM = pl.BlockSpec(memory_space=pltpu.VMEM)
 HBM = pl.BlockSpec(memory_space=pltpu.HBM)
+ANY = pl.BlockSpec(memory_space=pl.ANY)
 FWD_MIB, BWD_MIB = 24, 12
 
 
@@ -43,36 +46,48 @@
     return centre * inv, inv
 
 
-def call(kernel, outs, specs, scratch, limit_mib, name, flops=0):
+def call(kernel, outs, specs, scratch, limit_mib, name, out_specs=None, aliases=None, units=0):
     return pl.pallas_call(
         kernel,
         out_shape=[jax.ShapeDtypeStruct(s, d) for s, d in outs],
         in_specs=specs,
-        out_specs=[VMEM] * len(outs),
+        out_specs=out_specs or [VMEM] * len(outs),
+        input_output_aliases=aliases or {},
+        cost_estimate=pl.CostEstimate(
+            flops=units * 2 * B * H * H, bytes_accessed=units * 2 * B * H, transcendentals=0
+        ),
         scratch_shapes=scratch,
         compiler_params=pltpu.CompilerParams(vmem_limit_bytes=limit_mib << 20),
         name=name,
     )
 
 
-def weights_kernel(w_a, w_b, w_c, gain, weights, half, gain_here, sems):
-    copies = [pltpu.make_async_copy(gain, gain_here, sems.at[3])]
-    for which, ref in enumerate((w_a, w_b, w_c)):
-        copies.append(pltpu.make_async_copy(ref.at[0], weights.at[rows(which, H)], sems.at[which]))
+def weights_kernel(w_a, w_b, w_c, gain, weights, gain_here, terms, sems):
+    copies = [
+        pltpu.make_async_copy(ref.at[0], weights.at[rows(which, H)], sems.at[which])
+        for which, ref in enumerate((w_a, w_b, w_c))
+    ]
+    first = pltpu.make_async_copy(gain, gain_here, sems.at[3])
+    first.start()
     for copy in copies:
         copy.start()
-    copies[0].wait()
-    rest = jnp.broadcast_to(gain_here[0:1, :], (16, H))
+    first.wait()
+    rest = jnp.broadcast_to(gain_here[0:1, :], (32, H))
     high = rest.astype(BF16).astype(F32)
     rest = rest - high
     mid = rest.astype(BF16).astype(F32)
     low = rest - mid
-    row = lax.broadcasted_iota(jnp.int32, (16, H), 0)
-    terms = jnp.where(row == 0, high, jnp.where(row == 1, mid, jnp.where(row == 2, low, 0.0)))
-    weights[3 * H : 3 * H + 16, :] = terms.astype(BF16)
-    weights[3 * H + 16 : 3 * H + 32, :] = jnp.zeros((16, H), BF16)
-    for copy in copies[1:]:
+    row = lax.broadcasted_iota(jnp.int32, (32, H), 0)
+    held = jnp.where(row == 0, high, jnp.where(row == 1, mid, jnp.where(row == 2, low, 0.0)))
+    terms[...] = held.astype(BF16)
+    last = pltpu.make_async_copy(terms, weights.at[pl.ds(3 * H, 32)], sems.at[4])
+    last.start()
+    for copy in copies:
         copy.wait()
+    last.wait()
+
+
+def half_kernel(weights, half):
     core = lax.axis_index("core")
     half[...] = weights[pl.ds(pl.multiple_of(core * W_HALF, 16), W_HALF), :]
 
@@ -91,8 +106,8 @@
     for copy in copies[:3]:
         copy.wait()
     slots = tile.shape[0]
-    base = 2 * (lax.axis_index("chip") - 1)
-    for column in range(6):
+    base = 2 * lax.axis_index("chip") + lax.axis_index("core") - 2
+    for column in range(5):
         total = jnp.zeros((B, B), F32)
         for slot in range(slots):
             hit = (index[slot] - base == column) & (slot < count[0])
@@ -101,15 +116,15 @@
     for copy in copies[3:]:
         copy.wait()
     own[:, 0:H] = value[...]
-    own[:, H + BAND :] = slope[...]
-
-
-def pack_kernel(own, partner, pair, near, value):
+    own[:, WIDE:] = slope[...]
+
+
+def pack_kernel(own, partner, near, value, slope):
     core = lax.axis_index("core")
     for ref, held in ((own, core), (partner, 1 - core)):
-        pair[rows(held, B), :] = ref[...]
-        near[rows(held, B), :] = ref[:, 0 : H + BAND]
+        near[rows(held, B), :] = ref[:, 0:WIDE]
         value[rows(held, B), :] = ref[:, 0:H]
+        slope[rows(held, B), :] = ref[:, WIDE:]
 
 
 def layer_gain(weights, layer):
@@ -122,10 +137,15 @@
     return weights[start : start + H, :]
 
 
+def send_pieces(stacked, pieces, section):
+    for step, piece in enumerate(pieces):
+        piece[...] = stacked[(section + step) % 4]
+
+
 def forward_kernel(
-    own, m1, m2, m3, m4, t1, t2, t3, t4, w_own, w_m, w_t, w_mh, w_th,
-    latents, grad_pre, turned, v3_out, v2_out, v1_out, f2_out, f1_out, f0_out, weights, w_low,
-    v_a, v_b, band, unit, source,
+    own, cotangent, m1, m2, m3, m4, t1, t2, t3, t4, w_own, w_m, w_t, w_mh, w_th, _,
+    l0, l1, l2, l3, grad_pre, turned, v3_out, v2_out, v1_out, f2_out, f1_out, f0_out, weights,
+    latents, v_a, v_b, band, unit, source,
 ):
     section, core = lax.axis_index("section"), lax.axis_index("core")
     weights[pl.ds(pl.multiple_of(section * W_ROWS, 16), W_ROWS), :] = w_own[...]
@@ -138,18 +158,24 @@
     weights[pl.ds(pl.multiple_of(far * W_ROWS + core * W_HALF, 16), W_HALF), :] = w_mh[...]
     weights[pl.ds(pl.multiple_of(far * W_ROWS + (1 - core) * W_HALF, 16), W_HALF), :] = w_th[...]
 
+    def put_band(at, ref):
+        for k in range(2):
+            row = pl.ds(pl.multiple_of(at * PAIR + k * B, B), B)
+            band[row, k * B : k * B + SENT] = ref[k * B : (k + 1) * B, H:WIDE]
+            rim = (1 - k) * SENT
+            band[row, rim : rim + B] = jnp.zeros((B, B), BF16)
+
     v_a[rows(REACH), :] = own[:, 0:H]
-    band[rows(REACH - 1), :] = own[:, H : H + BAND]
+    put_band(REACH - 1, own)
     for step, (m, t) in enumerate(((m1, t1), (m2, t2), (m3, t3), (m4, t4)), start=1):
         at_m = REACH - step + 2 * step * core
         at_t = 2 * REACH - at_m
         v_a[rows(at_m), :] = m[:, 0:H]
         v_a[rows(at_t), :] = t[:, 0:H]
         if step < REACH:
-            band[rows(at_m - 1), :] = m[:, H : H + BAND]
-            band[rows(at_t - 1), :] = t[:, H : H + BAND]
-
-    w_low[...] = weights[0 : 2 * W_ROWS, :]
+            put_band(at_m - 1, m)
+            put_band(at_t - 1, t)
+
     now, later = v_a, v_b
     for layer in range(4):
         low, high = layer, 2 * REACH - layer
@@ -172,7 +198,7 @@
             if abs(j - REACH) <= reach:
                 factor = sigma * (1.0 + pre * (1.0 - sigma))
                 if layer == 3:
-                    incoming = dot_t(own[:, H + BAND :], weight(weights, 3, 2))
+                    incoming = dot_t(cotangent[...], weight(weights, 3, 2))
                     grad_pre[...] = (incoming * factor).astype(BF16)
                 else:
                     out = (f0_out, f1_out, f2_out)[layer]
@@ -192,6 +218,7 @@
         if layer == 2:
             v3_out[...] = later[3 * PAIR : 6 * PAIR, :]
         now, later = later, now
+    send_pieces(latents, (l0, l1, l2, l3), section)
 
     for j in range(3, 6):
         for i in range(j - 1, j + 2):
@@ -226,14 +253,12 @@
 
 
 def backward_a_kernel(
-    grad_pre, r1, r2, o1, o2, own, m1, t1, turned, v3, v2, f2, weights,
-    g3_out, g2_out, held, cot, g3, gp2,
+    grad_pre, r1, r2, o1, o2, own, c1, d1, v3, v2, f2, turned, v1, f1, f0, weights,
+    g3_out, g2_out, kept_turned, kept_v1, kept_f1, kept_f0, kept_weights, held, cot, g3, gp2,
 ):
     core = lax.axis_index("core")
     place(held, grad_pre, ((r1, o1), (r2, o2)), core)
-    cot[rows(1), :] = own[:, H + BAND :]
-    cot[rows(2 * core), :] = m1[:, H + BAND :]
-    cot[rows(2 - 2 * core), :] = t1[:, H + BAND :]
+    place(cot, own, ((c1, d1),), core)
     for j in range(3):
         g3[rows(j), :] = grad_pair(
             cot[rows(j), :], held[rows(j + 1), :], held[j * PAIR : j * PAIR + BAND, :],
@@ -248,7 +273,7 @@
 
 def backward_b_kernel(
     g2_own, r1, r2, o1, o2, g3_mine, turned, v1, own, f1, f0, weights,
-    grads, g2, gp1, g1, gp0,
+    p0, p1, p2, p3, grads, g2, gp1, g1, gp0,
 ):
     core = lax.axis_index("core")
     place(g2, g2_own, ((r1, o1), (r2, o2)), core)
@@ -264,9 +289,23 @@
     grads[3] = g3_mine[...]
     grads[2] = g2_own[rows(core, B), :]
     grads[1] = g1[mine, :]
-    g0 = grad_pair(g1[rows(1), :], gp0[rows(1), :], gp0[...], turned[rows(1), :], own[:, 0:H], weights, 0)
+    g0 = grad_pair(g1[rows(1), :], gp0[rows(1), :], gp0[...], turned[rows(1), :], own[...], weights, 0)
     g1[rows(1), :] = g0
     grads[0] = g1[mine, :]
+    send_pieces(grads, (p0, p1, p2, p3), lax.axis_index("section"))
+
+
+def collect_kernel(l0, l1, l2, l3, g0, g1, g2, g3, latents, grads, sems):
+    section = lax.axis_index("section")
+    copies = []
+    for side, (out, pieces) in enumerate(((latents, (l0, l1, l2, l3)), (grads, (g0, g1, g2, g3)))):
+        for step, piece in enumerate(pieces):
+            at = (section + 4 - step) % 4
+            copies.append(pltpu.make_async_copy(piece, out.at[at], sems.at[4 * side + step]))
+    for copy in copies:
+        copy.start()
+    for copy in copies:
+        copy.wait()
 
 
 def swap(value):
@@ -293,39 +332,27 @@
     return lax.ppermute(value, ("section", "core"), pairs)
 
 
-def opposite(value):
+def onward(value, steps):
     count = lax.axis_size("section")
-    return lax.ppermute(value, "section", [(s, (s + count // 2) % count) for s in range(count)])
-
-
-def to_layers(stacked, section):
-    count = stacked.shape[0]
-    out = jnp.zeros_like(stacked)
-    keep = lax.dynamic_index_in_dim(stacked, section, 0, keepdims=True)
-    out = lax.dynamic_update_slice_in_dim(out, keep, section, 0)
-    for step in range(1, count):
-        piece = lax.dynamic_index_in_dim(stacked, (section + step) % count, 0, keepdims=True)
-        got = lax.ppermute(piece, "section", [(s, (s + step) % count) for s in range(count)])
-        out = lax.dynamic_update_slice_in_dim(out, got, (section - step) % count, 0)
-    return out
+    return lax.ppermute(value, "section", [(s, (s + steps) % count) for s in range(count)])
 
 
 def body(latent, cotangent, w_a, w_b, w_c, gain, tiles, pair_source, live_pairs):
     section = lax.axis_index("section")
-    wide = H + BAND
-
-    w_own, w_half = call(
+
+    (w_own,) = call(
         weights_kernel,
-        [((W_ROWS, H), BF16), ((W_HALF, H), BF16)],
+        [((W_ROWS, H), BF16)],
         [HBM] * 4,
-        [pltpu.VMEM((1, H), F32), pltpu.SemaphoreType.DMA((4,))],
-        4,
+        [pltpu.VMEM((1, H), F32), pltpu.VMEM((32, H), BF16), pltpu.SemaphoreType.DMA((5,))],
+        56,
         "weights",
+        out_specs=[HBM],
     )(w_a, w_b, w_c, gain)
-    w_m, w_mh = around(w_own), opposite(w_half)
+    w_m = around(w_own)
     (own,) = call(
         prepare_kernel,
-        [((B, wide + H), BF16)],
+        [((B, WIDE + H), BF16)],
         [HBM] * 5,
         [
             pltpu.VMEM((B, H), BF16), pltpu.VMEM((B, H), BF16), pltpu.VMEM(tiles.shape, BF16),
@@ -335,67 +362,92 @@
         4,
         "prepare",
     )(pair_source, live_pairs, latent, cotangent, tiles)
-    pair, near, value = call(
+    near, value, slope = call(
         pack_kernel,
-        [((PAIR, wide + H), BF16), ((PAIR, wide), BF16), ((PAIR, H), BF16)],
+        [((PAIR, WIDE), BF16), ((PAIR, H), BF16), ((PAIR, H), BF16)],
         [VMEM] * 2,
         [],
         4,
         "pack",
     )(own, swap(own))
-    m1, m2, m3, m4 = spread(pair, 1), spread(near, 2), spread(near, 3), spread(value, 4)
-    w_m, m1, m2, m3, m4 = lax.optimization_barrier((w_m, m1, m2, m3, m4))
+    m1, m3, m4 = spread(near, 1), spread(near, 3), spread(value, 4)
+    arrived, m4 = lax.optimization_barrier((w_m, m4))
+    (w_half,) = call(half_kernel, [((W_HALF, H), BF16)], [VMEM], [], 4, "half")(arrived)
+    w_mh = around(w_half)
+    m2 = spread(m1, 1)
+    w_m, m1, m3, m4, after = lax.optimization_barrier((w_m, m1, m3, m4, slope))
+    c1 = spread(after, 1)
+    d1 = swap(c1)
     w_t, w_th = swap(w_m), swap(w_mh)
     t1, t2, t3, t4 = swap(m1), swap(m2), swap(m3), swap(m4)
 
     span = 2 * REACH + 1
-    latents, grad_pre, turned, v3, v2, v1, f2, f1, f0, weights, w_low = call(
+    l0, l1, l2, l3, grad_pre, turned, v3, v2, v1, f2, f1, f0, weights = call(
         forward_kernel,
         [
-            ((4, B, H), BF16), ((PAIR, H), BF16), ((3 * PAIR, BAND), BF16),
+            ((B, H), BF16), ((B, H), BF16), ((B, H), BF16), ((B, H), BF16),
+            ((PAIR, H), BF16), ((3 * PAIR, BAND), BF16),
             ((3 * PAIR, H), BF16), ((PAIR, H), BF16), ((3 * PAIR, H), BF16),
             ((3 * PAIR, H), BF16), ((5 * PAIR, H), BF16), ((3 * PAIR, H), BF16),
-            ((4 * W_ROWS, H), BF16), ((2 * W_ROWS, H), BF16),
+            ((4 * W_ROWS, H), BF16),
         ],
-        [VMEM] * 14,
+        [VMEM] * 15 + [ANY],
         [
+            pltpu.VMEM((4, B, H), BF16),
             pltpu.VMEM((span * PAIR, H), BF16), pltpu.VMEM((span * PAIR, H), BF16),
             pltpu.VMEM(((span - 2) * PAIR, BAND), BF16),
             pltpu.VMEM((span * PAIR, H), BF16), pltpu.VMEM((span * PAIR, H), BF16),
         ],
         FWD_MIB,
         "forward",
-    )(pair, m1, m2, m3, m4, t1, t2, t3, t4, w_own, w_m, w_t, w_mh, w_th)
-
-    r1, r2 = spread(grad_pre, 1), spread(grad_pre, 2)
-    g3, g2 = call(
+        units=160,
+    )(near, slope, m1, m2, m3, m4, t1, t2, t3, t4, w_own, w_m, w_t, w_mh, w_th, d1)
+
+    latents = [onward(l1, 1), onward(l2, 2), onward(l3, 3)]
+    r1 = spread(grad_pre, 1)
+    r2 = spread(r1, 1)
+    kept = [turned, v1, f1, f0, weights]
+    g3, g2, turned, v1, f1, f0, weights = call(
         backward_a_kernel,
-        [((B, H), BF16), ((PAIR, H), BF16)],
-        [VMEM] * 13,
+        [((B, H), BF16), ((PAIR, H), BF16)] + [(k.shape, k.dtype) for k in kept],
+        [VMEM] * 12 + [ANY] * 3 + [VMEM],
         [
             pltpu.VMEM((5 * PAIR, H), BF16), pltpu.VMEM((3 * PAIR, H), BF16),
             pltpu.VMEM((3 * PAIR, H), BF16), pltpu.VMEM((3 * PAIR, H), BF16),
         ],
         BWD_MIB,
         "backward_a",
-    )(grad_pre, r1, r2, swap(r1), swap(r2), pair, m1, t1, turned, v3, v2, f2, weights)
-
-    latent_result = to_layers(latents, section)
-
-    r1, r2 = spread(g2, 1), spread(g2, 2)
-    (grads,) = call(
+        out_specs=[VMEM] * 2 + [ANY] * len(kept),
+        aliases={11 + i: 2 + i for i in range(len(kept))},
+        units=60,
+    )(grad_pre, r1, r2, swap(r1), swap(r2), slope, c1, d1, v3, v2, f2, *kept)
+
+    r1 = spread(g2, 1)
+    r2 = spread(r1, 1)
+    grads = call(
         backward_b_kernel,
-        [((4, B, H), BF16)],
+        [((B, H), BF16)] * 4,
         [VMEM] * 12,
         [
+            pltpu.VMEM((4, B, H), BF16),
             pltpu.VMEM((5 * PAIR, H), BF16), pltpu.VMEM((5 * PAIR, H), BF16),
             pltpu.VMEM((3 * PAIR, H), BF16), pltpu.VMEM((3 * PAIR, H), BF16),
         ],
         BWD_MIB,
         "backward_b",
-    )(g2, r1, r2, swap(r1), swap(r2), g3, turned, v1, pair, f1, f0, w_low)
-
-    grad_result = to_layers(grads, section)
+        units=70,
+    )(g2, r1, r2, swap(r1), swap(r2), g3, turned, v1, value, f1, f0, weights)
+
+    moved = [onward(piece, step) for step, piece in enumerate(grads) if step]
+    latent_result, grad_result = call(
+        collect_kernel,
+        [((4, B, H), BF16)] * 2,
+        [VMEM] * 8,
+        [pltpu.SemaphoreType.DMA((8,))],
+        4,
+        "collect",
+        out_specs=[HBM] * 2,
+    )(l0, *latents, grads[0], *moved)
     return (latent_result[None], grad_result[None])
 
 

time: 180 us -> 217 us (1.21)
  the two profiles are of different devices: /device:TPU:104 before, /device:TPU:134 now
where the time goes in v3:
time: 217 us; the launch traced here: 216 us
  starting transfers between devices  75 us (35%)
  Pallas kernels  74.2 us (34%)
  waiting for transfers between devices  65.4 us (30%)
    ppermute x9, waiting for transfers between devices, spread(): return lax.ppermute(value, ('chip', 'core'), pairs)  55 us
    pallas_call x1, Pallas kernels, body(): call(weights_kernel, [((W_ROWS, H), BF16)], [HBM] * 4, [pltpu.VMEM((1, H)...  48.8 us
    ppermute x12, starting transfers between devices, swap(): return lax.ppermute(value, 'core', [(0, 1), (1, 0)])  27.1 us
    ppermute x9, starting transfers between devices, spread(): return lax.ppermute(value, ('chip', 'core'), pairs)  22.5 us
    ppermute x6, starting transfers between devices, onward(): lax.ppermute(value, 'section', [(s, (s + steps) % count) for s in range(c...  19 us
    pallas_call x1, Pallas kernels, body(): call(forward_kernel, [((B, H), BF16), ((B, H), BF16), ((B, H), BF16), ((B...  15.2 us
    ppermute x2, starting transfers between devices, around(): return lax.ppermute(value, ('section', 'core'), pairs)  6.24 us
    ppermute x6, waiting for transfers between devices, onward(): lax.ppermute(value, 'section', [(s, (s + steps) % count) for s in range(c...  5.45 us
  transfers between devices with their start and end apart: 29, of which 13 were waited for; matrix products, arithmetic and copies ran while one was open for 0% of the time, Pallas kernels for 3%

profile of v3, /device:TPU:134, one launch (start us, length us, event | category | flops | bytes accessed | tf_op | source)
XLA Modules:
  0.0 216.5 jit_solution(13794460421534178111)
XLA Ops:
  0.7 48.8 %weights.1.w_own = bf16[1568,512]{1,0:T(8,128)(2,1)} custom-call(bf16[1,512,512]{2,1,0:T(8,128)(2,1)} %w_a.1, bf16[1,512,512]{2,1,0:T(8,128)(2,1)} %w_b.1, bf16[1,512,512]{2,1,0:T(8,128)(2,1)} %w_c.1, f32[1,512]{1,0:T(1,128)} %gain.1), custom_call_target="tpu_custom_call" | custom-call | tf_op jit(solution)/shard_map/weights/pallas_call | solution.py:343
  49.5 2.4 %collective-permute-start.1 = (bf16[1568,512]{1,0:T(8,128)(2,1)}, bf16[1568,512]{1,0:T(8,128)(2,1)S(1)}, u32[]{:S(2)}, u32[]{:S(2)}) collective-permute-start(bf16[1568,512]{1,0:T(8,128)(2,1)} %weights.1.w_own), channel_id=1, source_target_pairs={{0,128},{1,385},{128,256},{129,1},{256,384},{257,129},{384,0},{385... | collective-permute-start | bytes 4816904 | tf_op jit(solution)/shard_map/ppermute | solution.py:332
  53.5 2.1 collective-permute-start
  57.4 4.9 %collective-permute-start.3 = (bf16[256,1152]{1,0:T(8,128)(2,1)S(1)}, bf16[256,1152]{1,0:T(8,128)(2,1)S(1)}, u32[]{:S(2)}, u32[]{:S(2)}) collective-permute-start(bf16[256,1152]{1,0:T(8,128)(2,1)S(1)} %get-tuple-element.38.own), channel_id=1, source_target_pairs={{0,6},{2,8},{4,10},{6,12},{7,1},{8,14},{9,3},{10,16},{11,5},{12,18... | collective-permute-start | bytes 1769480 | tf_op jit(solution)/shard_map/ppermute | solution.py:323
  62.3 2.3 %collective-permute-start.2 = (bf16[256,1152]{1,0:T(8,128)(2,1)S(1)}, bf16[256,1152]{1,0:T(8,128)(2,1)S(1)}, u32[]{:S(2)}, u32[]{:S(2)}) collective-permute-start(bf16[256,1152]{1,0:T(8,128)(2,1)S(1)} %get-tuple-element.38.own), channel_id=1, source_target_pairs={{0,2},{2,4},{3,1},{4,6},{5,3},{6,8},{7,5},{8,10},{9,7},{10,12},{11... | collective-permute-start | bytes 1769480 | tf_op jit(solution)/shard_map/ppermute | solution.py:323
  64.6 3.8 %collective-permute-start.4 = (bf16[256,512]{1,0:T(8,128)(2,1)S(1)}, bf16[256,512]{1,0:T(8,128)(2,1)S(1)}, u32[]{:S(2)}, u32[]{:S(2)}) collective-permute-start(bf16[256,512]{1,0:T(8,128)(2,1)S(1)} %get-tuple-element.40.own), channel_id=1, source_target_pairs={{0,8},{2,10},{4,12},{6,14},{8,16},{9,1},{10,18},{11,3},{12,20},{13... | collective-permute-start | bytes 786440 | tf_op jit(solution)/shard_map/ppermute | solution.py:323
  68.4 5.6 %collective-permute-done.4.m4 = bf16[256,512]{1,0:T(8,128)(2,1)S(1)} collective-permute-done((bf16[256,512]{1,0:T(8,128)(2,1)S(1)}, bf16[256,512]{1,0:T(8,128)(2,1)S(1)}, u32[]{:S(2)}, u32[]{:S(2)}) %collective-permute-start.4) | collective-permute-done | bytes 262176 | tf_op jit(solution)/shard_map/ppermute | solution.py:323
  74.1 2.0 collective-permute-done.3.m3
  76.0 3.3 %collective-permute-done.2.m1 = bf16[256,1152]{1,0:T(8,128)(2,1)S(1)} collective-permute-done((bf16[256,1152]{1,0:T(8,128)(2,1)S(1)}, bf16[256,1152]{1,0:T(8,128)(2,1)S(1)}, u32[]{:S(2)}, u32[]{:S(2)}) %collective-permute-start.2) | collective-permute-done | bytes 589856 | tf_op jit(solution)/shard_map/ppermute | solution.py:323
  79.4 3.8 %collective-permute-start.11 = (bf16[784,512]{1,0:T(8,128)(2,1)S(1)}, bf16[784,512]{1,0:T(8,128)(2,1)S(1)}, u32[]{:S(2)}, u32[]{:S(2)}) collective-permute-start(bf16[784,512]{1,0:T(8,128)(2,1)S(1)} %half.1), channel_id=1, source_target_pairs={{0,128},{1,385},{128,256},{129,1},{256,384},{257,129},{384,0},{385... | collective-permute-start | bytes 2408456 | tf_op jit(solution)/shard_map/ppermute | solution.py:332
  87.1 1.9 collective-permute-start.13
  89.1 4.5 %collective-permute-start.9 = (bf16[256,512]{1,0:T(8,128)(2,1)S(1)}, bf16[256,512]{1,0:T(8,128)(2,1)S(1)}, u32[]{:S(2)}, u32[]{:S(2)}) collective-permute-start(bf16[256,512]{1,0:T(8,128)(2,1)S(1)} %collective-permute-done.4.m4), channel_id=1, source_target_pairs={{0,1},{1,0},{2,3},{3,2},{4,5},{5,4},{6,7},{7,6},{8,9},{9,8},{10,11... | collective-permute-start | bytes 786440 | tf_op jit(solution)/shard_map/ppermute | solution.py:312
  93.6 9.5 %collective-permute-done.13.c1 = bf16[256,512]{1,0:T(8,128)(2,1)S(1)} collective-permute-done((bf16[256,512]{1,0:T(8,128)(2,1)S(1)}, bf16[256,512]{1,0:T(8,128)(2,1)S(1)}, u32[]{:S(2)}, u32[]{:S(2)}) %collective-permute-start.13) | collective-permute-done | bytes 262176 | tf_op jit(solution)/shard_map/ppermute | solution.py:323
  105.0 2.4 %collective-permute-start.12 = (bf16[784,512]{1,0:T(8,128)(2,1)S(1)}, bf16[784,512]{1,0:T(8,128)(2,1)S(1)}, u32[]{:S(2)}, u32[]{:S(2)}) collective-permute-start(bf16[784,512]{1,0:T(8,128)(2,1)S(1)} %collective-permute-done.11.w_mh), channel_id=1, source_target_pairs={{0,1},{1,0},{2,3},{3,2},{4,5},{5,4},{6,7},{7,6},{8,9},{9,8},{10,11... | collective-permute-start | bytes 2408456 | tf_op jit(solution)/shard_map/ppermute | solution.py:312
  109.4 2.4 %collective-permute-start.8 = (bf16[256,1152]{1,0:T(8,128)(2,1)S(1)}, bf16[256,1152]{1,0:T(8,128)(2,1)S(1)}, u32[]{:S(2)}, u32[]{:S(2)}) collective-permute-start(bf16[256,1152]{1,0:T(8,128)(2,1)S(1)} %collective-permute-done.3.m3), channel_id=1, source_target_pairs={{0,1},{1,0},{2,3},{3,2},{4,5},{5,4},{6,7},{7,6},{8,9},{9,8},{10,11... | collective-permute-start | bytes 1769480 | tf_op jit(solution)/shard_map/ppermute | solution.py:312
  111.8 2.1 collective-permute-start.7
  115.7 15.2 %forward.1 = (bf16[128,512]{1,0:T(8,128)(2,1)S(1)}, bf16[128,512]{1,0:T(8,128)(2,1)S(1)}, bf16[128,512]{1,0:T(8,128)(2,1)S(1)}, bf16[128,512]{1,0:T(8,128)(2,1)S...) custom-call(bf16[256,1152]{1,0:T(8,128)(2,1)S(1)} %get-tuple-element, ...), custom_call_target="tpu_custom_call" | custom-call | flops 10737418240 | bytes 20971520 | tf_op jit(solution)/shard_map/forward/pallas_call | solution.py:385
  132.9 9.7 %collective-permute-done.18.r1 = bf16[256,512]{1,0:T(8,128)(2,1)S(1)} collective-permute-done((bf16[256,512]{1,0:T(8,128)(2,1)S(1)}, bf16[256,512]{1,0:T(8,128)(2,1)S(1)}, u32[]{:S(2)}, u32[]{:S(2)}) %collective-permute-start.18) | collective-permute-done | bytes 262176 | tf_op jit(solution)/shard_map/ppermute | solution.py:323
  144.4 2.2 %collective-permute-start.20 = (bf16[256,512]{1,0:T(8,128)(2,1)S(1)}, bf16[256,512]{1,0:T(8,128)(2,1)S(1)}, u32[]{:S(2)}, u32[]{:S(2)}) collective-permute-start(bf16[256,512]{1,0:T(8,128)(2,1)S(1)} %collective-permute-done.18.r1), channel_id=1, source_target_pairs={{0,1},{1,0},{2,3},{3,2},{4,5},{5,4},{6,7},{7,6},{8,9},{9,8},{10,11... | collective-permute-start | bytes 786440 | tf_op jit(solution)/shard_map/ppermute | solution.py:312
  146.6 7.4 %collective-permute-done.19.r2 = bf16[256,512]{1,0:T(8,128)(2,1)S(1)} collective-permute-done((bf16[256,512]{1,0:T(8,128)(2,1)S(1)}, bf16[256,512]{1,0:T(8,128)(2,1)S(1)}, u32[]{:S(2)}, u32[]{:S(2)}) %collective-permute-start.19) | collective-permute-done | bytes 262176 | tf_op jit(solution)/shard_map/ppermute | solution.py:323
  157.5 3.7 %backward_a.1 = (bf16[128,512]{1,0:T(8,128)(2,1)S(1)}, bf16[256,512]{1,0:T(8,128)(2,1)S(1)}, bf16[768,768]{1,0:T(8,128)(2,1)S(1)}, bf16[768,512]{1,0:T(8,128)(2,...) custom-call(bf16[256,512]{1,0:T(8,128)(2,1)S(1)} %get-tuple-element., ...), custom_call_target="tpu_custom_call", output_to_operand_aliasing={{2}: (11, {}), {3}: (12, {}), {4}: (13, {}), {5}: (14, {}),... | custom-call | flops 4026531840 | bytes 7864320 | tf_op jit(solution)/shard_map/backward_a/pallas_call | solution.py:410
  163.1 9.7 %collective-permute-done.22.r1 = bf16[256,512]{1,0:T(8,128)(2,1)S(1)} collective-permute-done((bf16[256,512]{1,0:T(8,128)(2,1)S(1)}, bf16[256,512]{1,0:T(8,128)(2,1)S(1)}, u32[]{:S(2)}, u32[]{:S(2)}) %collective-permute-start.22) | collective-permute-done | bytes 262176 | tf_op jit(solution)/shard_map/ppermute | solution.py:323
  176.6 7.7 %collective-permute-done.23.r2 = bf16[256,512]{1,0:T(8,128)(2,1)S(1)} collective-permute-done((bf16[256,512]{1,0:T(8,128)(2,1)S(1)}, bf16[256,512]{1,0:T(8,128)(2,1)S(1)}, u32[]{:S(2)}, u32[]{:S(2)}) %collective-permute-start.23) | collective-permute-done | bytes 262176 | tf_op jit(solution)/shard_map/ppermute | solution.py:323
  186.3 2.9 %collective-permute-start.15 = (bf16[128,512]{1,0:T(8,128)(2,1)S(1)}, bf16[128,512]{1,0:T(8,128)(2,1)S(1)}, u32[]{:S(2)}, u32[]{:S(2)}) collective-permute-start(bf16[128,512]{1,0:T(8,128)(2,1)S(1)} %get-tuple-element.49), channel_id=1, source_target_pairs={{0,128},{128,256},{256,384},{384,0},{1,129},{129,257},{257,385},{3... | collective-permute-start | bytes 393224 | tf_op jit(solution)/shard_map/ppermute | solution.py:337
  189.2 3.0 %collective-permute-start.16 = (bf16[128,512]{1,0:T(8,128)(2,1)S(1)}, bf16[128,512]{1,0:T(8,128)(2,1)S(1)}, u32[]{:S(2)}, u32[]{:S(2)}) collective-permute-start(bf16[128,512]{1,0:T(8,128)(2,1)S(1)} %get-tuple-element.50), channel_id=1, source_target_pairs={{0,256},{128,384},{256,0},{384,128},{1,257},{129,385},{257,1},{385... | collective-permute-start | bytes 393224 | tf_op jit(solution)/shard_map/ppermute | solution.py:337
  192.3 2.8 %collective-permute-start.17 = (bf16[128,512]{1,0:T(8,128)(2,1)S(1)}, bf16[128,512]{1,0:T(8,128)(2,1)S(1)}, u32[]{:S(2)}, u32[]{:S(2)}) collective-permute-start(bf16[128,512]{1,0:T(8,128)(2,1)S(1)} %get-tuple-element.51), channel_id=1, source_target_pairs={{0,384},{128,0},{256,128},{384,256},{1,385},{129,1},{257,129},{385... | collective-permute-start | bytes 393224 | tf_op jit(solution)/shard_map/ppermute | solution.py:337
  195.1 4.4 %backward_b.1 = (bf16[128,512]{1,0:T(8,128)(2,1)S(1)}, bf16[128,512]{1,0:T(8,128)(2,1)S(1)}, bf16[128,512]{1,0:T(8,128)(2,1)S(1)}, bf16[128,512]{1,0:T(8,128)(2,1)S(1)}) custom-call(bf16[256,512]{1,0:T(8,128)(2,1)S(1)} %get-tuple-element.61.g2_own, bf16[256,512]{1,0:T(8,128)(2,1)S(1)} %collective-permute-done.22.r1, ...), custom_call_target="tpu_custom_call" | custom-call | flops 4697620480 | bytes 9175040 | tf_op jit(solution)/shard_map/backward_b/pallas_call | solution.py:427
  199.6 4.2 %collective-permute-start.26 = (bf16[128,512]{1,0:T(8,128)(2,1)S(1)}, bf16[128,512]{1,0:T(8,128)(2,1)S(1)}, u32[]{:S(2)}, u32[]{:S(2)}) collective-permute-start(bf16[128,512]{1,0:T(8,128)(2,1)S(1)} %get-tuple-element.69), channel_id=1, source_target_pairs={{0,128},{128,256},{256,384},{384,0},{1,129},{129,257},{257,385},{3... | collective-permute-start | bytes 393224 | tf_op jit(solution)/shard_map/ppermute | solution.py:337
  203.8 3.1 %collective-permute-start.27 = (bf16[128,512]{1,0:T(8,128)(2,1)S(1)}, bf16[128,512]{1,0:T(8,128)(2,1)S(1)}, u32[]{:S(2)}, u32[]{:S(2)}) collective-permute-start(bf16[128,512]{1,0:T(8,128)(2,1)S(1)} %get-tuple-element.70), channel_id=1, source_target_pairs={{0,256},{128,384},{256,0},{384,128},{1,257},{129,385},{257,1},{385... | collective-permute-start | bytes 393224 | tf_op jit(solution)/shard_map/ppermute | solution.py:337
  206.9 2.9 %collective-permute-start.28 = (bf16[128,512]{1,0:T(8,128)(2,1)S(1)}, bf16[128,512]{1,0:T(8,128)(2,1)S(1)}, u32[]{:S(2)}, u32[]{:S(2)}) collective-permute-start(bf16[128,512]{1,0:T(8,128)(2,1)S(1)} %get-tuple-element.71), channel_id=1, source_target_pairs={{0,384},{128,0},{256,128},{384,256},{1,385},{129,1},{257,129},{385... | collective-permute-start | bytes 393224 | tf_op jit(solution)/shard_map/ppermute | solution.py:337
  209.8 3.4 %collective-permute-done.27.g2 = bf16[128,512]{1,0:T(8,128)(2,1)S(1)} collective-permute-done((bf16[128,512]{1,0:T(8,128)(2,1)S(1)}, bf16[128,512]{1,0:T(8,128)(2,1)S(1)}, u32[]{:S(2)}, u32[]{:S(2)}) %collective-permute-start.27) | collective-permute-done | bytes 131104 | tf_op jit(solution)/shard_map/ppermute | solution.py:337
  213.2 2.0 collective-permute-done.28.g3
  (44 shorter events, 28.2 us)
Async XLA Ops:
  0.6 51.9 %copy-start.4 = (s32[4]{0:T(128)S(1)}, s32[4]{0:T(128)}, u32[]{:S(2)}) copy-start(s32[4]{0:T(128)} %source.1) | copy-start | bytes 52
  0.6 51.9 %copy-start.3 = (bf16[4,128,128]{2,1,0:T(8,128)(2,1)S(1)}, bf16[4,128,128]{2,1,0:T(8,128)(2,1)}, u32[]{:S(2)}) copy-start(bf16[4,128,128]{2,1,0:T(8,128)(2,1)} %tiles.1) | copy-start | bytes 393220
  49.5 24.6 %collective-permute-start.1 = (bf16[1568,512]{1,0:T(8,128)(2,1)}, bf16[1568,512]{1,0:T(8,128)(2,1)S(1)}, u32[]{:S(2)}, u32[]{:S(2)}) collective-permute-start(bf16[1568,512]{1,0:T(8,128)(2,1)} %weights.1.w_own), channel_id=1, source_target_pairs={{0,128},{1,385},{128,256},{129,1},{256,384},{257,129},{384,0},{385... | collective-permute-start | bytes 4816904 | tf_op jit(solution)/shard_map/ppermute | solution.py:332
  53.5 62.2 %copy-start = (bf16[1568,512]{1,0:T(8,128)(2,1)S(1)}, bf16[1568,512]{1,0:T(8,128)(2,1)}, u32[]{:S(2)}) copy-start(bf16[1568,512]{1,0:T(8,128)(2,1)} %weights.1.w_own) | copy-start | bytes 4816900
  53.5 3.8 %collective-permute-start = (bf16[128,1664]{1,0:T(8,128)(2,1)S(1)}, bf16[128,1664]{1,0:T(8,128)(2,1)S(1)}, u32[]{:S(2)}, u32[]{:S(2)}) collective-permute-start(bf16[128,1664]{1,0:T(8,128)(2,1)S(1)} %prepare.1.own), channel_id=1, source_target_pairs={{0,1},{1,0},{2,3},{3,2},{4,5},{5,4},{6,7},{7,6},{8,9},{9,8},{10,11... | collective-permute-start | bytes 1277960 | tf_op jit(solution)/shard_map/ppermute | solution.py:312
  57.4 18.7 %collective-permute-start.3 = (bf16[256,1152]{1,0:T(8,128)(2,1)S(1)}, bf16[256,1152]{1,0:T(8,128)(2,1)S(1)}, u32[]{:S(2)}, u32[]{:S(2)}) collective-permute-start(bf16[256,1152]{1,0:T(8,128)(2,1)S(1)} %get-tuple-element.38.own), channel_id=1, source_target_pairs={{0,6},{2,8},{4,10},{6,12},{7,1},{8,14},{9,3},{10,16},{11,5},{12,18... | collective-permute-start | bytes 1769480 | tf_op jit(solution)/shard_map/ppermute | solution.py:323
  62.3 17.1 %collective-permute-start.2 = (bf16[256,1152]{1,0:T(8,128)(2,1)S(1)}, bf16[256,1152]{1,0:T(8,128)(2,1)S(1)}, u32[]{:S(2)}, u32[]{:S(2)}) collective-permute-start(bf16[256,1152]{1,0:T(8,128)(2,1)S(1)} %get-tuple-element.38.own), channel_id=1, source_target_pairs={{0,2},{2,4},{3,1},{4,6},{5,3},{6,8},{7,5},{8,10},{9,7},{10,12},{11... | collective-permute-start | bytes 1769480 | tf_op jit(solution)/shard_map/ppermute | solution.py:323
  64.6 9.5 %collective-permute-start.4 = (bf16[256,512]{1,0:T(8,128)(2,1)S(1)}, bf16[256,512]{1,0:T(8,128)(2,1)S(1)}, u32[]{:S(2)}, u32[]{:S(2)}) collective-permute-start(bf16[256,512]{1,0:T(8,128)(2,1)S(1)} %get-tuple-element.40.own), channel_id=1, source_target_pairs={{0,8},{2,10},{4,12},{6,14},{8,16},{9,1},{10,18},{11,3},{12,20},{13... | collective-permute-start | bytes 786440 | tf_op jit(solution)/shard_map/ppermute | solution.py:323
  79.4 25.6 %collective-permute-start.11 = (bf16[784,512]{1,0:T(8,128)(2,1)S(1)}, bf16[784,512]{1,0:T(8,128)(2,1)S(1)}, u32[]{:S(2)}, u32[]{:S(2)}) collective-permute-start(bf16[784,512]{1,0:T(8,128)(2,1)S(1)} %half.1), channel_id=1, source_target_pairs={{0,128},{1,385},{128,256},{129,1},{256,384},{257,129},{384,0},{385... | collective-permute-start | bytes 2408456 | tf_op jit(solution)/shard_map/ppermute | solution.py:332
  83.3 32.5 %collective-permute-start.10 = (bf16[1568,512]{1,0:T(8,128)(2,1)S(1)}, bf16[1568,512]{1,0:T(8,128)(2,1)S(1)}, u32[]{:S(2)}, u32[]{:S(2)}) collective-permute-start(bf16[1568,512]{1,0:T(8,128)(2,1)S(1)} %collective-permute-done.1.weights.w_m), channel_id=1, source_target_pairs={{0,1},{1,0},{2,3},{3,2},{4,5},{5,4},{6,7},{7,6},{8,9},{9,8},{10,11... | collective-permute-start | bytes 4816904 | tf_op jit(solution)/shard_map/ppermute | solution.py:312
  85.2 22.3 %collective-permute-start.5 = (bf16[256,1152]{1,0:T(8,128)(2,1)S(1)}, bf16[256,1152]{1,0:T(8,128)(2,1)S(1)}, u32[]{:S(2)}, u32[]{:S(2)}) collective-permute-start(bf16[256,1152]{1,0:T(8,128)(2,1)S(1)} %collective-permute-done.2.m1), channel_id=1, source_target_pairs={{0,2},{2,4},{3,1},{4,6},{5,3},{6,8},{7,5},{8,10},{9,7},{10,12},{11... | collective-permute-start | bytes 1769480 | tf_op jit(solution)/shard_map/ppermute | solution.py:323
  87.1 16.0 %collective-permute-start.13 = (bf16[256,512]{1,0:T(8,128)(2,1)S(1)}, bf16[256,512]{1,0:T(8,128)(2,1)S(1)}, u32[]{:S(2)}, u32[]{:S(2)}) collective-permute-start(bf16[256,512]{1,0:T(8,128)(2,1)S(1)} %get-tuple-element.47.cotangent.own), channel_id=1, source_target_pairs={{0,2},{2,4},{3,1},{4,6},{5,3},{6,8},{7,5},{8,10},{9,7},{10,12},{11... | collective-permute-start | bytes 786440 | tf_op jit(solution)/shard_map/ppermute | solution.py:323
  89.1 20.3 %collective-permute-start.9 = (bf16[256,512]{1,0:T(8,128)(2,1)S(1)}, bf16[256,512]{1,0:T(8,128)(2,1)S(1)}, u32[]{:S(2)}, u32[]{:S(2)}) collective-permute-start(bf16[256,512]{1,0:T(8,128)(2,1)S(1)} %collective-permute-done.4.m4), channel_id=1, source_target_pairs={{0,1},{1,0},{2,3},{3,2},{4,5},{5,4},{6,7},{7,6},{8,9},{9,8},{10,11... | collective-permute-start | bytes 786440 | tf_op jit(solution)/shard_map/ppermute | solution.py:312
  103.1 8.7 %collective-permute-start.14 = (bf16[256,512]{1,0:T(8,128)(2,1)S(1)}, bf16[256,512]{1,0:T(8,128)(2,1)S(1)}, u32[]{:S(2)}, u32[]{:S(2)}) collective-permute-start(bf16[256,512]{1,0:T(8,128)(2,1)S(1)} %collective-permute-done.13.c1), channel_id=1, source_target_pairs={{0,1},{1,0},{2,3},{3,2},{4,5},{5,4},{6,7},{7,6},{8,9},{9,8},{10,11... | collective-permute-start | bytes 786440 | tf_op jit(solution)/shard_map/ppermute | solution.py:312
  105.0 10.7 %collective-permute-start.12 = (bf16[784,512]{1,0:T(8,128)(2,1)S(1)}, bf16[784,512]{1,0:T(8,128)(2,1)S(1)}, u32[]{:S(2)}, u32[]{:S(2)}) collective-permute-start(bf16[784,512]{1,0:T(8,128)(2,1)S(1)} %collective-permute-done.11.w_mh), channel_id=1, source_target_pairs={{0,1},{1,0},{2,3},{3,2},{4,5},{5,4},{6,7},{7,6},{8,9},{9,8},{10,11... | collective-permute-start | bytes 2408456 | tf_op jit(solution)/shard_map/ppermute | solution.py:312
  107.5 6.5 %collective-permute-start.6 = (bf16[256,1152]{1,0:T(8,128)(2,1)S(1)}, bf16[256,1152]{1,0:T(8,128)(2,1)S(1)}, u32[]{:S(2)}, u32[]{:S(2)}) collective-permute-start(bf16[256,1152]{1,0:T(8,128)(2,1)S(1)} %collective-permute-done.2.m1), channel_id=1, source_target_pairs={{0,1},{1,0},{2,3},{3,2},{4,5},{5,4},{6,7},{7,6},{8,9},{9,8},{10,11... | collective-permute-start | bytes 1769480 | tf_op jit(solution)/shard_map/ppermute | solution.py:312
  109.4 4.5 %collective-permute-start.8 = (bf16[256,1152]{1,0:T(8,128)(2,1)S(1)}, bf16[256,1152]{1,0:T(8,128)(2,1)S(1)}, u32[]{:S(2)}, u32[]{:S(2)}) collective-permute-start(bf16[256,1152]{1,0:T(8,128)(2,1)S(1)} %collective-permute-done.3.m3), channel_id=1, source_target_pairs={{0,1},{1,0},{2,3},{3,2},{4,5},{5,4},{6,7},{7,6},{8,9},{9,8},{10,11... | collective-permute-start | bytes 1769480 | tf_op jit(solution)/shard_map/ppermute | solution.py:312
  111.8 3.9 %collective-permute-start.7 = (bf16[256,1152]{1,0:T(8,128)(2,1)S(1)}, bf16[256,1152]{1,0:T(8,128)(2,1)S(1)}, u32[]{:S(2)}, u32[]{:S(2)}) collective-permute-start(bf16[256,1152]{1,0:T(8,128)(2,1)S(1)} %collective-permute-done.5.m2), channel_id=1, source_target_pairs={{0,1},{1,0},{2,3},{3,2},{4,5},{5,4},{6,7},{7,6},{8,9},{9,8},{10,11... | collective-permute-start | bytes 1769480 | tf_op jit(solution)/shard_map/ppermute | solution.py:312
  130.9 11.6 %collective-permute-start.18 = (bf16[256,512]{1,0:T(8,128)(2,1)S(1)}, bf16[256,512]{1,0:T(8,128)(2,1)S(1)}, u32[]{:S(2)}, u32[]{:S(2)}) collective-permute-start(bf16[256,512]{1,0:T(8,128)(2,1)S(1)} %get-tuple-element.52.grad_pre), channel_id=1, source_target_pairs={{0,2},{2,4},{3,1},{4,6},{5,3},{6,8},{7,5},{8,10},{9,7},{10,12},{11... | collective-permute-start | bytes 786440 | tf_op jit(solution)/shard_map/ppermute | solution.py:323
  142.5 11.6 %collective-permute-start.19 = (bf16[256,512]{1,0:T(8,128)(2,1)S(1)}, bf16[256,512]{1,0:T(8,128)(2,1)S(1)}, u32[]{:S(2)}, u32[]{:S(2)}) collective-permute-start(bf16[256,512]{1,0:T(8,128)(2,1)S(1)} %collective-permute-done.18.r1), channel_id=1, source_target_pairs={{0,2},{2,4},{3,1},{4,6},{5,3},{6,8},{7,5},{8,10},{9,7},{10,12},{11... | collective-permute-start | bytes 786440 | tf_op jit(solution)/shard_map/ppermute | solution.py:323
  144.4 11.6 %collective-permute-start.20 = (bf16[256,512]{1,0:T(8,128)(2,1)S(1)}, bf16[256,512]{1,0:T(8,128)(2,1)S(1)}, u32[]{:S(2)}, u32[]{:S(2)}) collective-permute-start(bf16[256,512]{1,0:T(8,128)(2,1)S(1)} %collective-permute-done.18.r1), channel_id=1, source_target_pairs={{0,1},{1,0},{2,3},{3,2},{4,5},{5,4},{6,7},{7,6},{8,9},{9,8},{10,11... | collective-permute-start | bytes 786440 | tf_op jit(solution)/shard_map/ppermute | solution.py:312
  154.1 3.4 %collective-permute-start.21 = (bf16[256,512]{1,0:T(8,128)(2,1)S(1)}, bf16[256,512]{1,0:T(8,128)(2,1)S(1)}, u32[]{:S(2)}, u32[]{:S(2)}) collective-permute-start(bf16[256,512]{1,0:T(8,128)(2,1)S(1)} %collective-permute-done.19.r2), channel_id=1, source_target_pairs={{0,1},{1,0},{2,3},{3,2},{4,5},{5,4},{6,7},{7,6},{8,9},{9,8},{10,11... | collective-permute-start | bytes 786440 | tf_op jit(solution)/shard_map/ppermute | solution.py:312
  161.2 11.6 %collective-permute-start.22 = (bf16[256,512]{1,0:T(8,128)(2,1)S(1)}, bf16[256,512]{1,0:T(8,128)(2,1)S(1)}, u32[]{:S(2)}, u32[]{:S(2)}) collective-permute-start(bf16[256,512]{1,0:T(8,128)(2,1)S(1)} %get-tuple-element.61.g2_own), channel_id=1, source_target_pairs={{0,2},{2,4},{3,1},{4,6},{5,3},{6,8},{7,5},{8,10},{9,7},{10,12},{11... | collective-permute-start | bytes 786440 | tf_op jit(solution)/shard_map/ppermute | solution.py:323
  172.8 11.6 %collective-permute-start.23 = (bf16[256,512]{1,0:T(8,128)(2,1)S(1)}, bf16[256,512]{1,0:T(8,128)(2,1)S(1)}, u32[]{:S(2)}, u32[]{:S(2)}) collective-permute-start(bf16[256,512]{1,0:T(8,128)(2,1)S(1)} %collective-permute-done.22.r1), channel_id=1, source_target_pairs={{0,2},{2,4},{3,1},{4,6},{5,3},{6,8},{7,5},{8,10},{9,7},{10,12},{11... | collective-permute-start | bytes 786440 | tf_op jit(solution)/shard_map/ppermute | solution.py:323
  174.7 20.4 %collective-permute-start.24 = (bf16[256,512]{1,0:T(8,128)(2,1)S(1)}, bf16[256,512]{1,0:T(8,128)(2,1)S(1)}, u32[]{:S(2)}, u32[]{:S(2)}) collective-permute-start(bf16[256,512]{1,0:T(8,128)(2,1)S(1)} %collective-permute-done.22.r1), channel_id=1, source_target_pairs={{0,1},{1,0},{2,3},{3,2},{4,5},{5,4},{6,7},{7,6},{8,9},{9,8},{10,11... | collective-permute-start | bytes 786440 | tf_op jit(solution)/shard_map/ppermute | solution.py:312
  184.3 10.8 %collective-permute-start.25 = (bf16[256,512]{1,0:T(8,128)(2,1)S(1)}, bf16[256,512]{1,0:T(8,128)(2,1)S(1)}, u32[]{:S(2)}, u32[]{:S(2)}) collective-permute-start(bf16[256,512]{1,0:T(8,128)(2,1)S(1)} %collective-permute-done.23.r2), channel_id=1, source_target_pairs={{0,1},{1,0},{2,3},{3,2},{4,5},{5,4},{6,7},{7,6},{8,9},{9,8},{10,11... | collective-permute-start | bytes 786440 | tf_op jit(solution)/shard_map/ppermute | solution.py:312
  186.3 20.6 %collective-permute-start.15 = (bf16[128,512]{1,0:T(8,128)(2,1)S(1)}, bf16[128,512]{1,0:T(8,128)(2,1)S(1)}, u32[]{:S(2)}, u32[]{:S(2)}) collective-permute-start(bf16[128,512]{1,0:T(8,128)(2,1)S(1)} %get-tuple-element.49), channel_id=1, source_target_pairs={{0,128},{128,256},{256,384},{384,0},{1,129},{129,257},{257,385},{3... | collective-permute-start | bytes 393224 | tf_op jit(solution)/shard_map/ppermute | solution.py:337
  189.2 20.6 %collective-permute-start.16 = (bf16[128,512]{1,0:T(8,128)(2,1)S(1)}, bf16[128,512]{1,0:T(8,128)(2,1)S(1)}, u32[]{:S(2)}, u32[]{:S(2)}) collective-permute-start(bf16[128,512]{1,0:T(8,128)(2,1)S(1)} %get-tuple-element.50), channel_id=1, source_target_pairs={{0,256},{128,384},{256,0},{384,128},{1,257},{129,385},{257,1},{385... | collective-permute-start | bytes 393224 | tf_op jit(solution)/shard_map/ppermute | solution.py:337
  192.3 17.6 %collective-permute-start.17 = (bf16[128,512]{1,0:T(8,128)(2,1)S(1)}, bf16[128,512]{1,0:T(8,128)(2,1)S(1)}, u32[]{:S(2)}, u32[]{:S(2)}) collective-permute-start(bf16[128,512]{1,0:T(8,128)(2,1)S(1)} %get-tuple-element.51), channel_id=1, source_target_pairs={{0,384},{128,0},{256,128},{384,256},{1,385},{129,1},{257,129},{385... | collective-permute-start | bytes 393224 | tf_op jit(solution)/shard_map/ppermute | solution.py:337
  199.6 10.3 %collective-permute-start.26 = (bf16[128,512]{1,0:T(8,128)(2,1)S(1)}, bf16[128,512]{1,0:T(8,128)(2,1)S(1)}, u32[]{:S(2)}, u32[]{:S(2)}) collective-permute-start(bf16[128,512]{1,0:T(8,128)(2,1)S(1)} %get-tuple-element.69), channel_id=1, source_target_pairs={{0,128},{128,256},{256,384},{384,0},{1,129},{129,257},{257,385},{3... | collective-permute-start | bytes 393224 | tf_op jit(solution)/shard_map/ppermute | solution.py:337
  203.8 9.5 %collective-permute-start.27 = (bf16[128,512]{1,0:T(8,128)(2,1)S(1)}, bf16[128,512]{1,0:T(8,128)(2,1)S(1)}, u32[]{:S(2)}, u32[]{:S(2)}) collective-permute-start(bf16[128,512]{1,0:T(8,128)(2,1)S(1)} %get-tuple-element.70), channel_id=1, source_target_pairs={{0,256},{128,384},{256,0},{384,128},{1,257},{129,385},{257,1},{385... | collective-permute-start | bytes 393224 | tf_op jit(solution)/shard_map/ppermute | solution.py:337
  206.9 8.4 %collective-permute-start.28 = (bf16[128,512]{1,0:T(8,128)(2,1)S(1)}, bf16[128,512]{1,0:T(8,128)(2,1)S(1)}, u32[]{:S(2)}, u32[]{:S(2)}) collective-permute-start(bf16[128,512]{1,0:T(8,128)(2,1)S(1)} %get-tuple-element.71), channel_id=1, source_target_pairs={{0,384},{128,0},{256,128},{384,256},{1,385},{129,1},{257,129},{385... | collective-permute-start | bytes 393224 | tf_op jit(solution)/shard_map/ppermute | solution.py:337
  (2 other events, 103.8 us)

commit v4 on v3

--- a/solution.py
+++ b/solution.py
@@ -15,6 +15,8 @@
 BAND = 3 * PAIR
 SENT = 5 * B
 WIDE = H + SENT
+AT3 = WIDE + H
+AT4 = AT3 + WIDE
 REACH = 4
 W_ROWS = 3 * H + 32
 W_HALF = W_ROWS // 2
@@ -22,7 +24,7 @@
 VMEM = pl.BlockSpec(memory_space=pltpu.VMEM)
 HBM = pl.BlockSpec(memory_space=pltpu.HBM)
 ANY = pl.BlockSpec(memory_space=pl.ANY)
-FWD_MIB, BWD_MIB = 24, 12
+FWD_MIB, BWD_MIB, WGT_MIB = 24, 12, 58
 
 
 def rows(index, size=PAIR):
@@ -62,7 +64,7 @@
     )
 
 
-def weights_kernel(w_a, w_b, w_c, gain, weights, gain_here, terms, sems):
+def weights_kernel(w_a, w_b, w_c, gain, weights, gain_here, sems):
     copies = [
         pltpu.make_async_copy(ref.at[0], weights.at[rows(which, H)], sems.at[which])
         for which, ref in enumerate((w_a, w_b, w_c))
@@ -79,12 +81,9 @@
     low = rest - mid
     row = lax.broadcasted_iota(jnp.int32, (32, H), 0)
     held = jnp.where(row == 0, high, jnp.where(row == 1, mid, jnp.where(row == 2, low, 0.0)))
-    terms[...] = held.astype(BF16)
-    last = pltpu.make_async_copy(terms, weights.at[pl.ds(3 * H, 32)], sems.at[4])
-    last.start()
+    weights[3 * H : 3 * H + 32, :] = held.astype(BF16)
     for copy in copies:
         copy.wait()
-    last.wait()
 
 
 def half_kernel(weights, half):
@@ -119,12 +118,19 @@
     own[:, WIDE:] = slope[...]
 
 
-def pack_kernel(own, partner, near, value, slope):
+def pack_kernel(own, partner, first, near, value):
     core = lax.axis_index("core")
     for ref, held in ((own, core), (partner, 1 - core)):
+        first[rows(held, B), :] = ref[...]
         near[rows(held, B), :] = ref[:, 0:WIDE]
         value[rows(held, B), :] = ref[:, 0:H]
-        slope[rows(held, B), :] = ref[:, WIDE:]
+
+
+def join_kernel(m1, m3, m4, joined, near):
+    joined[:, 0:AT3] = m1[...]
+    joined[:, AT3:AT4] = m3[...]
+    joined[:, AT4:] = m4[...]
+    near[...] = m1[:, 0:WIDE]
 
 
 def layer_gain(weights, layer):
@@ -143,7 +149,7 @@
 
 
 def forward_kernel(
-    own, cotangent, m1, m2, m3, m4, t1, t2, t3, t4, w_own, w_m, w_t, w_mh, w_th, _,
+    own, m1, m2, m3, m4, joined, t2, w_own, w_m, w_t, w_mh, w_th,
     l0, l1, l2, l3, grad_pre, turned, v3_out, v2_out, v1_out, f2_out, f1_out, f0_out, weights,
     latents, v_a, v_b, band, unit, source,
 ):
@@ -165,6 +171,7 @@
             rim = (1 - k) * SENT
             band[row, rim : rim + B] = jnp.zeros((B, B), BF16)
 
+    t1, t3, t4 = joined.at[:, 0:AT3], joined.at[:, AT3:AT4], joined.at[:, AT4:]
     v_a[rows(REACH), :] = own[:, 0:H]
     put_band(REACH - 1, own)
     for step, (m, t) in enumerate(((m1, t1), (m2, t2), (m3, t3), (m4, t4)), start=1):
@@ -198,7 +205,7 @@
             if abs(j - REACH) <= reach:
                 factor = sigma * (1.0 + pre * (1.0 - sigma))
                 if layer == 3:
-                    incoming = dot_t(cotangent[...], weight(weights, 3, 2))
+                    incoming = dot_t(own[:, WIDE:], weight(weights, 3, 2))
                     grad_pre[...] = (incoming * factor).astype(BF16)
                 else:
                     out = (f0_out, f1_out, f2_out)[layer]
@@ -253,12 +260,12 @@
 
 
 def backward_a_kernel(
-    grad_pre, r1, r2, o1, o2, own, c1, d1, v3, v2, f2, turned, v1, f1, f0, weights,
+    grad_pre, r1, r2, o1, o2, own, m1, t1, v3, v2, f2, turned, v1, f1, f0, weights,
     g3_out, g2_out, kept_turned, kept_v1, kept_f1, kept_f0, kept_weights, held, cot, g3, gp2,
 ):
     core = lax.axis_index("core")
     place(held, grad_pre, ((r1, o1), (r2, o2)), core)
-    place(cot, own, ((c1, d1),), core)
+    place(cot, own.at[:, WIDE:], ((m1.at[:, WIDE:], t1.at[:, WIDE:AT3]),), core)
     for j in range(3):
         g3[rows(j), :] = grad_pair(
             cot[rows(j), :], held[rows(j + 1), :], held[j * PAIR : j * PAIR + BAND, :],
@@ -289,7 +296,7 @@
     grads[3] = g3_mine[...]
     grads[2] = g2_own[rows(core, B), :]
     grads[1] = g1[mine, :]
-    g0 = grad_pair(g1[rows(1), :], gp0[rows(1), :], gp0[...], turned[rows(1), :], own[...], weights, 0)
+    g0 = grad_pair(g1[rows(1), :], gp0[rows(1), :], gp0[...], turned[rows(1), :], own[:, 0:H], weights, 0)
     g1[rows(1), :] = g0
     grads[0] = g1[mine, :]
     send_pieces(grads, (p0, p1, p2, p3), lax.axis_index("section"))
@@ -344,10 +351,9 @@
         weights_kernel,
         [((W_ROWS, H), BF16)],
         [HBM] * 4,
-        [pltpu.VMEM((1, H), F32), pltpu.VMEM((32, H), BF16), pltpu.SemaphoreType.DMA((5,))],
-        56,
+        [pltpu.VMEM((1, H), F32), pltpu.SemaphoreType.DMA((4,))],
+        WGT_MIB,
         "weights",
-        out_specs=[HBM],
     )(w_a, w_b, w_c, gain)
     w_m = around(w_own)
     (own,) = call(
@@ -362,24 +368,30 @@
         4,
         "prepare",
     )(pair_source, live_pairs, latent, cotangent, tiles)
-    near, value, slope = call(
+    first, near, value = call(
         pack_kernel,
-        [((PAIR, WIDE), BF16), ((PAIR, H), BF16), ((PAIR, H), BF16)],
+        [((PAIR, AT3), BF16), ((PAIR, WIDE), BF16), ((PAIR, H), BF16)],
         [VMEM] * 2,
         [],
         4,
         "pack",
     )(own, swap(own))
-    m1, m3, m4 = spread(near, 1), spread(near, 3), spread(value, 4)
+    m1, m3, m4 = spread(first, 1), spread(near, 3), spread(value, 4)
+    joined, near = call(
+        join_kernel,
+        [((PAIR, AT4 + H), BF16), ((PAIR, WIDE), BF16)],
+        [VMEM] * 3,
+        [],
+        4,
+        "join",
+    )(m1, m3, m4)
     arrived, m4 = lax.optimization_barrier((w_m, m4))
     (w_half,) = call(half_kernel, [((W_HALF, H), BF16)], [VMEM], [], 4, "half")(arrived)
     w_mh = around(w_half)
-    m2 = spread(m1, 1)
-    w_m, m1, m3, m4, after = lax.optimization_barrier((w_m, m1, m3, m4, slope))
-    c1 = spread(after, 1)
-    d1 = swap(c1)
-    w_t, w_th = swap(w_m), swap(w_mh)
-    t1, t2, t3, t4 = swap(m1), swap(m2), swap(m3), swap(m4)
+    m2 = spread(near, 1)
+    w_m, joined = lax.optimization_barrier((w_m, joined))
+    joined, w_t = swap(joined), swap(w_m)
+    t2, w_th = swap(m2), swap(w_mh)
 
     span = 2 * REACH + 1
     l0, l1, l2, l3, grad_pre, turned, v3, v2, v1, f2, f1, f0, weights = call(
@@ -391,7 +403,7 @@
             ((3 * PAIR, H), BF16), ((5 * PAIR, H), BF16), ((3 * PAIR, H), BF16),
             ((4 * W_ROWS, H), BF16),
         ],
-        [VMEM] * 15 + [ANY],
+        [VMEM] * 12,
         [
             pltpu.VMEM((4, B, H), BF16),
             pltpu.VMEM((span * PAIR, H), BF16), pltpu.VMEM((span * PAIR, H), BF16),
@@ -401,11 +413,11 @@
         FWD_MIB,
         "forward",
         units=160,
-    )(near, slope, m1, m2, m3, m4, t1, t2, t3, t4, w_own, w_m, w_t, w_mh, w_th, d1)
-
-    latents = [onward(l1, 1), onward(l2, 2), onward(l3, 3)]
+    )(first, m1, m2, m3, m4, joined, t2, w_own, w_m, w_t, w_mh, w_th)
+
     r1 = spread(grad_pre, 1)
-    r2 = spread(r1, 1)
+    r2 = spread(grad_pre, 2)
+    l2, r2 = lax.optimization_barrier((onward(l2, 2), r2))
     kept = [turned, v1, f1, f0, weights]
     g3, g2, turned, v1, f1, f0, weights = call(
         backward_a_kernel,
@@ -420,10 +432,11 @@
         out_specs=[VMEM] * 2 + [ANY] * len(kept),
         aliases={11 + i: 2 + i for i in range(len(kept))},
         units=60,
-    )(grad_pre, r1, r2, swap(r1), swap(r2), slope, c1, d1, v3, v2, f2, *kept)
+    )(grad_pre, r1, r2, swap(r1), swap(r2), first, m1, joined, v3, v2, f2, *kept)
 
     r1 = spread(g2, 1)
-    r2 = spread(r1, 1)
+    r2 = spread(g2, 2)
+    l1, l3, r2 = lax.optimization_barrier((onward(l1, 1), onward(l3, 3), r2))
     grads = call(
         backward_b_kernel,
         [((B, H), BF16)] * 4,
@@ -436,7 +449,7 @@
         BWD_MIB,
         "backward_b",
         units=70,
-    )(g2, r1, r2, swap(r1), swap(r2), g3, turned, v1, value, f1, f0, weights)
+    )(g2, r1, r2, swap(r1), swap(r2), g3, turned, v1, first, f1, f0, weights)
 
     moved = [onward(piece, step) for step, piece in enumerate(grads) if step]
     latent_result, grad_result = call(
@@ -447,7 +460,7 @@
         4,
         "collect",
         out_specs=[HBM] * 2,
-    )(l0, *latents, grads[0], *moved)
+    )(l0, l1, l2, l3, grads[0], *moved)
     return (latent_result[None], grad_result[None])
 
 

time: 217 us -> 150 us (0.69)
  the two profiles are of different devices: /device:TPU:134 before, /device:TPU:80 now
where the time goes in v4:
time: 150 us
  starting transfers between devices  87.3 us (58%)
  waiting for transfers between devices  32.1 us (21%)
  Pallas kernels  28.3 us (19%)
  between operations  1.84 us (1%)
    ppermute x8, starting transfers between devices, spread(): return lax.ppermute(value, ('chip', 'core'), pairs)  39.3 us
    ppermute x6, starting transfers between devices, onward(): lax.ppermute(value, 'section', [(s, (s + steps) % count) for s in range(c...  21.9 us
    ppermute x9, starting transfers between devices, swap(): return lax.ppermute(value, 'core', [(0, 1), (1, 0)])  19.8 us
    pallas_call x1, Pallas kernels, body(): call(forward_kernel, [((B, H), BF16), ((B, H), BF16), ((B, H), BF16), ((B...  15.2 us
    ppermute x6, waiting for transfers between devices, onward(): lax.ppermute(value, 'section', [(s, (s + steps) % count) for s in range(c...  12.1 us
    ppermute x8, waiting for transfers between devices, spread(): return lax.ppermute(value, ('chip', 'core'), pairs)  9.92 us
    ppermute x2, starting transfers between devices, around(): return lax.ppermute(value, ('section', 'core'), pairs)  6.35 us
    ppermute x9, waiting for transfers between devices, swap(): return lax.ppermute(value, 'core', [(0, 1), (1, 0)])  5.44 us
  transfers between devices with their start and end apart: 25, of which 13 were waited for; matrix products, arithmetic and copies ran while one was open for 0% of the time, Pallas kernels for 1%

profile of v4, /device:TPU:80, one launch (start us, length us, event | category | flops | bytes accessed | tf_op | source)
XLA Modules:
  0.0 149.5 jit_solution(6283283829167917068)
XLA Ops:
  0.7 2.7 %weights.1.w_own = bf16[1568,512]{1,0:T(8,128)(2,1)} custom-call(bf16[1,512,512]{2,1,0:T(8,128)(2,1)} %w_a.1, bf16[1,512,512]{2,1,0:T(8,128)(2,1)} %w_b.1, bf16[1,512,512]{2,1,0:T(8,128)(2,1)} %w_c.1, f32[1,512]{1,0:T(1,128)} %gain.1), custom_call_target="tpu_custom_call" | custom-call | tf_op jit(solution)/shard_map/weights/pallas_call | solution.py:350
  3.4 3.4 %collective-permute-start.5 = (bf16[1568,512]{1,0:T(8,128)(2,1)}, bf16[1568,512]{1,0:T(8,128)(2,1)S(1)}, u32[]{:S(2)}, u32[]{:S(2)}) collective-permute-start(bf16[1568,512]{1,0:T(8,128)(2,1)} %weights.1.w_own), channel_id=1, source_target_pairs={{0,128},{1,385},{128,256},{129,1},{256,384},{257,129},{384,0},{385... | collective-permute-start | bytes 4816904 | tf_op jit(solution)/shard_map/ppermute | solution.py:339
  8.4 2.7 %collective-permute-start = (bf16[128,1664]{1,0:T(8,128)(2,1)S(1)}, bf16[128,1664]{1,0:T(8,128)(2,1)S(1)}, u32[]{:S(2)}, u32[]{:S(2)}) collective-permute-start(bf16[128,1664]{1,0:T(8,128)(2,1)S(1)} %prepare.1.own), channel_id=1, source_target_pairs={{0,1},{1,0},{2,3},{3,2},{4,5},{5,4},{6,7},{7,6},{8,9},{9,8},{10,11... | collective-permute-start | bytes 1277960 | tf_op jit(solution)/shard_map/ppermute | solution.py:319
  12.6 3.2 %collective-permute-start.1 = (bf16[256,1664]{1,0:T(8,128)(2,1)S(1)}, bf16[256,1664]{1,0:T(8,128)(2,1)S(1)}, u32[]{:S(2)}, u32[]{:S(2)}) collective-permute-start(bf16[256,1664]{1,0:T(8,128)(2,1)S(1)} %get-tuple-element.42.own), channel_id=1, source_target_pairs={{0,2},{2,4},{3,1},{4,6},{5,3},{6,8},{7,5},{8,10},{9,7},{10,12},{11... | collective-permute-start | bytes 2555912 | tf_op jit(solution)/shard_map/ppermute | solution.py:330
  15.8 4.0 %collective-permute-start.2 = (bf16[256,1152]{1,0:T(8,128)(2,1)S(1)}, bf16[256,1152]{1,0:T(8,128)(2,1)S(1)}, u32[]{:S(2)}, u32[]{:S(2)}) collective-permute-start(bf16[256,1152]{1,0:T(8,128)(2,1)S(1)} %get-tuple-element.43), channel_id=1, source_target_pairs={{0,6},{2,8},{4,10},{6,12},{7,1},{8,14},{9,3},{10,16},{11,5},{12,18... | collective-permute-start | bytes 1769480 | tf_op jit(solution)/shard_map/ppermute | solution.py:330
  19.9 5.0 %collective-permute-start.3 = (bf16[256,512]{1,0:T(8,128)(2,1)S(1)}, bf16[256,512]{1,0:T(8,128)(2,1)S(1)}, u32[]{:S(2)}, u32[]{:S(2)}) collective-permute-start(bf16[256,512]{1,0:T(8,128)(2,1)S(1)} %get-tuple-element.44), channel_id=1, source_target_pairs={{0,8},{2,10},{4,12},{6,14},{8,16},{9,1},{10,18},{11,3},{12,20},{13... | collective-permute-start | bytes 786440 | tf_op jit(solution)/shard_map/ppermute | solution.py:330
  24.9 5.8 %collective-permute-done.3.m4 = bf16[256,512]{1,0:T(8,128)(2,1)S(1)} collective-permute-done((bf16[256,512]{1,0:T(8,128)(2,1)S(1)}, bf16[256,512]{1,0:T(8,128)(2,1)S(1)}, u32[]{:S(2)}, u32[]{:S(2)}) %collective-permute-start.3) | collective-permute-done | bytes 262176 | tf_op jit(solution)/shard_map/ppermute | solution.py:330
  30.7 3.3 %collective-permute-done.2.m3 = bf16[256,1152]{1,0:T(8,128)(2,1)S(1)} collective-permute-done((bf16[256,1152]{1,0:T(8,128)(2,1)S(1)}, bf16[256,1152]{1,0:T(8,128)(2,1)S(1)}, u32[]{:S(2)}, u32[]{:S(2)}) %collective-permute-start.2) | collective-permute-done | bytes 589856 | tf_op jit(solution)/shard_map/ppermute | solution.py:330
  34.2 2.1 %collective-permute-start.6 = (bf16[256,3328]{1,0:T(8,128)(2,1)S(1)}, bf16[256,3328]{1,0:T(8,128)(2,1)S(1)}, u32[]{:S(2)}, u32[]{:S(2)}) collective-permute-start(bf16[256,3328]{1,0:T(8,128)(2,1)S(1)} %get-tuple-element.48), channel_id=1, source_target_pairs={{0,1},{1,0},{2,3},{3,2},{4,5},{5,4},{6,7},{7,6},{8,9},{9,8},{10,11... | collective-permute-start | bytes 5111816 | tf_op jit(solution)/shard_map/ppermute | solution.py:319
  36.3 3.0 %collective-permute-start.9 = (bf16[784,512]{1,0:T(8,128)(2,1)S(1)}, bf16[784,512]{1,0:T(8,128)(2,1)S(1)}, u32[]{:S(2)}, u32[]{:S(2)}) collective-permute-start(bf16[784,512]{1,0:T(8,128)(2,1)S(1)} %half.1), channel_id=1, source_target_pairs={{0,128},{1,385},{128,256},{129,1},{256,384},{257,129},{384,0},{385... | collective-permute-start | bytes 2408456 | tf_op jit(solution)/shard_map/ppermute | solution.py:339
  39.2 2.4 %collective-permute-start.8 = (bf16[1568,512]{1,0:T(8,128)(2,1)S(1)}, bf16[1568,512]{1,0:T(8,128)(2,1)S(1)}, u32[]{:S(2)}, u32[]{:S(2)}) collective-permute-start(bf16[1568,512]{1,0:T(8,128)(2,1)S(1)} %collective-permute-done.5.weights.w_m), channel_id=1, source_target_pairs={{0,1},{1,0},{2,3},{3,2},{4,5},{5,4},{6,7},{7,6},{8,9},{9,8},{10,11... | collective-permute-start | bytes 4816904 | tf_op jit(solution)/shard_map/ppermute | solution.py:319
  41.6 5.3 %collective-permute-start.4 = (bf16[256,1152]{1,0:T(8,128)(2,1)S(1)}, bf16[256,1152]{1,0:T(8,128)(2,1)S(1)}, u32[]{:S(2)}, u32[]{:S(2)}) collective-permute-start(bf16[256,1152]{1,0:T(8,128)(2,1)S(1)} %get-tuple-element.45), channel_id=1, source_target_pairs={{0,2},{2,4},{3,1},{4,6},{5,3},{6,8},{7,5},{8,10},{9,7},{10,12},{11... | collective-permute-start | bytes 1769480 | tf_op jit(solution)/shard_map/ppermute | solution.py:330
  46.9 4.6 %collective-permute-done.9.w_mh = bf16[784,512]{1,0:T(8,128)(2,1)S(1)} collective-permute-done((bf16[784,512]{1,0:T(8,128)(2,1)S(1)}, bf16[784,512]{1,0:T(8,128)(2,1)S(1)}, u32[]{:S(2)}, u32[]{:S(2)}) %collective-permute-start.9) | collective-permute-done | bytes 802848 | tf_op jit(solution)/shard_map/ppermute | solution.py:339
  54.3 2.1 %collective-permute-start.7 = (bf16[256,1152]{1,0:T(8,128)(2,1)S(1)}, bf16[256,1152]{1,0:T(8,128)(2,1)S(1)}, u32[]{:S(2)}, u32[]{:S(2)}) collective-permute-start(bf16[256,1152]{1,0:T(8,128)(2,1)S(1)} %collective-permute-done.4.m2), channel_id=1, source_target_pairs={{0,1},{1,0},{2,3},{3,2},{4,5},{5,4},{6,7},{7,6},{8,9},{9,8},{10,11... | collective-permute-start | bytes 1769480 | tf_op jit(solution)/shard_map/ppermute | solution.py:319
  58.2 15.2 %forward.1 = (bf16[128,512]{1,0:T(8,128)(2,1)S(1)}, bf16[128,512]{1,0:T(8,128)(2,1)S(1)}, bf16[128,512]{1,0:T(8,128)(2,1)S(1)}, bf16[128,512]{1,0:T(8,128)(2,1)S...) custom-call(bf16[256,1664]{1,0:T(8,128)(2,1)S(1)} %get-tuple-element, ...), custom_call_target="tpu_custom_call" | custom-call | flops 10737418240 | bytes 20971520 | tf_op jit(solution)/shard_map/forward/pallas_call | solution.py:397
  73.4 9.4 %collective-permute-start.15 = (bf16[256,512]{1,0:T(8,128)(2,1)S(1)}, bf16[256,512]{1,0:T(8,128)(2,1)S(1)}, u32[]{:S(2)}, u32[]{:S(2)}) collective-permute-start(bf16[256,512]{1,0:T(8,128)(2,1)S(1)} %get-tuple-element.54.grad_pre), channel_id=1, source_target_pairs={{0,4},{2,6},{4,8},{5,1},{6,10},{7,3},{8,12},{9,5},{10,14},{11,7},{... | collective-permute-start | bytes 786440 | tf_op jit(solution)/shard_map/ppermute | solution.py:330
  82.8 1.9 %collective-permute-start.13 = (bf16[256,512]{1,0:T(8,128)(2,1)S(1)}, bf16[256,512]{1,0:T(8,128)(2,1)S(1)}, u32[]{:S(2)}, u32[]{:S(2)}) collective-permute-start(bf16[256,512]{1,0:T(8,128)(2,1)S(1)} %get-tuple-element.54.grad_pre), channel_id=1, source_target_pairs={{0,2},{2,4},{3,1},{4,6},{5,3},{6,8},{7,5},{8,10},{9,7},{10,12},{11... | collective-permute-start | bytes 786440 | tf_op jit(solution)/shard_map/ppermute | solution.py:330
  84.7 3.7 %collective-permute-start.14 = (bf16[128,512]{1,0:T(8,128)(2,1)S(1)}, bf16[128,512]{1,0:T(8,128)(2,1)S(1)}, u32[]{:S(2)}, u32[]{:S(2)}) collective-permute-start(bf16[128,512]{1,0:T(8,128)(2,1)S(1)} %get-tuple-element.55), channel_id=1, source_target_pairs={{0,256},{128,384},{256,0},{384,128},{1,257},{129,385},{257,1},{385... | collective-permute-start | bytes 393224 | tf_op jit(solution)/shard_map/ppermute | solution.py:344
  88.5 4.6 %collective-permute-done.14.l2 = bf16[128,512]{1,0:T(8,128)(2,1)S(1)} collective-permute-done((bf16[128,512]{1,0:T(8,128)(2,1)S(1)}, bf16[128,512]{1,0:T(8,128)(2,1)S(1)}, u32[]{:S(2)}, u32[]{:S(2)}) %collective-permute-start.14) | collective-permute-done | bytes 131104 | tf_op jit(solution)/shard_map/ppermute | solution.py:344
  95.0 2.4 %collective-permute-start.16 = (bf16[256,512]{1,0:T(8,128)(2,1)S(1)}, bf16[256,512]{1,0:T(8,128)(2,1)S(1)}, u32[]{:S(2)}, u32[]{:S(2)}) collective-permute-start(bf16[256,512]{1,0:T(8,128)(2,1)S(1)} %collective-permute-done.13.r1), channel_id=1, source_target_pairs={{0,1},{1,0},{2,3},{3,2},{4,5},{5,4},{6,7},{7,6},{8,9},{9,8},{10,11... | collective-permute-start | bytes 786440 | tf_op jit(solution)/shard_map/ppermute | solution.py:319
  98.6 3.7 %backward_a.1 = (bf16[128,512]{1,0:T(8,128)(2,1)S(1)}, bf16[256,512]{1,0:T(8,128)(2,1)S(1)}, bf16[768,768]{1,0:T(8,128)(2,1)S(1)}, bf16[768,512]{1,0:T(8,128)(2,...) custom-call(bf16[256,512]{1,0:T(8,128)(2,1)S(1)} %get-tuple-element., ...), custom_call_target="tpu_custom_call", output_to_operand_aliasing={{2}: (11, {}), {3}: (12, {}), {4}: (13, {}), {5}: (14, {}),... | custom-call | flops 4026531840 | bytes 7864320 | tf_op jit(solution)/shard_map/backward_a/pallas_call | solution.py:422
  102.3 3.6 %collective-permute-start.18 = (bf16[256,512]{1,0:T(8,128)(2,1)S(1)}, bf16[256,512]{1,0:T(8,128)(2,1)S(1)}, u32[]{:S(2)}, u32[]{:S(2)}) collective-permute-start(bf16[256,512]{1,0:T(8,128)(2,1)S(1)} %get-tuple-element.65.g2_own), channel_id=1, source_target_pairs={{0,4},{2,6},{4,8},{5,1},{6,10},{7,3},{8,12},{9,5},{10,14},{11,7},{... | collective-permute-start | bytes 786440 | tf_op jit(solution)/shard_map/ppermute | solution.py:330
  105.9 6.9 %collective-permute-start.19 = (bf16[256,512]{1,0:T(8,128)(2,1)S(1)}, bf16[256,512]{1,0:T(8,128)(2,1)S(1)}, u32[]{:S(2)}, u32[]{:S(2)}) collective-permute-start(bf16[256,512]{1,0:T(8,128)(2,1)S(1)} %get-tuple-element.65.g2_own), channel_id=1, source_target_pairs={{0,2},{2,4},{3,1},{4,6},{5,3},{6,8},{7,5},{8,10},{9,7},{10,12},{11... | collective-permute-start | bytes 786440 | tf_op jit(solution)/shard_map/ppermute | solution.py:330
  112.8 3.1 %collective-permute-start.11 = (bf16[128,512]{1,0:T(8,128)(2,1)S(1)}, bf16[128,512]{1,0:T(8,128)(2,1)S(1)}, u32[]{:S(2)}, u32[]{:S(2)}) collective-permute-start(bf16[128,512]{1,0:T(8,128)(2,1)S(1)} %get-tuple-element.52), channel_id=1, source_target_pairs={{0,128},{128,256},{256,384},{384,0},{1,129},{129,257},{257,385},{3... | collective-permute-start | bytes 393224 | tf_op jit(solution)/shard_map/ppermute | solution.py:344
  115.9 4.0 %collective-permute-start.12 = (bf16[128,512]{1,0:T(8,128)(2,1)S(1)}, bf16[128,512]{1,0:T(8,128)(2,1)S(1)}, u32[]{:S(2)}, u32[]{:S(2)}) collective-permute-start(bf16[128,512]{1,0:T(8,128)(2,1)S(1)} %get-tuple-element.53), channel_id=1, source_target_pairs={{0,384},{128,0},{256,128},{384,256},{1,385},{129,1},{257,129},{385... | collective-permute-start | bytes 393224 | tf_op jit(solution)/shard_map/ppermute | solution.py:344
  124.7 2.4 %collective-permute-start.21 = (bf16[256,512]{1,0:T(8,128)(2,1)S(1)}, bf16[256,512]{1,0:T(8,128)(2,1)S(1)}, u32[]{:S(2)}, u32[]{:S(2)}) collective-permute-start(bf16[256,512]{1,0:T(8,128)(2,1)S(1)} %collective-permute-done.18.r2), channel_id=1, source_target_pairs={{0,1},{1,0},{2,3},{3,2},{4,5},{5,4},{6,7},{7,6},{8,9},{9,8},{10,11... | collective-permute-start | bytes 786440 | tf_op jit(solution)/shard_map/ppermute | solution.py:319
  128.2 4.4 %backward_b.1 = (bf16[128,512]{1,0:T(8,128)(2,1)S(1)}, bf16[128,512]{1,0:T(8,128)(2,1)S(1)}, bf16[128,512]{1,0:T(8,128)(2,1)S(1)}, bf16[128,512]{1,0:T(8,128)(2,1)S(1)}) custom-call(bf16[256,512]{1,0:T(8,128)(2,1)S(1)} %get-tuple-element.65.g2_own, bf16[256,512]{1,0:T(8,128)(2,1)S(1)} %collective-permute-done.19.r1, ...), custom_call_target="tpu_custom_call" | custom-call | flops 4697620480 | bytes 9175040 | tf_op jit(solution)/shard_map/backward_b/pallas_call | solution.py:440
  132.7 2.6 %collective-permute-start.22 = (bf16[128,512]{1,0:T(8,128)(2,1)S(1)}, bf16[128,512]{1,0:T(8,128)(2,1)S(1)}, u32[]{:S(2)}, u32[]{:S(2)}) collective-permute-start(bf16[128,512]{1,0:T(8,128)(2,1)S(1)} %get-tuple-element.77), channel_id=1, source_target_pairs={{0,128},{128,256},{256,384},{384,0},{1,129},{129,257},{257,385},{3... | collective-permute-start | bytes 393224 | tf_op jit(solution)/shard_map/ppermute | solution.py:344
  135.2 6.0 %collective-permute-start.23 = (bf16[128,512]{1,0:T(8,128)(2,1)S(1)}, bf16[128,512]{1,0:T(8,128)(2,1)S(1)}, u32[]{:S(2)}, u32[]{:S(2)}) collective-permute-start(bf16[128,512]{1,0:T(8,128)(2,1)S(1)} %get-tuple-element.78), channel_id=1, source_target_pairs={{0,256},{128,384},{256,0},{384,128},{1,257},{129,385},{257,1},{385... | collective-permute-start | bytes 393224 | tf_op jit(solution)/shard_map/ppermute | solution.py:344
  141.2 2.5 %collective-permute-start.24 = (bf16[128,512]{1,0:T(8,128)(2,1)S(1)}, bf16[128,512]{1,0:T(8,128)(2,1)S(1)}, u32[]{:S(2)}, u32[]{:S(2)}) collective-permute-start(bf16[128,512]{1,0:T(8,128)(2,1)S(1)} %get-tuple-element.79), channel_id=1, source_target_pairs={{0,384},{128,0},{256,128},{384,256},{1,385},{129,1},{257,129},{385... | collective-permute-start | bytes 393224 | tf_op jit(solution)/shard_map/ppermute | solution.py:344
  143.8 2.1 %collective-permute-done.23.g2 = bf16[128,512]{1,0:T(8,128)(2,1)S(1)} collective-permute-done((bf16[128,512]{1,0:T(8,128)(2,1)S(1)}, bf16[128,512]{1,0:T(8,128)(2,1)S(1)}, u32[]{:S(2)}, u32[]{:S(2)}) %collective-permute-start.23) | collective-permute-done | bytes 131104 | tf_op jit(solution)/shard_map/ppermute | solution.py:344
  145.8 2.5 %collective-permute-done.24.g3 = bf16[128,512]{1,0:T(8,128)(2,1)S(1)} collective-permute-done((bf16[128,512]{1,0:T(8,128)(2,1)S(1)}, bf16[128,512]{1,0:T(8,128)(2,1)S(1)}, u32[]{:S(2)}, u32[]{:S(2)}) %collective-permute-start.24) | collective-permute-done | bytes 131104 | tf_op jit(solution)/shard_map/ppermute | solution.py:344
  (37 shorter events, 17.2 us)
Async XLA Ops:
  0.6 6.8 %copy-start.4 = (s32[4]{0:T(128)S(1)}, s32[4]{0:T(128)}, u32[]{:S(2)}) copy-start(s32[4]{0:T(128)} %source.1) | copy-start | bytes 52
  0.6 6.8 %copy-start.3 = (bf16[4,128,128]{2,1,0:T(8,128)(2,1)S(1)}, bf16[4,128,128]{2,1,0:T(8,128)(2,1)}, u32[]{:S(2)}) copy-start(bf16[4,128,128]{2,1,0:T(8,128)(2,1)} %tiles.1) | copy-start | bytes 393220
  0.7 6.8 %copy-start.2 = (bf16[4,128,512]{2,1,0:T(8,128)(2,1)S(1)}, bf16[4,128,512]{2,1,0:T(8,128)(2,1)}, u32[]{:S(2)}) copy-start(bf16[4,128,512]{2,1,0:T(8,128)(2,1)} %cotangent.1) | copy-start | bytes 1572868
  0.7 6.8 %copy-start.1 = (bf16[4,128,512]{2,1,0:T(8,128)(2,1)S(1)}, bf16[4,128,512]{2,1,0:T(8,128)(2,1)}, u32[]{:S(2)}) copy-start(bf16[4,128,512]{2,1,0:T(8,128)(2,1)} %latent.1) | copy-start | bytes 1572868
  3.4 30.8 %collective-permute-start.5 = (bf16[1568,512]{1,0:T(8,128)(2,1)}, bf16[1568,512]{1,0:T(8,128)(2,1)S(1)}, u32[]{:S(2)}, u32[]{:S(2)}) collective-permute-start(bf16[1568,512]{1,0:T(8,128)(2,1)} %weights.1.w_own), channel_id=1, source_target_pairs={{0,128},{1,385},{128,256},{129,1},{256,384},{257,129},{384,0},{385... | collective-permute-start | bytes 4816904 | tf_op jit(solution)/shard_map/ppermute | solution.py:339
  8.4 4.1 %collective-permute-start = (bf16[128,1664]{1,0:T(8,128)(2,1)S(1)}, bf16[128,1664]{1,0:T(8,128)(2,1)S(1)}, u32[]{:S(2)}, u32[]{:S(2)}) collective-permute-start(bf16[128,1664]{1,0:T(8,128)(2,1)S(1)} %prepare.1.own), channel_id=1, source_target_pairs={{0,1},{1,0},{2,3},{3,2},{4,5},{5,4},{6,7},{7,6},{8,9},{9,8},{10,11... | collective-permute-start | bytes 1277960 | tf_op jit(solution)/shard_map/ppermute | solution.py:319
  12.6 21.3 %collective-permute-start.1 = (bf16[256,1664]{1,0:T(8,128)(2,1)S(1)}, bf16[256,1664]{1,0:T(8,128)(2,1)S(1)}, u32[]{:S(2)}, u32[]{:S(2)}) collective-permute-start(bf16[256,1664]{1,0:T(8,128)(2,1)S(1)} %get-tuple-element.42.own), channel_id=1, source_target_pairs={{0,2},{2,4},{3,1},{4,6},{5,3},{6,8},{7,5},{8,10},{9,7},{10,12},{11... | collective-permute-start | bytes 2555912 | tf_op jit(solution)/shard_map/ppermute | solution.py:330
  15.8 18.1 %collective-permute-start.2 = (bf16[256,1152]{1,0:T(8,128)(2,1)S(1)}, bf16[256,1152]{1,0:T(8,128)(2,1)S(1)}, u32[]{:S(2)}, u32[]{:S(2)}) collective-permute-start(bf16[256,1152]{1,0:T(8,128)(2,1)S(1)} %get-tuple-element.43), channel_id=1, source_target_pairs={{0,6},{2,8},{4,10},{6,12},{7,1},{8,14},{9,3},{10,16},{11,5},{12,18... | collective-permute-start | bytes 1769480 | tf_op jit(solution)/shard_map/ppermute | solution.py:330
  19.9 10.8 %collective-permute-start.3 = (bf16[256,512]{1,0:T(8,128)(2,1)S(1)}, bf16[256,512]{1,0:T(8,128)(2,1)S(1)}, u32[]{:S(2)}, u32[]{:S(2)}) collective-permute-start(bf16[256,512]{1,0:T(8,128)(2,1)S(1)} %get-tuple-element.44), channel_id=1, source_target_pairs={{0,8},{2,10},{4,12},{6,14},{8,16},{9,1},{10,18},{11,3},{12,20},{13... | collective-permute-start | bytes 786440 | tf_op jit(solution)/shard_map/ppermute | solution.py:330
  34.1 24.1 %copy-start = (bf16[1568,512]{1,0:T(8,128)(2,1)S(1)}, bf16[1568,512]{1,0:T(8,128)(2,1)}, u32[]{:S(2)}) copy-start(bf16[1568,512]{1,0:T(8,128)(2,1)} %weights.1.w_own) | copy-start | bytes 4816900
  34.2 24.0 %collective-permute-start.6 = (bf16[256,3328]{1,0:T(8,128)(2,1)S(1)}, bf16[256,3328]{1,0:T(8,128)(2,1)S(1)}, u32[]{:S(2)}, u32[]{:S(2)}) collective-permute-start(bf16[256,3328]{1,0:T(8,128)(2,1)S(1)} %get-tuple-element.48), channel_id=1, source_target_pairs={{0,1},{1,0},{2,3},{3,2},{4,5},{5,4},{6,7},{7,6},{8,9},{9,8},{10,11... | collective-permute-start | bytes 5111816 | tf_op jit(solution)/shard_map/ppermute | solution.py:319
  36.3 15.3 %collective-permute-start.9 = (bf16[784,512]{1,0:T(8,128)(2,1)S(1)}, bf16[784,512]{1,0:T(8,128)(2,1)S(1)}, u32[]{:S(2)}, u32[]{:S(2)}) collective-permute-start(bf16[784,512]{1,0:T(8,128)(2,1)S(1)} %half.1), channel_id=1, source_target_pairs={{0,128},{1,385},{128,256},{129,1},{256,384},{257,129},{384,0},{385... | collective-permute-start | bytes 2408456 | tf_op jit(solution)/shard_map/ppermute | solution.py:339
  39.2 19.0 %collective-permute-start.8 = (bf16[1568,512]{1,0:T(8,128)(2,1)S(1)}, bf16[1568,512]{1,0:T(8,128)(2,1)S(1)}, u32[]{:S(2)}, u32[]{:S(2)}) collective-permute-start(bf16[1568,512]{1,0:T(8,128)(2,1)S(1)} %collective-permute-done.5.weights.w_m), channel_id=1, source_target_pairs={{0,1},{1,0},{2,3},{3,2},{4,5},{5,4},{6,7},{7,6},{8,9},{9,8},{10,11... | collective-permute-start | bytes 4816904 | tf_op jit(solution)/shard_map/ppermute | solution.py:319
  41.6 12.7 %collective-permute-start.4 = (bf16[256,1152]{1,0:T(8,128)(2,1)S(1)}, bf16[256,1152]{1,0:T(8,128)(2,1)S(1)}, u32[]{:S(2)}, u32[]{:S(2)}) collective-permute-start(bf16[256,1152]{1,0:T(8,128)(2,1)S(1)} %get-tuple-element.45), channel_id=1, source_target_pairs={{0,2},{2,4},{3,1},{4,6},{5,3},{6,8},{7,5},{8,10},{9,7},{10,12},{11... | collective-permute-start | bytes 1769480 | tf_op jit(solution)/shard_map/ppermute | solution.py:330
  51.6 6.6 %collective-permute-start.10 = (bf16[784,512]{1,0:T(8,128)(2,1)S(1)}, bf16[784,512]{1,0:T(8,128)(2,1)S(1)}, u32[]{:S(2)}, u32[]{:S(2)}) collective-permute-start(bf16[784,512]{1,0:T(8,128)(2,1)S(1)} %collective-permute-done.9.w_mh), channel_id=1, source_target_pairs={{0,1},{1,0},{2,3},{3,2},{4,5},{5,4},{6,7},{7,6},{8,9},{9,8},{10,11... | collective-permute-start | bytes 2408456 | tf_op jit(solution)/shard_map/ppermute | solution.py:319
  54.3 3.9 %collective-permute-start.7 = (bf16[256,1152]{1,0:T(8,128)(2,1)S(1)}, bf16[256,1152]{1,0:T(8,128)(2,1)S(1)}, u32[]{:S(2)}, u32[]{:S(2)}) collective-permute-start(bf16[256,1152]{1,0:T(8,128)(2,1)S(1)} %collective-permute-done.4.m2), channel_id=1, source_target_pairs={{0,1},{1,0},{2,3},{3,2},{4,5},{5,4},{6,7},{7,6},{8,9},{9,8},{10,11... | collective-permute-start | bytes 1769480 | tf_op jit(solution)/shard_map/ppermute | solution.py:319
  73.4 19.7 %collective-permute-start.15 = (bf16[256,512]{1,0:T(8,128)(2,1)S(1)}, bf16[256,512]{1,0:T(8,128)(2,1)S(1)}, u32[]{:S(2)}, u32[]{:S(2)}) collective-permute-start(bf16[256,512]{1,0:T(8,128)(2,1)S(1)} %get-tuple-element.54.grad_pre), channel_id=1, source_target_pairs={{0,4},{2,6},{4,8},{5,1},{6,10},{7,3},{8,12},{9,5},{10,14},{11,7},{... | collective-permute-start | bytes 786440 | tf_op jit(solution)/shard_map/ppermute | solution.py:330
  82.8 12.2 %collective-permute-start.13 = (bf16[256,512]{1,0:T(8,128)(2,1)S(1)}, bf16[256,512]{1,0:T(8,128)(2,1)S(1)}, u32[]{:S(2)}, u32[]{:S(2)}) collective-permute-start(bf16[256,512]{1,0:T(8,128)(2,1)S(1)} %get-tuple-element.54.grad_pre), channel_id=1, source_target_pairs={{0,2},{2,4},{3,1},{4,6},{5,3},{6,8},{7,5},{8,10},{9,7},{10,12},{11... | collective-permute-start | bytes 786440 | tf_op jit(solution)/shard_map/ppermute | solution.py:330
  84.7 8.4 %collective-permute-start.14 = (bf16[128,512]{1,0:T(8,128)(2,1)S(1)}, bf16[128,512]{1,0:T(8,128)(2,1)S(1)}, u32[]{:S(2)}, u32[]{:S(2)}) collective-permute-start(bf16[128,512]{1,0:T(8,128)(2,1)S(1)} %get-tuple-element.55), channel_id=1, source_target_pairs={{0,256},{128,384},{256,0},{384,128},{1,257},{129,385},{257,1},{385... | collective-permute-start | bytes 393224 | tf_op jit(solution)/shard_map/ppermute | solution.py:344
  93.1 4.3 %collective-permute-start.17 = (bf16[256,512]{1,0:T(8,128)(2,1)S(1)}, bf16[256,512]{1,0:T(8,128)(2,1)S(1)}, u32[]{:S(2)}, u32[]{:S(2)}) collective-permute-start(bf16[256,512]{1,0:T(8,128)(2,1)S(1)} %collective-permute-done.15.r2), channel_id=1, source_target_pairs={{0,1},{1,0},{2,3},{3,2},{4,5},{5,4},{6,7},{7,6},{8,9},{9,8},{10,11... | collective-permute-start | bytes 786440 | tf_op jit(solution)/shard_map/ppermute | solution.py:319
  95.0 3.6 %collective-permute-start.16 = (bf16[256,512]{1,0:T(8,128)(2,1)S(1)}, bf16[256,512]{1,0:T(8,128)(2,1)S(1)}, u32[]{:S(2)}, u32[]{:S(2)}) collective-permute-start(bf16[256,512]{1,0:T(8,128)(2,1)S(1)} %collective-permute-done.13.r1), channel_id=1, source_target_pairs={{0,1},{1,0},{2,3},{3,2},{4,5},{5,4},{6,7},{7,6},{8,9},{9,8},{10,11... | collective-permute-start | bytes 786440 | tf_op jit(solution)/shard_map/ppermute | solution.py:319
  102.3 20.5 %collective-permute-start.18 = (bf16[256,512]{1,0:T(8,128)(2,1)S(1)}, bf16[256,512]{1,0:T(8,128)(2,1)S(1)}, u32[]{:S(2)}, u32[]{:S(2)}) collective-permute-start(bf16[256,512]{1,0:T(8,128)(2,1)S(1)} %get-tuple-element.65.g2_own), channel_id=1, source_target_pairs={{0,4},{2,6},{4,8},{5,1},{6,10},{7,3},{8,12},{9,5},{10,14},{11,7},{... | collective-permute-start | bytes 786440 | tf_op jit(solution)/shard_map/ppermute | solution.py:330
  105.9 16.9 %collective-permute-start.19 = (bf16[256,512]{1,0:T(8,128)(2,1)S(1)}, bf16[256,512]{1,0:T(8,128)(2,1)S(1)}, u32[]{:S(2)}, u32[]{:S(2)}) collective-permute-start(bf16[256,512]{1,0:T(8,128)(2,1)S(1)} %get-tuple-element.65.g2_own), channel_id=1, source_target_pairs={{0,2},{2,4},{3,1},{4,6},{5,3},{6,8},{7,5},{8,10},{9,7},{10,12},{11... | collective-permute-start | bytes 786440 | tf_op jit(solution)/shard_map/ppermute | solution.py:330
  112.8 8.1 %collective-permute-start.11 = (bf16[128,512]{1,0:T(8,128)(2,1)S(1)}, bf16[128,512]{1,0:T(8,128)(2,1)S(1)}, u32[]{:S(2)}, u32[]{:S(2)}) collective-permute-start(bf16[128,512]{1,0:T(8,128)(2,1)S(1)} %get-tuple-element.52), channel_id=1, source_target_pairs={{0,128},{128,256},{256,384},{384,0},{1,129},{129,257},{257,385},{3... | collective-permute-start | bytes 393224 | tf_op jit(solution)/shard_map/ppermute | solution.py:344
  115.9 6.9 %collective-permute-start.12 = (bf16[128,512]{1,0:T(8,128)(2,1)S(1)}, bf16[128,512]{1,0:T(8,128)(2,1)S(1)}, u32[]{:S(2)}, u32[]{:S(2)}) collective-permute-start(bf16[128,512]{1,0:T(8,128)(2,1)S(1)} %get-tuple-element.53), channel_id=1, source_target_pairs={{0,384},{128,0},{256,128},{384,256},{1,385},{129,1},{257,129},{385... | collective-permute-start | bytes 393224 | tf_op jit(solution)/shard_map/ppermute | solution.py:344
  122.8 4.3 %collective-permute-start.20 = (bf16[256,512]{1,0:T(8,128)(2,1)S(1)}, bf16[256,512]{1,0:T(8,128)(2,1)S(1)}, u32[]{:S(2)}, u32[]{:S(2)}) collective-permute-start(bf16[256,512]{1,0:T(8,128)(2,1)S(1)} %collective-permute-done.19.r1), channel_id=1, source_target_pairs={{0,1},{1,0},{2,3},{3,2},{4,5},{5,4},{6,7},{7,6},{8,9},{9,8},{10,11... | collective-permute-start | bytes 786440 | tf_op jit(solution)/shard_map/ppermute | solution.py:319
  124.7 3.6 %collective-permute-start.21 = (bf16[256,512]{1,0:T(8,128)(2,1)S(1)}, bf16[256,512]{1,0:T(8,128)(2,1)S(1)}, u32[]{:S(2)}, u32[]{:S(2)}) collective-permute-start(bf16[256,512]{1,0:T(8,128)(2,1)S(1)} %collective-permute-done.18.r2), channel_id=1, source_target_pairs={{0,1},{1,0},{2,3},{3,2},{4,5},{5,4},{6,7},{7,6},{8,9},{9,8},{10,11... | collective-permute-start | bytes 786440 | tf_op jit(solution)/shard_map/ppermute | solution.py:319
  132.7 11.1 %collective-permute-start.22 = (bf16[128,512]{1,0:T(8,128)(2,1)S(1)}, bf16[128,512]{1,0:T(8,128)(2,1)S(1)}, u32[]{:S(2)}, u32[]{:S(2)}) collective-permute-start(bf16[128,512]{1,0:T(8,128)(2,1)S(1)} %get-tuple-element.77), channel_id=1, source_target_pairs={{0,128},{128,256},{256,384},{384,0},{1,129},{129,257},{257,385},{3... | collective-permute-start | bytes 393224 | tf_op jit(solution)/shard_map/ppermute | solution.py:344
  135.2 10.6 %collective-permute-start.23 = (bf16[128,512]{1,0:T(8,128)(2,1)S(1)}, bf16[128,512]{1,0:T(8,128)(2,1)S(1)}, u32[]{:S(2)}, u32[]{:S(2)}) collective-permute-start(bf16[128,512]{1,0:T(8,128)(2,1)S(1)} %get-tuple-element.78), channel_id=1, source_target_pairs={{0,256},{128,384},{256,0},{384,128},{1,257},{129,385},{257,1},{385... | collective-permute-start | bytes 393224 | tf_op jit(solution)/shard_map/ppermute | solution.py:344
  141.2 7.1 %collective-permute-start.24 = (bf16[128,512]{1,0:T(8,128)(2,1)S(1)}, bf16[128,512]{1,0:T(8,128)(2,1)S(1)}, u32[]{:S(2)}, u32[]{:S(2)}) collective-permute-start(bf16[128,512]{1,0:T(8,128)(2,1)S(1)} %get-tuple-element.79), channel_id=1, source_target_pairs={{0,384},{128,0},{256,128},{384,256},{1,385},{129,1},{257,129},{385... | collective-permute-start | bytes 393224 | tf_op jit(solution)/shard_map/ppermute | solution.py:344

commit v5 on v4

--- a/solution.py
+++ b/solution.py
@@ -15,7 +15,8 @@
 BAND = 3 * PAIR
 SENT = 5 * B
 WIDE = H + SENT
-AT3 = WIDE + H
+AT2 = WIDE + H
+AT3 = AT2 + WIDE
 AT4 = AT3 + WIDE
 REACH = 4
 W_ROWS = 3 * H + 32
@@ -126,11 +127,15 @@
         value[rows(held, B), :] = ref[:, 0:H]
 
 
-def join_kernel(m1, m3, m4, joined, near):
-    joined[:, 0:AT3] = m1[...]
+def cut_kernel(m1, _, near):
+    near[...] = m1[:, 0:WIDE]
+
+
+def join_kernel(m1, m2, m3, m4, _, __, joined):
+    joined[:, 0:AT2] = m1[...]
+    joined[:, AT2:AT3] = m2[...]
     joined[:, AT3:AT4] = m3[...]
     joined[:, AT4:] = m4[...]
-    near[...] = m1[:, 0:WIDE]
 
 
 def layer_gain(weights, layer):
@@ -143,15 +148,10 @@
     return weights[start : start + H, :]
 
 
-def send_pieces(stacked, pieces, section):
-    for step, piece in enumerate(pieces):
-        piece[...] = stacked[(section + step) % 4]
-
-
 def forward_kernel(
-    own, m1, m2, m3, m4, joined, t2, w_own, w_m, w_t, w_mh, w_th,
-    l0, l1, l2, l3, grad_pre, turned, v3_out, v2_out, v1_out, f2_out, f1_out, f0_out, weights,
-    latents, v_a, v_b, band, unit, source,
+    own, m1, m2, m3, m4, joined, w_own, w_m, w_t, w_mh, w_th,
+    latents, grad_pre, turned, v3_out, v2_out, v1_out, f2_out, f1_out, f0_out, weights,
+    v_a, v_b, band, unit, source,
 ):
     section, core = lax.axis_index("section"), lax.axis_index("core")
     weights[pl.ds(pl.multiple_of(section * W_ROWS, 16), W_ROWS), :] = w_own[...]
@@ -171,7 +171,8 @@
             rim = (1 - k) * SENT
             band[row, rim : rim + B] = jnp.zeros((B, B), BF16)
 
-    t1, t3, t4 = joined.at[:, 0:AT3], joined.at[:, AT3:AT4], joined.at[:, AT4:]
+    t1, t2 = joined.at[:, 0:AT2], joined.at[:, AT2:AT3]
+    t3, t4 = joined.at[:, AT3:AT4], joined.at[:, AT4:]
     v_a[rows(REACH), :] = own[:, 0:H]
     put_band(REACH - 1, own)
     for step, (m, t) in enumerate(((m1, t1), (m2, t2), (m3, t3), (m4, t4)), start=1):
@@ -225,7 +226,6 @@
         if layer == 2:
             v3_out[...] = later[3 * PAIR : 6 * PAIR, :]
         now, later = later, now
-    send_pieces(latents, (l0, l1, l2, l3), section)
 
     for j in range(3, 6):
         for i in range(j - 1, j + 2):
@@ -260,12 +260,12 @@
 
 
 def backward_a_kernel(
-    grad_pre, r1, r2, o1, o2, own, m1, t1, v3, v2, f2, turned, v1, f1, f0, weights,
-    g3_out, g2_out, kept_turned, kept_v1, kept_f1, kept_f0, kept_weights, held, cot, g3, gp2,
+    grad_pre, r1, r2, o1, o2, own, m1, t1, v3, v2, f2, turned, v1, f1, f0, latents, weights,
+    g3_out, g2_out, kept_turned, kept_v1, kept_f1, kept_f0, kept_latents, kept_weights, held, cot, g3, gp2,
 ):
     core = lax.axis_index("core")
     place(held, grad_pre, ((r1, o1), (r2, o2)), core)
-    place(cot, own.at[:, WIDE:], ((m1.at[:, WIDE:], t1.at[:, WIDE:AT3]),), core)
+    place(cot, own.at[:, WIDE:], ((m1.at[:, WIDE:], t1.at[:, WIDE:AT2]),), core)
     for j in range(3):
         g3[rows(j), :] = grad_pair(
             cot[rows(j), :], held[rows(j + 1), :], held[j * PAIR : j * PAIR + BAND, :],
@@ -279,8 +279,8 @@
 
 
 def backward_b_kernel(
-    g2_own, r1, r2, o1, o2, g3_mine, turned, v1, own, f1, f0, weights,
-    p0, p1, p2, p3, grads, g2, gp1, g1, gp0,
+    g2_own, r1, r2, o1, o2, g3_mine, turned, v1, own, f1, f0, latents, weights,
+    results, g2, gp1, g1, gp0,
 ):
     core = lax.axis_index("core")
     place(g2, g2_own, ((r1, o1), (r2, o2)), core)
@@ -293,22 +293,20 @@
         )
         gp0[rows(j), :] = (dot_t(g1[rows(j), :], weight(weights, 0, 2)) * f0[rows(j), :]).astype(BF16)
     mine = pl.ds(pl.multiple_of(PAIR + core * B, B), B)
-    grads[3] = g3_mine[...]
-    grads[2] = g2_own[rows(core, B), :]
-    grads[1] = g1[mine, :]
+    results[:, 0:B, :] = latents[...]
+    results[3, B:PAIR, :] = g3_mine[...]
+    results[2, B:PAIR, :] = g2_own[rows(core, B), :]
+    results[1, B:PAIR, :] = g1[mine, :]
     g0 = grad_pair(g1[rows(1), :], gp0[rows(1), :], gp0[...], turned[rows(1), :], own[:, 0:H], weights, 0)
     g1[rows(1), :] = g0
-    grads[0] = g1[mine, :]
-    send_pieces(grads, (p0, p1, p2, p3), lax.axis_index("section"))
-
-
-def collect_kernel(l0, l1, l2, l3, g0, g1, g2, g3, latents, grads, sems):
-    section = lax.axis_index("section")
-    copies = []
-    for side, (out, pieces) in enumerate(((latents, (l0, l1, l2, l3)), (grads, (g0, g1, g2, g3)))):
-        for step, piece in enumerate(pieces):
-            at = (section + 4 - step) % 4
-            copies.append(pltpu.make_async_copy(piece, out.at[at], sems.at[4 * side + step]))
+    results[0, B:PAIR, :] = g1[mine, :]
+
+
+def split_kernel(results, latents, grads, sems):
+    copies = [
+        pltpu.make_async_copy(results.at[:, pl.ds(0, B)], latents, sems.at[0]),
+        pltpu.make_async_copy(results.at[:, pl.ds(B, B)], grads, sems.at[1]),
+    ]
     for copy in copies:
         copy.start()
     for copy in copies:
@@ -337,11 +335,6 @@
         pairs.append((2 * s, 2 * ((s + 1) % count)))
         pairs.append((2 * s + 1, 2 * ((s - 1) % count) + 1))
     return lax.ppermute(value, ("section", "core"), pairs)
-
-
-def onward(value, steps):
-    count = lax.axis_size("section")
-    return lax.ppermute(value, "section", [(s, (s + steps) % count) for s in range(count)])
 
 
 def body(latent, cotangent, w_a, w_b, w_c, gain, tiles, pair_source, live_pairs):
@@ -370,42 +363,35 @@
     )(pair_source, live_pairs, latent, cotangent, tiles)
     first, near, value = call(
         pack_kernel,
-        [((PAIR, AT3), BF16), ((PAIR, WIDE), BF16), ((PAIR, H), BF16)],
+        [((PAIR, AT2), BF16), ((PAIR, WIDE), BF16), ((PAIR, H), BF16)],
         [VMEM] * 2,
         [],
         4,
         "pack",
     )(own, swap(own))
     m1, m3, m4 = spread(first, 1), spread(near, 3), spread(value, 4)
-    joined, near = call(
-        join_kernel,
-        [((PAIR, AT4 + H), BF16), ((PAIR, WIDE), BF16)],
-        [VMEM] * 3,
-        [],
-        4,
-        "join",
-    )(m1, m3, m4)
     arrived, m4 = lax.optimization_barrier((w_m, m4))
     (w_half,) = call(half_kernel, [((W_HALF, H), BF16)], [VMEM], [], 4, "half")(arrived)
     w_mh = around(w_half)
+    (near,) = call(cut_kernel, [((PAIR, WIDE), BF16)], [VMEM, ANY], [], 4, "cut")(m1, w_half)
     m2 = spread(near, 1)
-    w_m, joined = lax.optimization_barrier((w_m, joined))
-    joined, w_t = swap(joined), swap(w_m)
-    t2, w_th = swap(m2), swap(w_mh)
+    w_t = swap(w_m)
+    (joined,) = call(
+        join_kernel, [((PAIR, AT4 + H), BF16)], [VMEM] * 4 + [ANY] * 2, [], 4, "join"
+    )(m1, m2, m3, m4, w_mh, w_t)
+    joined, w_th = swap(joined), swap(w_mh)
 
     span = 2 * REACH + 1
-    l0, l1, l2, l3, grad_pre, turned, v3, v2, v1, f2, f1, f0, weights = call(
+    latents, grad_pre, turned, v3, v2, v1, f2, f1, f0, weights = call(
         forward_kernel,
         [
-            ((B, H), BF16), ((B, H), BF16), ((B, H), BF16), ((B, H), BF16),
-            ((PAIR, H), BF16), ((3 * PAIR, BAND), BF16),
+            ((4, B, H), BF16), ((PAIR, H), BF16), ((3 * PAIR, BAND), BF16),
             ((3 * PAIR, H), BF16), ((PAIR, H), BF16), ((3 * PAIR, H), BF16),
             ((3 * PAIR, H), BF16), ((5 * PAIR, H), BF16), ((3 * PAIR, H), BF16),
             ((4 * W_ROWS, H), BF16),
         ],
-        [VMEM] * 12,
+        [VMEM] * 11,
         [
-            pltpu.VMEM((4, B, H), BF16),
             pltpu.VMEM((span * PAIR, H), BF16), pltpu.VMEM((span * PAIR, H), BF16),
             pltpu.VMEM(((span - 2) * PAIR, BAND), BF16),
             pltpu.VMEM((span * PAIR, H), BF16), pltpu.VMEM((span * PAIR, H), BF16),
@@ -413,16 +399,15 @@
         FWD_MIB,
         "forward",
         units=160,
-    )(first, m1, m2, m3, m4, joined, t2, w_own, w_m, w_t, w_mh, w_th)
+    )(first, m1, m2, m3, m4, joined, w_own, w_m, w_t, w_mh, w_th)
 
     r1 = spread(grad_pre, 1)
     r2 = spread(grad_pre, 2)
-    l2, r2 = lax.optimization_barrier((onward(l2, 2), r2))
-    kept = [turned, v1, f1, f0, weights]
-    g3, g2, turned, v1, f1, f0, weights = call(
+    kept = [turned, v1, f1, f0, latents, weights]
+    g3, g2, turned, v1, f1, f0, latents, weights = call(
         backward_a_kernel,
         [((B, H), BF16), ((PAIR, H), BF16)] + [(k.shape, k.dtype) for k in kept],
-        [VMEM] * 12 + [ANY] * 3 + [VMEM],
+        [VMEM] * 12 + [ANY] * 4 + [VMEM],
         [
             pltpu.VMEM((5 * PAIR, H), BF16), pltpu.VMEM((3 * PAIR, H), BF16),
             pltpu.VMEM((3 * PAIR, H), BF16), pltpu.VMEM((3 * PAIR, H), BF16),
@@ -436,31 +421,29 @@
 
     r1 = spread(g2, 1)
     r2 = spread(g2, 2)
-    l1, l3, r2 = lax.optimization_barrier((onward(l1, 1), onward(l3, 3), r2))
-    grads = call(
+    (results,) = call(
         backward_b_kernel,
-        [((B, H), BF16)] * 4,
-        [VMEM] * 12,
+        [((4, PAIR, H), BF16)],
+        [VMEM] * 13,
         [
-            pltpu.VMEM((4, B, H), BF16),
             pltpu.VMEM((5 * PAIR, H), BF16), pltpu.VMEM((5 * PAIR, H), BF16),
             pltpu.VMEM((3 * PAIR, H), BF16), pltpu.VMEM((3 * PAIR, H), BF16),
         ],
         BWD_MIB,
         "backward_b",
         units=70,
-    )(g2, r1, r2, swap(r1), swap(r2), g3, turned, v1, first, f1, f0, weights)
-
-    moved = [onward(piece, step) for step, piece in enumerate(grads) if step]
+    )(g2, r1, r2, swap(r1), swap(r2), g3, turned, v1, first, f1, f0, latents, weights)
+
+    results = lax.all_to_all(results, "section", 0, 0, tiled=True)
     latent_result, grad_result = call(
-        collect_kernel,
+        split_kernel,
         [((4, B, H), BF16)] * 2,
-        [VMEM] * 8,
-        [pltpu.SemaphoreType.DMA((8,))],
+        [ANY],
+        [pltpu.SemaphoreType.DMA((2,))],
         4,
-        "collect",
+        "split",
         out_specs=[HBM] * 2,
-    )(l0, l1, l2, l3, grads[0], *moved)
+    )(results)
     return (latent_result[None], grad_result[None])
 
 

time: 150 us -> 164 us (1.093)
  the two profiles are of different devices: /device:TPU:80 before, /device:TPU:120 now
where the time goes in v5:
time: 164 us
  waiting for transfers between devices  58.8 us (36%)
  starting transfers between devices  56.2 us (34%)
  Pallas kernels  28.2 us (17%)
  blocking collectives  18.7 us (11%)
  between operations  1.79 us (1%)
    ppermute x8, waiting for transfers between devices, spread(): return lax.ppermute(value, ('chip', 'core'), pairs)  37.1 us
    ppermute x8, starting transfers between devices, spread(): return lax.ppermute(value, ('chip', 'core'), pairs)  30.4 us
    ppermute x8, starting transfers between devices, swap(): return lax.ppermute(value, 'core', [(0, 1), (1, 0)])  20.3 us
    all_to_all x1, blocking collectives, body(): results = lax.all_to_all(results, 'section', 0, 0, tiled=True)  18.7 us
    ppermute x2, waiting for transfers between devices, around(): return lax.ppermute(value, ('section', 'core'), pairs)  16.3 us
    pallas_call x1, Pallas kernels, body(): call(forward_kernel, [((4, B, H), BF16), ((PAIR, H), BF16), ((3 * PAIR, B...  15.2 us
    ppermute x2, starting transfers between devices, around(): return lax.ppermute(value, ('section', 'core'), pairs)  5.59 us
    ppermute x8, waiting for transfers between devices, swap(): return lax.ppermute(value, 'core', [(0, 1), (1, 0)])  5.36 us
  transfers between devices with their start and end apart: 18, of which 9 were waited for; matrix products, arithmetic and copies ran while one was open for 0% of the time, Pallas kernels for 1%

profile of v5, /device:TPU:120, one launch (start us, length us, event | category | flops | bytes accessed | tf_op | source)
XLA Modules:
  0.0 163.8 jit_solution(11007798248812944212)
XLA Ops:
  0.7 2.7 %weights.1.w_own = bf16[1568,512]{1,0:T(8,128)(2,1)} custom-call(bf16[1,512,512]{2,1,0:T(8,128)(2,1)} %w_a.1, bf16[1,512,512]{2,1,0:T(8,128)(2,1)} %w_b.1, bf16[1,512,512]{2,1,0:T(8,128)(2,1)} %w_c.1, f32[1,512]{1,0:T(1,128)} %gain.1), custom_call_target="tpu_custom_call" | custom-call | tf_op jit(solution)/shard_map/weights/pallas_call | solution.py:343
  3.4 3.4 %collective-permute-start.2 = (bf16[1568,512]{1,0:T(8,128)(2,1)}, bf16[1568,512]{1,0:T(8,128)(2,1)S(1)}, u32[]{:S(2)}, u32[]{:S(2)}) collective-permute-start(bf16[1568,512]{1,0:T(8,128)(2,1)} %weights.1.w_own), channel_id=1, source_target_pairs={{0,128},{1,385},{128,256},{129,1},{256,384},{257,129},{384,0},{385... | collective-permute-start | bytes 4816904 | tf_op jit(solution)/shard_map/ppermute | solution.py:337
  8.4 2.7 %collective-permute-start = (bf16[128,1664]{1,0:T(8,128)(2,1)S(1)}, bf16[128,1664]{1,0:T(8,128)(2,1)S(1)}, u32[]{:S(2)}, u32[]{:S(2)}) collective-permute-start(bf16[128,1664]{1,0:T(8,128)(2,1)S(1)} %prepare.1.own), channel_id=1, source_target_pairs={{0,1},{1,0},{2,3},{3,2},{4,5},{5,4},{6,7},{7,6},{8,9},{9,8},{10,11... | collective-permute-start | bytes 1277960 | tf_op jit(solution)/shard_map/ppermute | solution.py:317
  11.1 16.3 %collective-permute-done.2.weights.w_m = bf16[1568,512]{1,0:T(8,128)(2,1)S(1)} collective-permute-done((bf16[1568,512]{1,0:T(8,128)(2,1)}, bf16[1568,512]{1,0:T(8,128)(2,1)S(1)}, u32[]{:S(2)}, u32[]{:S(2)}) %collective-permute-start.2) | collective-permute-done | bytes 1605664 | tf_op jit(solution)/shard_map/ppermute | solution.py:337
  27.4 1.9 %collective-permute-start.7 = (bf16[1568,512]{1,0:T(8,128)(2,1)S(1)}, bf16[1568,512]{1,0:T(8,128)(2,1)S(1)}, u32[]{:S(2)}, u32[]{:S(2)}) collective-permute-start(bf16[1568,512]{1,0:T(8,128)(2,1)S(1)} %collective-permute-done.2.weights.w_m), channel_id=1, source_target_pairs={{0,1},{1,0},{2,3},{3,2},{4,5},{5,4},{6,7},{7,6},{8,9},{9,8},{10,11... | collective-permute-start | bytes 4816904 | tf_op jit(solution)/shard_map/ppermute | solution.py:317
  29.5 4.7 %collective-permute-start.1 = (bf16[256,1664]{1,0:T(8,128)(2,1)S(1)}, bf16[256,1664]{1,0:T(8,128)(2,1)S(1)}, u32[]{:S(2)}, u32[]{:S(2)}) collective-permute-start(bf16[256,1664]{1,0:T(8,128)(2,1)S(1)} %get-tuple-element.27.own), channel_id=1, source_target_pairs={{0,2},{2,4},{3,1},{4,6},{5,3},{6,8},{7,5},{8,10},{9,7},{10,12},{11... | collective-permute-start | bytes 2555912 | tf_op jit(solution)/shard_map/ppermute | solution.py:328
  34.2 3.8 %collective-permute-start.3 = (bf16[256,512]{1,0:T(8,128)(2,1)S(1)}, bf16[256,512]{1,0:T(8,128)(2,1)S(1)}, u32[]{:S(2)}, u32[]{:S(2)}) collective-permute-start(bf16[256,512]{1,0:T(8,128)(2,1)S(1)} %get-tuple-element.28), channel_id=1, source_target_pairs={{0,8},{2,10},{4,12},{6,14},{8,16},{9,1},{10,18},{11,3},{12,20},{13... | collective-permute-start | bytes 786440 | tf_op jit(solution)/shard_map/ppermute | solution.py:328
  38.0 9.2 %collective-permute-done.3.m4 = bf16[256,512]{1,0:T(8,128)(2,1)S(1)} collective-permute-done((bf16[256,512]{1,0:T(8,128)(2,1)S(1)}, bf16[256,512]{1,0:T(8,128)(2,1)S(1)}, u32[]{:S(2)}, u32[]{:S(2)}) %collective-permute-start.3) | collective-permute-done | bytes 262176 | tf_op jit(solution)/shard_map/ppermute | solution.py:328
  47.3 2.2 %collective-permute-start.6 = (bf16[784,512]{1,0:T(8,128)(2,1)S(1)}, bf16[784,512]{1,0:T(8,128)(2,1)S(1)}, u32[]{:S(2)}, u32[]{:S(2)}) collective-permute-start(bf16[784,512]{1,0:T(8,128)(2,1)S(1)} %half.1._), channel_id=1, source_target_pairs={{0,128},{1,385},{128,256},{129,1},{256,384},{257,129},{384,0},{385... | collective-permute-start | bytes 2408456 | tf_op jit(solution)/shard_map/ppermute | solution.py:337
  49.5 1.9 %collective-permute-start.5 = (bf16[256,1152]{1,0:T(8,128)(2,1)S(1)}, bf16[256,1152]{1,0:T(8,128)(2,1)S(1)}, u32[]{:S(2)}, u32[]{:S(2)}) collective-permute-start(bf16[256,1152]{1,0:T(8,128)(2,1)S(1)} %get-tuple-element.30), channel_id=1, source_target_pairs={{0,6},{2,8},{4,10},{6,12},{7,1},{8,14},{9,3},{10,16},{11,5},{12,18... | collective-permute-start | bytes 1769480 | tf_op jit(solution)/shard_map/ppermute | solution.py:328
  51.5 8.4 %collective-permute-start.4 = (bf16[256,1152]{1,0:T(8,128)(2,1)S(1)}, bf16[256,1152]{1,0:T(8,128)(2,1)S(1)}, u32[]{:S(2)}, u32[]{:S(2)}) collective-permute-start(bf16[256,1152]{1,0:T(8,128)(2,1)S(1)} %cut.1), channel_id=1, source_target_pairs={{0,2},{2,4},{3,1},{4,6},{5,3},{6,8},{7,5},{8,10},{9,7},{10,12},{11... | collective-permute-start | bytes 1769480 | tf_op jit(solution)/shard_map/ppermute | solution.py:328
  59.9 2.6 %collective-permute-done.5.m3 = bf16[256,1152]{1,0:T(8,128)(2,1)S(1)} collective-permute-done((bf16[256,1152]{1,0:T(8,128)(2,1)S(1)}, bf16[256,1152]{1,0:T(8,128)(2,1)S(1)}, u32[]{:S(2)}, u32[]{:S(2)}) %collective-permute-start.5) | collective-permute-done | bytes 589856 | tf_op jit(solution)/shard_map/ppermute | solution.py:328
  62.5 4.8 %collective-permute-done.4.m2 = bf16[256,1152]{1,0:T(8,128)(2,1)S(1)} collective-permute-done((bf16[256,1152]{1,0:T(8,128)(2,1)S(1)}, bf16[256,1152]{1,0:T(8,128)(2,1)S(1)}, u32[]{:S(2)}, u32[]{:S(2)}) %collective-permute-start.4) | collective-permute-done | bytes 589856 | tf_op jit(solution)/shard_map/ppermute | solution.py:328
  67.5 4.9 %collective-permute-start.8 = (bf16[256,4480]{1,0:T(8,128)(2,1)S(1)}, bf16[256,4480]{1,0:T(8,128)(2,1)S(1)}, u32[]{:S(2)}, u32[]{:S(2)}) collective-permute-start(bf16[256,4480]{1,0:T(8,128)(2,1)S(1)} %join.1), channel_id=1, source_target_pairs={{0,1},{1,0},{2,3},{3,2},{4,5},{5,4},{6,7},{7,6},{8,9},{9,8},{10,11... | collective-permute-start | bytes 6881288 | tf_op jit(solution)/shard_map/ppermute | solution.py:317
  72.4 2.1 %collective-permute-start.9 = (bf16[784,512]{1,0:T(8,128)(2,1)S(1)}, bf16[784,512]{1,0:T(8,128)(2,1)S(1)}, u32[]{:S(2)}, u32[]{:S(2)}) collective-permute-start(bf16[784,512]{1,0:T(8,128)(2,1)S(1)} %collective-permute-done.6._.w_mh), channel_id=1, source_target_pairs={{0,1},{1,0},{2,3},{3,2},{4,5},{5,4},{6,7},{7,6},{8,9},{9,8},{10,11... | collective-permute-start | bytes 2408456 | tf_op jit(solution)/shard_map/ppermute | solution.py:317
  74.5 3.1 %collective-permute-done.9.w_th = bf16[784,512]{1,0:T(8,128)(2,1)S(1)} collective-permute-done((bf16[784,512]{1,0:T(8,128)(2,1)S(1)}, bf16[784,512]{1,0:T(8,128)(2,1)S(1)}, u32[]{:S(2)}, u32[]{:S(2)}) %collective-permute-start.9) | collective-permute-done | bytes 802848 | tf_op jit(solution)/shard_map/ppermute | solution.py:317
  77.6 15.2 %forward.1 = (bf16[4,128,512]{2,1,0:T(8,128)(2,1)S(1)}, bf16[256,512]{1,0:T(8,128)(2,1)S(1)}, bf16[768,768]{1,0:T(8,128)(2,1)S(1)}, bf16[768,512]{1,0:T(8,128)(2...) custom-call(bf16[256,1664]{1,0:T(8,128)(2,1)S(1)} %get-tuple-element, ...), custom_call_target="tpu_custom_call" | custom-call | flops 10737418240 | bytes 20971520 | tf_op jit(solution)/shard_map/forward/pallas_call | solution.py:385
  92.7 5.2 %collective-permute-start.11 = (bf16[256,512]{1,0:T(8,128)(2,1)S(1)}, bf16[256,512]{1,0:T(8,128)(2,1)S(1)}, u32[]{:S(2)}, u32[]{:S(2)}) collective-permute-start(bf16[256,512]{1,0:T(8,128)(2,1)S(1)} %get-tuple-element.32.grad_pre), channel_id=1, source_target_pairs={{0,4},{2,6},{4,8},{5,1},{6,10},{7,3},{8,12},{9,5},{10,14},{11,7},{... | collective-permute-start | bytes 786440 | tf_op jit(solution)/shard_map/ppermute | solution.py:328
  98.0 1.9 %collective-permute-start.10 = (bf16[256,512]{1,0:T(8,128)(2,1)S(1)}, bf16[256,512]{1,0:T(8,128)(2,1)S(1)}, u32[]{:S(2)}, u32[]{:S(2)}) collective-permute-start(bf16[256,512]{1,0:T(8,128)(2,1)S(1)} %get-tuple-element.32.grad_pre), channel_id=1, source_target_pairs={{0,2},{2,4},{3,1},{4,6},{5,3},{6,8},{7,5},{8,10},{9,7},{10,12},{11... | collective-permute-start | bytes 786440 | tf_op jit(solution)/shard_map/ppermute | solution.py:328
  99.9 8.9 %collective-permute-done.11.r2 = bf16[256,512]{1,0:T(8,128)(2,1)S(1)} collective-permute-done((bf16[256,512]{1,0:T(8,128)(2,1)S(1)}, bf16[256,512]{1,0:T(8,128)(2,1)S(1)}, u32[]{:S(2)}, u32[]{:S(2)}) %collective-permute-start.11) | collective-permute-done | bytes 262176 | tf_op jit(solution)/shard_map/ppermute | solution.py:328
  108.8 1.9 %collective-permute-start.13 = (bf16[256,512]{1,0:T(8,128)(2,1)S(1)}, bf16[256,512]{1,0:T(8,128)(2,1)S(1)}, u32[]{:S(2)}, u32[]{:S(2)}) collective-permute-start(bf16[256,512]{1,0:T(8,128)(2,1)S(1)} %collective-permute-done.11.r2), channel_id=1, source_target_pairs={{0,1},{1,0},{2,3},{3,2},{4,5},{5,4},{6,7},{7,6},{8,9},{9,8},{10,11... | collective-permute-start | bytes 786440 | tf_op jit(solution)/shard_map/ppermute | solution.py:317
  110.7 2.4 %collective-permute-start.12 = (bf16[256,512]{1,0:T(8,128)(2,1)S(1)}, bf16[256,512]{1,0:T(8,128)(2,1)S(1)}, u32[]{:S(2)}, u32[]{:S(2)}) collective-permute-start(bf16[256,512]{1,0:T(8,128)(2,1)S(1)} %collective-permute-done.10.r1), channel_id=1, source_target_pairs={{0,1},{1,0},{2,3},{3,2},{4,5},{5,4},{6,7},{7,6},{8,9},{9,8},{10,11... | collective-permute-start | bytes 786440 | tf_op jit(solution)/shard_map/ppermute | solution.py:317
  113.1 1.1 collective-permute-done.12.o1
  114.2 3.7 %backward_a.1 = (bf16[128,512]{1,0:T(8,128)(2,1)S(1)}, bf16[256,512]{1,0:T(8,128)(2,1)S(1)}, bf16[768,768]{1,0:T(8,128)(2,1)S(1)}, bf16[768,512]{1,0:T(8,128)(2,...) custom-call(bf16[256,512]{1,0:T(8,128)(2,1)S(1)} %get-tuple-element., ...), custom_call_target="tpu_custom_call", output_to_operand_aliasing={{2}: (11, {}), {3}: (12, {}), {4}: (13, {}), {5}: (14, {}),... | custom-call | flops 4026531840 | bytes 7864320 | tf_op jit(solution)/shard_map/backward_a/pallas_call | solution.py:407
  117.9 1.9 %collective-permute-start.15 = (bf16[256,512]{1,0:T(8,128)(2,1)S(1)}, bf16[256,512]{1,0:T(8,128)(2,1)S(1)}, u32[]{:S(2)}, u32[]{:S(2)}) collective-permute-start(bf16[256,512]{1,0:T(8,128)(2,1)S(1)} %get-tuple-element.42.g2_own), channel_id=1, source_target_pairs={{0,4},{2,6},{4,8},{5,1},{6,10},{7,3},{8,12},{9,5},{10,14},{11,7},{... | collective-permute-start | bytes 786440 | tf_op jit(solution)/shard_map/ppermute | solution.py:328
  119.9 2.5 %collective-permute-start.14 = (bf16[256,512]{1,0:T(8,128)(2,1)S(1)}, bf16[256,512]{1,0:T(8,128)(2,1)S(1)}, u32[]{:S(2)}, u32[]{:S(2)}) collective-permute-start(bf16[256,512]{1,0:T(8,128)(2,1)S(1)} %get-tuple-element.42.g2_own), channel_id=1, source_target_pairs={{0,2},{2,4},{3,1},{4,6},{5,3},{6,8},{7,5},{8,10},{9,7},{10,12},{11... | collective-permute-start | bytes 786440 | tf_op jit(solution)/shard_map/ppermute | solution.py:328
  122.3 11.7 %collective-permute-done.15.r2 = bf16[256,512]{1,0:T(8,128)(2,1)S(1)} collective-permute-done((bf16[256,512]{1,0:T(8,128)(2,1)S(1)}, bf16[256,512]{1,0:T(8,128)(2,1)S(1)}, u32[]{:S(2)}, u32[]{:S(2)}) %collective-permute-start.15) | collective-permute-done | bytes 262176 | tf_op jit(solution)/shard_map/ppermute | solution.py:328
  134.0 1.9 %collective-permute-start.17 = (bf16[256,512]{1,0:T(8,128)(2,1)S(1)}, bf16[256,512]{1,0:T(8,128)(2,1)S(1)}, u32[]{:S(2)}, u32[]{:S(2)}) collective-permute-start(bf16[256,512]{1,0:T(8,128)(2,1)S(1)} %collective-permute-done.15.r2), channel_id=1, source_target_pairs={{0,1},{1,0},{2,3},{3,2},{4,5},{5,4},{6,7},{7,6},{8,9},{9,8},{10,11... | collective-permute-start | bytes 786440 | tf_op jit(solution)/shard_map/ppermute | solution.py:317
  135.9 2.4 %collective-permute-start.16 = (bf16[256,512]{1,0:T(8,128)(2,1)S(1)}, bf16[256,512]{1,0:T(8,128)(2,1)S(1)}, u32[]{:S(2)}, u32[]{:S(2)}) collective-permute-start(bf16[256,512]{1,0:T(8,128)(2,1)S(1)} %collective-permute-done.14.r1), channel_id=1, source_target_pairs={{0,1},{1,0},{2,3},{3,2},{4,5},{5,4},{6,7},{7,6},{8,9},{9,8},{10,11... | collective-permute-start | bytes 786440 | tf_op jit(solution)/shard_map/ppermute | solution.py:317
  138.4 1.1 collective-permute-done.16.o1
  139.5 4.4 %backward_b.1 = bf16[4,256,512]{2,1,0:T(8,128)(2,1)S(1)} custom-call(bf16[256,512]{1,0:T(8,128)(2,1)S(1)} %get-tuple-element.42.g2_own, bf16[256,512]{1,0:T(8,128)(2,1)S(1)} %collective-permute-done.14.r1, bf16[256,512]{1,0:T(8,128)(2,1)S(1)} %collective-permute-done.15.r2, bf16[256,512]{1,0:T(8,128)(2,1)S(1)} %collective-permute-done.16.o1, ...), custom_call_target="tpu_custom_call" | custom-call | flops 4697620480 | bytes 9175040 | tf_op jit(solution)/shard_map/backward_b/pallas_call | solution.py:424
  143.9 18.7 %all_to_all.5.results = bf16[4,256,512]{2,1,0:T(8,128)(2,1)S(1)} all-to-all(bf16[4,256,512]{2,1,0:T(8,128)(2,1)S(1)} %backward_b.1), channel_id=1, replica_groups=mesh['section'=4,'chip'=64,'core'=2] {'section'}, dimensions={0} | all-to-all | bytes 2097152 | tf_op jit(solution)/shard_map/all_to_all | solution.py:437
  (25 shorter events, 2.3 us)
Async XLA Ops:
  0.6 6.8 %copy-start.4 = (s32[4]{0:T(128)S(1)}, s32[4]{0:T(128)}, u32[]{:S(2)}) copy-start(s32[4]{0:T(128)} %source.1) | copy-start | bytes 52
  0.6 6.8 %copy-start.3 = (bf16[4,128,128]{2,1,0:T(8,128)(2,1)S(1)}, bf16[4,128,128]{2,1,0:T(8,128)(2,1)}, u32[]{:S(2)}) copy-start(bf16[4,128,128]{2,1,0:T(8,128)(2,1)} %tiles.1) | copy-start | bytes 393220
  0.7 6.8 %copy-start.2 = (bf16[4,128,512]{2,1,0:T(8,128)(2,1)S(1)}, bf16[4,128,512]{2,1,0:T(8,128)(2,1)}, u32[]{:S(2)}) copy-start(bf16[4,128,512]{2,1,0:T(8,128)(2,1)} %cotangent.1) | copy-start | bytes 1572868
  0.7 6.8 %copy-start.1 = (bf16[4,128,512]{2,1,0:T(8,128)(2,1)S(1)}, bf16[4,128,512]{2,1,0:T(8,128)(2,1)}, u32[]{:S(2)}) copy-start(bf16[4,128,512]{2,1,0:T(8,128)(2,1)} %latent.1) | copy-start | bytes 1572868
  3.4 24.1 %collective-permute-start.2 = (bf16[1568,512]{1,0:T(8,128)(2,1)}, bf16[1568,512]{1,0:T(8,128)(2,1)S(1)}, u32[]{:S(2)}, u32[]{:S(2)}) collective-permute-start(bf16[1568,512]{1,0:T(8,128)(2,1)} %weights.1.w_own), channel_id=1, source_target_pairs={{0,128},{1,385},{128,256},{129,1},{256,384},{257,129},{384,0},{385... | collective-permute-start | bytes 4816904 | tf_op jit(solution)/shard_map/ppermute | solution.py:337
  8.4 21.0 %collective-permute-start = (bf16[128,1664]{1,0:T(8,128)(2,1)S(1)}, bf16[128,1664]{1,0:T(8,128)(2,1)S(1)}, u32[]{:S(2)}, u32[]{:S(2)}) collective-permute-start(bf16[128,1664]{1,0:T(8,128)(2,1)S(1)} %prepare.1.own), channel_id=1, source_target_pairs={{0,1},{1,0},{2,3},{3,2},{4,5},{5,4},{6,7},{7,6},{8,9},{9,8},{10,11... | collective-permute-start | bytes 1277960 | tf_op jit(solution)/shard_map/ppermute | solution.py:317
  27.4 39.9 %collective-permute-start.7 = (bf16[1568,512]{1,0:T(8,128)(2,1)S(1)}, bf16[1568,512]{1,0:T(8,128)(2,1)S(1)}, u32[]{:S(2)}, u32[]{:S(2)}) collective-permute-start(bf16[1568,512]{1,0:T(8,128)(2,1)S(1)} %collective-permute-done.2.weights.w_m), channel_id=1, source_target_pairs={{0,1},{1,0},{2,3},{3,2},{4,5},{5,4},{6,7},{7,6},{8,9},{9,8},{10,11... | collective-permute-start | bytes 4816904 | tf_op jit(solution)/shard_map/ppermute | solution.py:317
  29.5 21.9 %collective-permute-start.1 = (bf16[256,1664]{1,0:T(8,128)(2,1)S(1)}, bf16[256,1664]{1,0:T(8,128)(2,1)S(1)}, u32[]{:S(2)}, u32[]{:S(2)}) collective-permute-start(bf16[256,1664]{1,0:T(8,128)(2,1)S(1)} %get-tuple-element.27.own), channel_id=1, source_target_pairs={{0,2},{2,4},{3,1},{4,6},{5,3},{6,8},{7,5},{8,10},{9,7},{10,12},{11... | collective-permute-start | bytes 2555912 | tf_op jit(solution)/shard_map/ppermute | solution.py:328
  34.2 13.0 %collective-permute-start.3 = (bf16[256,512]{1,0:T(8,128)(2,1)S(1)}, bf16[256,512]{1,0:T(8,128)(2,1)S(1)}, u32[]{:S(2)}, u32[]{:S(2)}) collective-permute-start(bf16[256,512]{1,0:T(8,128)(2,1)S(1)} %get-tuple-element.28), channel_id=1, source_target_pairs={{0,8},{2,10},{4,12},{6,14},{8,16},{9,1},{10,18},{11,3},{12,20},{13... | collective-permute-start | bytes 786440 | tf_op jit(solution)/shard_map/ppermute | solution.py:328
  47.3 20.0 %collective-permute-start.6 = (bf16[784,512]{1,0:T(8,128)(2,1)S(1)}, bf16[784,512]{1,0:T(8,128)(2,1)S(1)}, u32[]{:S(2)}, u32[]{:S(2)}) collective-permute-start(bf16[784,512]{1,0:T(8,128)(2,1)S(1)} %half.1._), channel_id=1, source_target_pairs={{0,128},{1,385},{128,256},{129,1},{256,384},{257,129},{384,0},{385... | collective-permute-start | bytes 2408456 | tf_op jit(solution)/shard_map/ppermute | solution.py:337
  49.5 13.0 %collective-permute-start.5 = (bf16[256,1152]{1,0:T(8,128)(2,1)S(1)}, bf16[256,1152]{1,0:T(8,128)(2,1)S(1)}, u32[]{:S(2)}, u32[]{:S(2)}) collective-permute-start(bf16[256,1152]{1,0:T(8,128)(2,1)S(1)} %get-tuple-element.30), channel_id=1, source_target_pairs={{0,6},{2,8},{4,10},{6,12},{7,1},{8,14},{9,3},{10,16},{11,5},{12,18... | collective-permute-start | bytes 1769480 | tf_op jit(solution)/shard_map/ppermute | solution.py:328
  51.5 26.1 %copy-start = (bf16[1568,512]{1,0:T(8,128)(2,1)S(1)}, bf16[1568,512]{1,0:T(8,128)(2,1)}, u32[]{:S(2)}) copy-start(bf16[1568,512]{1,0:T(8,128)(2,1)} %weights.1.w_own) | copy-start | bytes 4816900
  51.5 15.8 %collective-permute-start.4 = (bf16[256,1152]{1,0:T(8,128)(2,1)S(1)}, bf16[256,1152]{1,0:T(8,128)(2,1)S(1)}, u32[]{:S(2)}, u32[]{:S(2)}) collective-permute-start(bf16[256,1152]{1,0:T(8,128)(2,1)S(1)} %cut.1), channel_id=1, source_target_pairs={{0,2},{2,4},{3,1},{4,6},{5,3},{6,8},{7,5},{8,10},{9,7},{10,12},{11... | collective-permute-start | bytes 1769480 | tf_op jit(solution)/shard_map/ppermute | solution.py:328
  67.5 10.1 %collective-permute-start.8 = (bf16[256,4480]{1,0:T(8,128)(2,1)S(1)}, bf16[256,4480]{1,0:T(8,128)(2,1)S(1)}, u32[]{:S(2)}, u32[]{:S(2)}) collective-permute-start(bf16[256,4480]{1,0:T(8,128)(2,1)S(1)} %join.1), channel_id=1, source_target_pairs={{0,1},{1,0},{2,3},{3,2},{4,5},{5,4},{6,7},{7,6},{8,9},{9,8},{10,11... | collective-permute-start | bytes 6881288 | tf_op jit(solution)/shard_map/ppermute | solution.py:317
  72.4 5.2 %collective-permute-start.9 = (bf16[784,512]{1,0:T(8,128)(2,1)S(1)}, bf16[784,512]{1,0:T(8,128)(2,1)S(1)}, u32[]{:S(2)}, u32[]{:S(2)}) collective-permute-start(bf16[784,512]{1,0:T(8,128)(2,1)S(1)} %collective-permute-done.6._.w_mh), channel_id=1, source_target_pairs={{0,1},{1,0},{2,3},{3,2},{4,5},{5,4},{6,7},{7,6},{8,9},{9,8},{10,11... | collective-permute-start | bytes 2408456 | tf_op jit(solution)/shard_map/ppermute | solution.py:317
  92.7 16.0 %collective-permute-start.11 = (bf16[256,512]{1,0:T(8,128)(2,1)S(1)}, bf16[256,512]{1,0:T(8,128)(2,1)S(1)}, u32[]{:S(2)}, u32[]{:S(2)}) collective-permute-start(bf16[256,512]{1,0:T(8,128)(2,1)S(1)} %get-tuple-element.32.grad_pre), channel_id=1, source_target_pairs={{0,4},{2,6},{4,8},{5,1},{6,10},{7,3},{8,12},{9,5},{10,14},{11,7},{... | collective-permute-start | bytes 786440 | tf_op jit(solution)/shard_map/ppermute | solution.py:328
  98.0 12.7 %collective-permute-start.10 = (bf16[256,512]{1,0:T(8,128)(2,1)S(1)}, bf16[256,512]{1,0:T(8,128)(2,1)S(1)}, u32[]{:S(2)}, u32[]{:S(2)}) collective-permute-start(bf16[256,512]{1,0:T(8,128)(2,1)S(1)} %get-tuple-element.32.grad_pre), channel_id=1, source_target_pairs={{0,2},{2,4},{3,1},{4,6},{5,3},{6,8},{7,5},{8,10},{9,7},{10,12},{11... | collective-permute-start | bytes 786440 | tf_op jit(solution)/shard_map/ppermute | solution.py:328
  108.8 4.3 %collective-permute-start.13 = (bf16[256,512]{1,0:T(8,128)(2,1)S(1)}, bf16[256,512]{1,0:T(8,128)(2,1)S(1)}, u32[]{:S(2)}, u32[]{:S(2)}) collective-permute-start(bf16[256,512]{1,0:T(8,128)(2,1)S(1)} %collective-permute-done.11.r2), channel_id=1, source_target_pairs={{0,1},{1,0},{2,3},{3,2},{4,5},{5,4},{6,7},{7,6},{8,9},{9,8},{10,11... | collective-permute-start | bytes 786440 | tf_op jit(solution)/shard_map/ppermute | solution.py:317
  110.7 3.6 %collective-permute-start.12 = (bf16[256,512]{1,0:T(8,128)(2,1)S(1)}, bf16[256,512]{1,0:T(8,128)(2,1)S(1)}, u32[]{:S(2)}, u32[]{:S(2)}) collective-permute-start(bf16[256,512]{1,0:T(8,128)(2,1)S(1)} %collective-permute-done.10.r1), channel_id=1, source_target_pairs={{0,1},{1,0},{2,3},{3,2},{4,5},{5,4},{6,7},{7,6},{8,9},{9,8},{10,11... | collective-permute-start | bytes 786440 | tf_op jit(solution)/shard_map/ppermute | solution.py:317
  117.9 16.1 %collective-permute-start.15 = (bf16[256,512]{1,0:T(8,128)(2,1)S(1)}, bf16[256,512]{1,0:T(8,128)(2,1)S(1)}, u32[]{:S(2)}, u32[]{:S(2)}) collective-permute-start(bf16[256,512]{1,0:T(8,128)(2,1)S(1)} %get-tuple-element.42.g2_own), channel_id=1, source_target_pairs={{0,4},{2,6},{4,8},{5,1},{6,10},{7,3},{8,12},{9,5},{10,14},{11,7},{... | collective-permute-start | bytes 786440 | tf_op jit(solution)/shard_map/ppermute | solution.py:328
  119.9 16.1 %collective-permute-start.14 = (bf16[256,512]{1,0:T(8,128)(2,1)S(1)}, bf16[256,512]{1,0:T(8,128)(2,1)S(1)}, u32[]{:S(2)}, u32[]{:S(2)}) collective-permute-start(bf16[256,512]{1,0:T(8,128)(2,1)S(1)} %get-tuple-element.42.g2_own), channel_id=1, source_target_pairs={{0,2},{2,4},{3,1},{4,6},{5,3},{6,8},{7,5},{8,10},{9,7},{10,12},{11... | collective-permute-start | bytes 786440 | tf_op jit(solution)/shard_map/ppermute | solution.py:328
  134.0 4.3 %collective-permute-start.17 = (bf16[256,512]{1,0:T(8,128)(2,1)S(1)}, bf16[256,512]{1,0:T(8,128)(2,1)S(1)}, u32[]{:S(2)}, u32[]{:S(2)}) collective-permute-start(bf16[256,512]{1,0:T(8,128)(2,1)S(1)} %collective-permute-done.15.r2), channel_id=1, source_target_pairs={{0,1},{1,0},{2,3},{3,2},{4,5},{5,4},{6,7},{7,6},{8,9},{9,8},{10,11... | collective-permute-start | bytes 786440 | tf_op jit(solution)/shard_map/ppermute | solution.py:317
  135.9 3.6 %collective-permute-start.16 = (bf16[256,512]{1,0:T(8,128)(2,1)S(1)}, bf16[256,512]{1,0:T(8,128)(2,1)S(1)}, u32[]{:S(2)}, u32[]{:S(2)}) collective-permute-start(bf16[256,512]{1,0:T(8,128)(2,1)S(1)} %collective-permute-done.14.r1), channel_id=1, source_target_pairs={{0,1},{1,0},{2,3},{3,2},{4,5},{5,4},{6,7},{7,6},{8,9},{9,8},{10,11... | collective-permute-start | bytes 786440 | tf_op jit(solution)/shard_map/ppermute | solution.py:317

commit v6 on v5

--- a/solution.py
+++ b/solution.py
@@ -127,7 +127,7 @@
         value[rows(held, B), :] = ref[:, 0:H]
 
 
-def cut_kernel(m1, _, near):
+def cut_kernel(m1, _, __, near):
     near[...] = m1[:, 0:WIDE]
 
 
@@ -373,7 +373,8 @@
     arrived, m4 = lax.optimization_barrier((w_m, m4))
     (w_half,) = call(half_kernel, [((W_HALF, H), BF16)], [VMEM], [], 4, "half")(arrived)
     w_mh = around(w_half)
-    (near,) = call(cut_kernel, [((PAIR, WIDE), BF16)], [VMEM, ANY], [], 4, "cut")(m1, w_half)
+    (near,) = call(cut_kernel, [((PAIR, WIDE), BF16)], [VMEM, ANY, ANY], [], 4, "cut")(m1, w_half, m3)
+    w_m, near = lax.optimization_barrier((w_m, near))
     m2 = spread(near, 1)
     w_t = swap(w_m)
     (joined,) = call(

time: 164 us -> 150 us (0.915)
  the two profiles are of different devices: /device:TPU:120 before, /device:TPU:248 now
where the time goes in v6:
time: 150 us; the launch traced here: 149 us
  starting transfers between devices  58.4 us (39%)
  waiting for transfers between devices  41.9 us (28%)
  Pallas kernels  28.2 us (19%)
  blocking collectives  18.9 us (13%)
  between operations  1.79 us (1%)
    ppermute x8, waiting for transfers between devices, spread(): return lax.ppermute(value, ('chip', 'core'), pairs)  35.2 us
    ppermute x8, starting transfers between devices, spread(): return lax.ppermute(value, ('chip', 'core'), pairs)  33.4 us
    all_to_all x1, blocking collectives, body(): results = lax.all_to_all(results, 'section', 0, 0, tiled=True)  18.9 us
    ppermute x8, starting transfers between devices, swap(): return lax.ppermute(value, 'core', [(0, 1), (1, 0)])  18.6 us
    pallas_call x1, Pallas kernels, body(): call(forward_kernel, [((4, B, H), BF16), ((PAIR, H), BF16), ((3 * PAIR, B...  15.1 us
    ppermute x8, waiting for transfers between devices, swap(): return lax.ppermute(value, 'core', [(0, 1), (1, 0)])  6.73 us
    ppermute x2, starting transfers between devices, around(): return lax.ppermute(value, ('section', 'core'), pairs)  6.35 us
    pallas_call x1, Pallas kernels, body(): call(backward_b_kernel, [((4, PAIR, H), BF16)], [VMEM] * 13, [pltpu.VMEM(...  4.42 us
  transfers between devices with their start and end apart: 18, of which 8 were waited for; matrix products, arithmetic and copies ran while one was open for 0% of the time, Pallas kernels for 1%

profile of v6, /device:TPU:248, one launch (start us, length us, event | category | flops | bytes accessed | tf_op | source)
XLA Modules:
  0.0 149.2 jit_solution(2539604335196185699)
XLA Ops:
  0.7 2.7 %weights.1.w_own = bf16[1568,512]{1,0:T(8,128)(2,1)} custom-call(bf16[1,512,512]{2,1,0:T(8,128)(2,1)} %w_a.1, bf16[1,512,512]{2,1,0:T(8,128)(2,1)} %w_b.1, bf16[1,512,512]{2,1,0:T(8,128)(2,1)} %w_c.1, f32[1,512]{1,0:T(1,128)} %gain.1), custom_call_target="tpu_custom_call" | custom-call | tf_op jit(solution)/shard_map/weights/pallas_call | solution.py:343
  3.4 3.4 %collective-permute-start.2 = (bf16[1568,512]{1,0:T(8,128)(2,1)}, bf16[1568,512]{1,0:T(8,128)(2,1)S(1)}, u32[]{:S(2)}, u32[]{:S(2)}) collective-permute-start(bf16[1568,512]{1,0:T(8,128)(2,1)} %weights.1.w_own), channel_id=1, source_target_pairs={{0,128},{1,385},{128,256},{129,1},{256,384},{257,129},{384,0},{385... | collective-permute-start | bytes 4816904 | tf_op jit(solution)/shard_map/ppermute | solution.py:337
  8.4 2.7 %collective-permute-start = (bf16[128,1664]{1,0:T(8,128)(2,1)S(1)}, bf16[128,1664]{1,0:T(8,128)(2,1)S(1)}, u32[]{:S(2)}, u32[]{:S(2)}) collective-permute-start(bf16[128,1664]{1,0:T(8,128)(2,1)S(1)} %prepare.1.own), channel_id=1, source_target_pairs={{0,1},{1,0},{2,3},{3,2},{4,5},{5,4},{6,7},{7,6},{8,9},{9,8},{10,11... | collective-permute-start | bytes 1277960 | tf_op jit(solution)/shard_map/ppermute | solution.py:317
  11.1 1.4 collective-permute-done.partner
  12.6 4.7 %collective-permute-start.1 = (bf16[256,1664]{1,0:T(8,128)(2,1)S(1)}, bf16[256,1664]{1,0:T(8,128)(2,1)S(1)}, u32[]{:S(2)}, u32[]{:S(2)}) collective-permute-start(bf16[256,1664]{1,0:T(8,128)(2,1)S(1)} %get-tuple-element.29.own), channel_id=1, source_target_pairs={{0,2},{2,4},{3,1},{4,6},{5,3},{6,8},{7,5},{8,10},{9,7},{10,12},{11... | collective-permute-start | bytes 2555912 | tf_op jit(solution)/shard_map/ppermute | solution.py:328
  17.3 3.7 %collective-permute-start.4 = (bf16[256,1152]{1,0:T(8,128)(2,1)S(1)}, bf16[256,1152]{1,0:T(8,128)(2,1)S(1)}, u32[]{:S(2)}, u32[]{:S(2)}) collective-permute-start(bf16[256,1152]{1,0:T(8,128)(2,1)S(1)} %get-tuple-element.32), channel_id=1, source_target_pairs={{0,6},{2,8},{4,10},{6,12},{7,1},{8,14},{9,3},{10,16},{11,5},{12,18... | collective-permute-start | bytes 1769480 | tf_op jit(solution)/shard_map/ppermute | solution.py:328
  21.1 2.9 %collective-permute-start.3 = (bf16[256,512]{1,0:T(8,128)(2,1)S(1)}, bf16[256,512]{1,0:T(8,128)(2,1)S(1)}, u32[]{:S(2)}, u32[]{:S(2)}) collective-permute-start(bf16[256,512]{1,0:T(8,128)(2,1)S(1)} %get-tuple-element.30), channel_id=1, source_target_pairs={{0,8},{2,10},{4,12},{6,14},{8,16},{9,1},{10,18},{11,3},{12,20},{13... | collective-permute-start | bytes 786440 | tf_op jit(solution)/shard_map/ppermute | solution.py:328
  24.0 12.7 %collective-permute-done.3.m4 = bf16[256,512]{1,0:T(8,128)(2,1)S(1)} collective-permute-done((bf16[256,512]{1,0:T(8,128)(2,1)S(1)}, bf16[256,512]{1,0:T(8,128)(2,1)S(1)}, u32[]{:S(2)}, u32[]{:S(2)}) %collective-permute-start.3) | collective-permute-done | bytes 262176 | tf_op jit(solution)/shard_map/ppermute | solution.py:328
  36.8 2.1 %collective-permute-start.7 = (bf16[1568,512]{1,0:T(8,128)(2,1)S(1)}, bf16[1568,512]{1,0:T(8,128)(2,1)S(1)}, u32[]{:S(2)}, u32[]{:S(2)}) collective-permute-start(bf16[1568,512]{1,0:T(8,128)(2,1)S(1)} %collective-permute-done.2.weights.w_m), channel_id=1, source_target_pairs={{0,1},{1,0},{2,3},{3,2},{4,5},{5,4},{6,7},{7,6},{8,9},{9,8},{10,11... | collective-permute-start | bytes 4816904 | tf_op jit(solution)/shard_map/ppermute | solution.py:317
  38.9 3.0 %collective-permute-start.6 = (bf16[784,512]{1,0:T(8,128)(2,1)S(1)}, bf16[784,512]{1,0:T(8,128)(2,1)S(1)}, u32[]{:S(2)}, u32[]{:S(2)}) collective-permute-start(bf16[784,512]{1,0:T(8,128)(2,1)S(1)} %half.1._), channel_id=1, source_target_pairs={{0,128},{1,385},{128,256},{129,1},{256,384},{257,129},{384,0},{385... | collective-permute-start | bytes 2408456 | tf_op jit(solution)/shard_map/ppermute | solution.py:337
  41.9 5.8 %collective-permute-start.5 = (bf16[256,1152]{1,0:T(8,128)(2,1)S(1)}, bf16[256,1152]{1,0:T(8,128)(2,1)S(1)}, u32[]{:S(2)}, u32[]{:S(2)}) collective-permute-start(bf16[256,1152]{1,0:T(8,128)(2,1)S(1)} %cut.1), channel_id=1, source_target_pairs={{0,2},{2,4},{3,1},{4,6},{5,3},{6,8},{7,5},{8,10},{9,7},{10,12},{11... | collective-permute-start | bytes 1769480 | tf_op jit(solution)/shard_map/ppermute | solution.py:328
  47.7 7.4 %collective-permute-done.5.m2 = bf16[256,1152]{1,0:T(8,128)(2,1)S(1)} collective-permute-done((bf16[256,1152]{1,0:T(8,128)(2,1)S(1)}, bf16[256,1152]{1,0:T(8,128)(2,1)S(1)}, u32[]{:S(2)}, u32[]{:S(2)}) %collective-permute-start.5) | collective-permute-done | bytes 589856 | tf_op jit(solution)/shard_map/ppermute | solution.py:328
  55.2 3.1 %collective-permute-start.8 = (bf16[256,4480]{1,0:T(8,128)(2,1)S(1)}, bf16[256,4480]{1,0:T(8,128)(2,1)S(1)}, u32[]{:S(2)}, u32[]{:S(2)}) collective-permute-start(bf16[256,4480]{1,0:T(8,128)(2,1)S(1)} %join.1), channel_id=1, source_target_pairs={{0,1},{1,0},{2,3},{3,2},{4,5},{5,4},{6,7},{7,6},{8,9},{9,8},{10,11... | collective-permute-start | bytes 6881288 | tf_op jit(solution)/shard_map/ppermute | solution.py:317
  58.4 2.1 %collective-permute-start.9 = (bf16[784,512]{1,0:T(8,128)(2,1)S(1)}, bf16[784,512]{1,0:T(8,128)(2,1)S(1)}, u32[]{:S(2)}, u32[]{:S(2)}) collective-permute-start(bf16[784,512]{1,0:T(8,128)(2,1)S(1)} %collective-permute-done.6._.w_mh), channel_id=1, source_target_pairs={{0,1},{1,0},{2,3},{3,2},{4,5},{5,4},{6,7},{7,6},{8,9},{9,8},{10,11... | collective-permute-start | bytes 2408456 | tf_op jit(solution)/shard_map/ppermute | solution.py:317
  60.5 3.1 %collective-permute-done.9.w_th = bf16[784,512]{1,0:T(8,128)(2,1)S(1)} collective-permute-done((bf16[784,512]{1,0:T(8,128)(2,1)S(1)}, bf16[784,512]{1,0:T(8,128)(2,1)S(1)}, u32[]{:S(2)}, u32[]{:S(2)}) %collective-permute-start.9) | collective-permute-done | bytes 802848 | tf_op jit(solution)/shard_map/ppermute | solution.py:317
  63.6 15.1 %forward.1 = (bf16[4,128,512]{2,1,0:T(8,128)(2,1)S(1)}, bf16[256,512]{1,0:T(8,128)(2,1)S(1)}, bf16[768,768]{1,0:T(8,128)(2,1)S(1)}, bf16[768,512]{1,0:T(8,128)(2...) custom-call(bf16[256,1664]{1,0:T(8,128)(2,1)S(1)} %get-tuple-element, ...), custom_call_target="tpu_custom_call" | custom-call | flops 10737418240 | bytes 20971520 | tf_op jit(solution)/shard_map/forward/pallas_call | solution.py:386
  78.7 3.0 %collective-permute-start.11 = (bf16[256,512]{1,0:T(8,128)(2,1)S(1)}, bf16[256,512]{1,0:T(8,128)(2,1)S(1)}, u32[]{:S(2)}, u32[]{:S(2)}) collective-permute-start(bf16[256,512]{1,0:T(8,128)(2,1)S(1)} %get-tuple-element.36.grad_pre), channel_id=1, source_target_pairs={{0,4},{2,6},{4,8},{5,1},{6,10},{7,3},{8,12},{9,5},{10,14},{11,7},{... | collective-permute-start | bytes 786440 | tf_op jit(solution)/shard_map/ppermute | solution.py:328
  81.7 5.8 %collective-permute-start.10 = (bf16[256,512]{1,0:T(8,128)(2,1)S(1)}, bf16[256,512]{1,0:T(8,128)(2,1)S(1)}, u32[]{:S(2)}, u32[]{:S(2)}) collective-permute-start(bf16[256,512]{1,0:T(8,128)(2,1)S(1)} %get-tuple-element.36.grad_pre), channel_id=1, source_target_pairs={{0,2},{2,4},{3,1},{4,6},{5,3},{6,8},{7,5},{8,10},{9,7},{10,12},{11... | collective-permute-start | bytes 786440 | tf_op jit(solution)/shard_map/ppermute | solution.py:328
  87.5 6.5 %collective-permute-done.11.r2 = bf16[256,512]{1,0:T(8,128)(2,1)S(1)} collective-permute-done((bf16[256,512]{1,0:T(8,128)(2,1)S(1)}, bf16[256,512]{1,0:T(8,128)(2,1)S(1)}, u32[]{:S(2)}, u32[]{:S(2)}) %collective-permute-start.11) | collective-permute-done | bytes 262176 | tf_op jit(solution)/shard_map/ppermute | solution.py:328
  94.0 1.9 %collective-permute-start.13 = (bf16[256,512]{1,0:T(8,128)(2,1)S(1)}, bf16[256,512]{1,0:T(8,128)(2,1)S(1)}, u32[]{:S(2)}, u32[]{:S(2)}) collective-permute-start(bf16[256,512]{1,0:T(8,128)(2,1)S(1)} %collective-permute-done.11.r2), channel_id=1, source_target_pairs={{0,1},{1,0},{2,3},{3,2},{4,5},{5,4},{6,7},{7,6},{8,9},{9,8},{10,11... | collective-permute-start | bytes 786440 | tf_op jit(solution)/shard_map/ppermute | solution.py:317
  96.0 2.4 %collective-permute-start.12 = (bf16[256,512]{1,0:T(8,128)(2,1)S(1)}, bf16[256,512]{1,0:T(8,128)(2,1)S(1)}, u32[]{:S(2)}, u32[]{:S(2)}) collective-permute-start(bf16[256,512]{1,0:T(8,128)(2,1)S(1)} %collective-permute-done.10.r1), channel_id=1, source_target_pairs={{0,1},{1,0},{2,3},{3,2},{4,5},{5,4},{6,7},{7,6},{8,9},{9,8},{10,11... | collective-permute-start | bytes 786440 | tf_op jit(solution)/shard_map/ppermute | solution.py:317
  98.4 1.1 collective-permute-done.12.o1
  99.5 3.7 %backward_a.1 = (bf16[128,512]{1,0:T(8,128)(2,1)S(1)}, bf16[256,512]{1,0:T(8,128)(2,1)S(1)}, bf16[768,768]{1,0:T(8,128)(2,1)S(1)}, bf16[768,512]{1,0:T(8,128)(2,...) custom-call(bf16[256,512]{1,0:T(8,128)(2,1)S(1)} %get-tuple-element., ...), custom_call_target="tpu_custom_call", output_to_operand_aliasing={{2}: (11, {}), {3}: (12, {}), {4}: (13, {}), {5}: (14, {}),... | custom-call | flops 4026531840 | bytes 7864320 | tf_op jit(solution)/shard_map/backward_a/pallas_call | solution.py:408
  103.2 3.3 %collective-permute-start.15 = (bf16[256,512]{1,0:T(8,128)(2,1)S(1)}, bf16[256,512]{1,0:T(8,128)(2,1)S(1)}, u32[]{:S(2)}, u32[]{:S(2)}) collective-permute-start(bf16[256,512]{1,0:T(8,128)(2,1)S(1)} %get-tuple-element.46.g2_own), channel_id=1, source_target_pairs={{0,4},{2,6},{4,8},{5,1},{6,10},{7,3},{8,12},{9,5},{10,14},{11,7},{... | collective-permute-start | bytes 786440 | tf_op jit(solution)/shard_map/ppermute | solution.py:328
  106.5 4.2 %collective-permute-start.14 = (bf16[256,512]{1,0:T(8,128)(2,1)S(1)}, bf16[256,512]{1,0:T(8,128)(2,1)S(1)}, u32[]{:S(2)}, u32[]{:S(2)}) collective-permute-start(bf16[256,512]{1,0:T(8,128)(2,1)S(1)} %get-tuple-element.46.g2_own), channel_id=1, source_target_pairs={{0,2},{2,4},{3,1},{4,6},{5,3},{6,8},{7,5},{8,10},{9,7},{10,12},{11... | collective-permute-start | bytes 786440 | tf_op jit(solution)/shard_map/ppermute | solution.py:328
  110.6 8.6 %collective-permute-done.15.r2 = bf16[256,512]{1,0:T(8,128)(2,1)S(1)} collective-permute-done((bf16[256,512]{1,0:T(8,128)(2,1)S(1)}, bf16[256,512]{1,0:T(8,128)(2,1)S(1)}, u32[]{:S(2)}, u32[]{:S(2)}) %collective-permute-start.15) | collective-permute-done | bytes 262176 | tf_op jit(solution)/shard_map/ppermute | solution.py:328
  119.2 1.9 %collective-permute-start.17 = (bf16[256,512]{1,0:T(8,128)(2,1)S(1)}, bf16[256,512]{1,0:T(8,128)(2,1)S(1)}, u32[]{:S(2)}, u32[]{:S(2)}) collective-permute-start(bf16[256,512]{1,0:T(8,128)(2,1)S(1)} %collective-permute-done.15.r2), channel_id=1, source_target_pairs={{0,1},{1,0},{2,3},{3,2},{4,5},{5,4},{6,7},{7,6},{8,9},{9,8},{10,11... | collective-permute-start | bytes 786440 | tf_op jit(solution)/shard_map/ppermute | solution.py:317
  121.2 2.4 %collective-permute-start.16 = (bf16[256,512]{1,0:T(8,128)(2,1)S(1)}, bf16[256,512]{1,0:T(8,128)(2,1)S(1)}, u32[]{:S(2)}, u32[]{:S(2)}) collective-permute-start(bf16[256,512]{1,0:T(8,128)(2,1)S(1)} %collective-permute-done.14.r1), channel_id=1, source_target_pairs={{0,1},{1,0},{2,3},{3,2},{4,5},{5,4},{6,7},{7,6},{8,9},{9,8},{10,11... | collective-permute-start | bytes 786440 | tf_op jit(solution)/shard_map/ppermute | solution.py:317
  123.6 1.1 collective-permute-done.16.o1
  124.7 4.4 %backward_b.1 = bf16[4,256,512]{2,1,0:T(8,128)(2,1)S(1)} custom-call(bf16[256,512]{1,0:T(8,128)(2,1)S(1)} %get-tuple-element.46.g2_own, bf16[256,512]{1,0:T(8,128)(2,1)S(1)} %collective-permute-done.14.r1, bf16[256,512]{1,0:T(8,128)(2,1)S(1)} %collective-permute-done.15.r2, bf16[256,512]{1,0:T(8,128)(2,1)S(1)} %collective-permute-done.16.o1, ...), custom_call_target="tpu_custom_call" | custom-call | flops 4697620480 | bytes 9175040 | tf_op jit(solution)/shard_map/backward_b/pallas_call | solution.py:425
  129.1 18.9 %all_to_all.5.results = bf16[4,256,512]{2,1,0:T(8,128)(2,1)S(1)} all-to-all(bf16[4,256,512]{2,1,0:T(8,128)(2,1)S(1)} %backward_b.1), channel_id=1, replica_groups=mesh['section'=4,'chip'=64,'core'=2] {'section'}, dimensions={0} | all-to-all | bytes 2097152 | tf_op jit(solution)/shard_map/all_to_all | solution.py:438
  148.1 1.0 split.1
  (25 shorter events, 1.4 us)
Async XLA Ops:
  0.6 6.8 %copy-start.4 = (s32[4]{0:T(128)S(1)}, s32[4]{0:T(128)}, u32[]{:S(2)}) copy-start(s32[4]{0:T(128)} %source.1) | copy-start | bytes 52
  0.6 6.8 %copy-start.3 = (bf16[4,128,128]{2,1,0:T(8,128)(2,1)S(1)}, bf16[4,128,128]{2,1,0:T(8,128)(2,1)}, u32[]{:S(2)}) copy-start(bf16[4,128,128]{2,1,0:T(8,128)(2,1)} %tiles.1) | copy-start | bytes 393220
  0.7 6.8 %copy-start.2 = (bf16[4,128,512]{2,1,0:T(8,128)(2,1)S(1)}, bf16[4,128,512]{2,1,0:T(8,128)(2,1)}, u32[]{:S(2)}) copy-start(bf16[4,128,512]{2,1,0:T(8,128)(2,1)} %cotangent.1) | copy-start | bytes 1572868
  0.7 6.8 %copy-start.1 = (bf16[4,128,512]{2,1,0:T(8,128)(2,1)S(1)}, bf16[4,128,512]{2,1,0:T(8,128)(2,1)}, u32[]{:S(2)}) copy-start(bf16[4,128,512]{2,1,0:T(8,128)(2,1)} %latent.1) | copy-start | bytes 1572868
  3.4 33.3 %collective-permute-start.2 = (bf16[1568,512]{1,0:T(8,128)(2,1)}, bf16[1568,512]{1,0:T(8,128)(2,1)S(1)}, u32[]{:S(2)}, u32[]{:S(2)}) collective-permute-start(bf16[1568,512]{1,0:T(8,128)(2,1)} %weights.1.w_own), channel_id=1, source_target_pairs={{0,128},{1,385},{128,256},{129,1},{256,384},{257,129},{384,0},{385... | collective-permute-start | bytes 4816904 | tf_op jit(solution)/shard_map/ppermute | solution.py:337
  8.4 4.1 %collective-permute-start = (bf16[128,1664]{1,0:T(8,128)(2,1)S(1)}, bf16[128,1664]{1,0:T(8,128)(2,1)S(1)}, u32[]{:S(2)}, u32[]{:S(2)}) collective-permute-start(bf16[128,1664]{1,0:T(8,128)(2,1)S(1)} %prepare.1.own), channel_id=1, source_target_pairs={{0,1},{1,0},{2,3},{3,2},{4,5},{5,4},{6,7},{7,6},{8,9},{9,8},{10,11... | collective-permute-start | bytes 1277960 | tf_op jit(solution)/shard_map/ppermute | solution.py:317
  12.6 24.1 %collective-permute-start.1 = (bf16[256,1664]{1,0:T(8,128)(2,1)S(1)}, bf16[256,1664]{1,0:T(8,128)(2,1)S(1)}, u32[]{:S(2)}, u32[]{:S(2)}) collective-permute-start(bf16[256,1664]{1,0:T(8,128)(2,1)S(1)} %get-tuple-element.29.own), channel_id=1, source_target_pairs={{0,2},{2,4},{3,1},{4,6},{5,3},{6,8},{7,5},{8,10},{9,7},{10,12},{11... | collective-permute-start | bytes 2555912 | tf_op jit(solution)/shard_map/ppermute | solution.py:328
  17.3 19.4 %collective-permute-start.4 = (bf16[256,1152]{1,0:T(8,128)(2,1)S(1)}, bf16[256,1152]{1,0:T(8,128)(2,1)S(1)}, u32[]{:S(2)}, u32[]{:S(2)}) collective-permute-start(bf16[256,1152]{1,0:T(8,128)(2,1)S(1)} %get-tuple-element.32), channel_id=1, source_target_pairs={{0,6},{2,8},{4,10},{6,12},{7,1},{8,14},{9,3},{10,16},{11,5},{12,18... | collective-permute-start | bytes 1769480 | tf_op jit(solution)/shard_map/ppermute | solution.py:328
  21.1 15.6 %collective-permute-start.3 = (bf16[256,512]{1,0:T(8,128)(2,1)S(1)}, bf16[256,512]{1,0:T(8,128)(2,1)S(1)}, u32[]{:S(2)}, u32[]{:S(2)}) collective-permute-start(bf16[256,512]{1,0:T(8,128)(2,1)S(1)} %get-tuple-element.30), channel_id=1, source_target_pairs={{0,8},{2,10},{4,12},{6,14},{8,16},{9,1},{10,18},{11,3},{12,20},{13... | collective-permute-start | bytes 786440 | tf_op jit(solution)/shard_map/ppermute | solution.py:328
  36.8 26.7 %copy-start = (bf16[1568,512]{1,0:T(8,128)(2,1)S(1)}, bf16[1568,512]{1,0:T(8,128)(2,1)}, u32[]{:S(2)}) copy-start(bf16[1568,512]{1,0:T(8,128)(2,1)} %weights.1.w_own) | copy-start | bytes 4816900
  36.8 18.2 %collective-permute-start.7 = (bf16[1568,512]{1,0:T(8,128)(2,1)S(1)}, bf16[1568,512]{1,0:T(8,128)(2,1)S(1)}, u32[]{:S(2)}, u32[]{:S(2)}) collective-permute-start(bf16[1568,512]{1,0:T(8,128)(2,1)S(1)} %collective-permute-done.2.weights.w_m), channel_id=1, source_target_pairs={{0,1},{1,0},{2,3},{3,2},{4,5},{5,4},{6,7},{7,6},{8,9},{9,8},{10,11... | collective-permute-start | bytes 4816904 | tf_op jit(solution)/shard_map/ppermute | solution.py:317
  38.9 16.2 %collective-permute-start.6 = (bf16[784,512]{1,0:T(8,128)(2,1)S(1)}, bf16[784,512]{1,0:T(8,128)(2,1)S(1)}, u32[]{:S(2)}, u32[]{:S(2)}) collective-permute-start(bf16[784,512]{1,0:T(8,128)(2,1)S(1)} %half.1._), channel_id=1, source_target_pairs={{0,128},{1,385},{128,256},{129,1},{256,384},{257,129},{384,0},{385... | collective-permute-start | bytes 2408456 | tf_op jit(solution)/shard_map/ppermute | solution.py:337
  41.9 13.2 %collective-permute-start.5 = (bf16[256,1152]{1,0:T(8,128)(2,1)S(1)}, bf16[256,1152]{1,0:T(8,128)(2,1)S(1)}, u32[]{:S(2)}, u32[]{:S(2)}) collective-permute-start(bf16[256,1152]{1,0:T(8,128)(2,1)S(1)} %cut.1), channel_id=1, source_target_pairs={{0,2},{2,4},{3,1},{4,6},{5,3},{6,8},{7,5},{8,10},{9,7},{10,12},{11... | collective-permute-start | bytes 1769480 | tf_op jit(solution)/shard_map/ppermute | solution.py:328
  55.2 8.3 %collective-permute-start.8 = (bf16[256,4480]{1,0:T(8,128)(2,1)S(1)}, bf16[256,4480]{1,0:T(8,128)(2,1)S(1)}, u32[]{:S(2)}, u32[]{:S(2)}) collective-permute-start(bf16[256,4480]{1,0:T(8,128)(2,1)S(1)} %join.1), channel_id=1, source_target_pairs={{0,1},{1,0},{2,3},{3,2},{4,5},{5,4},{6,7},{7,6},{8,9},{9,8},{10,11... | collective-permute-start | bytes 6881288 | tf_op jit(solution)/shard_map/ppermute | solution.py:317
  58.4 5.2 %collective-permute-start.9 = (bf16[784,512]{1,0:T(8,128)(2,1)S(1)}, bf16[784,512]{1,0:T(8,128)(2,1)S(1)}, u32[]{:S(2)}, u32[]{:S(2)}) collective-permute-start(bf16[784,512]{1,0:T(8,128)(2,1)S(1)} %collective-permute-done.6._.w_mh), channel_id=1, source_target_pairs={{0,1},{1,0},{2,3},{3,2},{4,5},{5,4},{6,7},{7,6},{8,9},{9,8},{10,11... | collective-permute-start | bytes 2408456 | tf_op jit(solution)/shard_map/ppermute | solution.py:317
  78.7 15.3 %collective-permute-start.11 = (bf16[256,512]{1,0:T(8,128)(2,1)S(1)}, bf16[256,512]{1,0:T(8,128)(2,1)S(1)}, u32[]{:S(2)}, u32[]{:S(2)}) collective-permute-start(bf16[256,512]{1,0:T(8,128)(2,1)S(1)} %get-tuple-element.36.grad_pre), channel_id=1, source_target_pairs={{0,4},{2,6},{4,8},{5,1},{6,10},{7,3},{8,12},{9,5},{10,14},{11,7},{... | collective-permute-start | bytes 786440 | tf_op jit(solution)/shard_map/ppermute | solution.py:328
  81.7 14.2 %collective-permute-start.10 = (bf16[256,512]{1,0:T(8,128)(2,1)S(1)}, bf16[256,512]{1,0:T(8,128)(2,1)S(1)}, u32[]{:S(2)}, u32[]{:S(2)}) collective-permute-start(bf16[256,512]{1,0:T(8,128)(2,1)S(1)} %get-tuple-element.36.grad_pre), channel_id=1, source_target_pairs={{0,2},{2,4},{3,1},{4,6},{5,3},{6,8},{7,5},{8,10},{9,7},{10,12},{11... | collective-permute-start | bytes 786440 | tf_op jit(solution)/shard_map/ppermute | solution.py:328
  94.0 4.3 %collective-permute-start.13 = (bf16[256,512]{1,0:T(8,128)(2,1)S(1)}, bf16[256,512]{1,0:T(8,128)(2,1)S(1)}, u32[]{:S(2)}, u32[]{:S(2)}) collective-permute-start(bf16[256,512]{1,0:T(8,128)(2,1)S(1)} %collective-permute-done.11.r2), channel_id=1, source_target_pairs={{0,1},{1,0},{2,3},{3,2},{4,5},{5,4},{6,7},{7,6},{8,9},{9,8},{10,11... | collective-permute-start | bytes 786440 | tf_op jit(solution)/shard_map/ppermute | solution.py:317
  96.0 3.6 %collective-permute-start.12 = (bf16[256,512]{1,0:T(8,128)(2,1)S(1)}, bf16[256,512]{1,0:T(8,128)(2,1)S(1)}, u32[]{:S(2)}, u32[]{:S(2)}) collective-permute-start(bf16[256,512]{1,0:T(8,128)(2,1)S(1)} %collective-permute-done.10.r1), channel_id=1, source_target_pairs={{0,1},{1,0},{2,3},{3,2},{4,5},{5,4},{6,7},{7,6},{8,9},{9,8},{10,11... | collective-permute-start | bytes 786440 | tf_op jit(solution)/shard_map/ppermute | solution.py:317
  103.2 16.0 %collective-permute-start.15 = (bf16[256,512]{1,0:T(8,128)(2,1)S(1)}, bf16[256,512]{1,0:T(8,128)(2,1)S(1)}, u32[]{:S(2)}, u32[]{:S(2)}) collective-permute-start(bf16[256,512]{1,0:T(8,128)(2,1)S(1)} %get-tuple-element.46.g2_own), channel_id=1, source_target_pairs={{0,4},{2,6},{4,8},{5,1},{6,10},{7,3},{8,12},{9,5},{10,14},{11,7},{... | collective-permute-start | bytes 786440 | tf_op jit(solution)/shard_map/ppermute | solution.py:328
  106.5 14.7 %collective-permute-start.14 = (bf16[256,512]{1,0:T(8,128)(2,1)S(1)}, bf16[256,512]{1,0:T(8,128)(2,1)S(1)}, u32[]{:S(2)}, u32[]{:S(2)}) collective-permute-start(bf16[256,512]{1,0:T(8,128)(2,1)S(1)} %get-tuple-element.46.g2_own), channel_id=1, source_target_pairs={{0,2},{2,4},{3,1},{4,6},{5,3},{6,8},{7,5},{8,10},{9,7},{10,12},{11... | collective-permute-start | bytes 786440 | tf_op jit(solution)/shard_map/ppermute | solution.py:328
  119.2 4.3 %collective-permute-start.17 = (bf16[256,512]{1,0:T(8,128)(2,1)S(1)}, bf16[256,512]{1,0:T(8,128)(2,1)S(1)}, u32[]{:S(2)}, u32[]{:S(2)}) collective-permute-start(bf16[256,512]{1,0:T(8,128)(2,1)S(1)} %collective-permute-done.15.r2), channel_id=1, source_target_pairs={{0,1},{1,0},{2,3},{3,2},{4,5},{5,4},{6,7},{7,6},{8,9},{9,8},{10,11... | collective-permute-start | bytes 786440 | tf_op jit(solution)/shard_map/ppermute | solution.py:317
  121.2 3.6 %collective-permute-start.16 = (bf16[256,512]{1,0:T(8,128)(2,1)S(1)}, bf16[256,512]{1,0:T(8,128)(2,1)S(1)}, u32[]{:S(2)}, u32[]{:S(2)}) collective-permute-start(bf16[256,512]{1,0:T(8,128)(2,1)S(1)} %collective-permute-done.14.r1), channel_id=1, source_target_pairs={{0,1},{1,0},{2,3},{3,2},{4,5},{5,4},{6,7},{7,6},{8,9},{9,8},{10,11... | collective-permute-start | bytes 786440 | tf_op jit(solution)/shard_map/ppermute | solution.py:317
